TPU v7x, 32 devices: a whole 2x2x4 slice. The times are simulated.
32 devices in a mesh: group: 2 (over x), comp: 16 (over z, y, core).
Axes of the slice: x: 2, y: 2, z: 4, core: 2. Of those that a mesh axis runs over, the one named last changes fastest.
Arguments:
- state: float32 [2, 5, 163840], P(None, None, ('group', 'comp')), parts along dimension 2, may hold values from -6 to 6
- surface_kind: int32 [81920], P('comp'), may hold values from 0 to 2
- send_block: int32 [16, 8, 32], P('comp'), may hold values from 0 to 39, as said below
- send_count: int32 [16, 8], P('comp'), may hold values from 0 to 32, as said below
- src_slot: int32 [640, 4], P('comp'), may hold values from 0 to 255
- src_count: int32 [640], P('comp'), may hold values from 1 to 4
- remap_weight: float32 [640, 4, 128, 128], P('comp'), may hold values from -0.25 to 0.25
Outputs:
- fluxes: float32 [2, 4, 163840], P(None, None, ('group', 'comp')), parts along dimension 2
There are 2 independent parts, one for each index of `group`. A program takes and returns all parts, laid end to end along the dimension named above; an argument that names none is the same for every part. Nothing has to cross between parts.
Inputs may be any that keep to these rules, and one draw needn't show every extreme that they name: `send_count`: A tile at position p = s mod (8) intersects the other half's tiles at positions p - n + 4 that lie in 0 to 7; such pairs count 1 to 32, all others 0. Some source tile sends 32 slots to every tile it intersects, and some tile receives 32 slots from every tile that intersects it. send_block[s, n, c] is a block of tile s; entries with c at or beyond send_count[s, n] are 0.
All inputs are finite; a program needn't handle non-finite values.
Results may differ from a plain program's by a relative error of at most 0.000059.
Values sent between devices are 32-bit elements; how exact they have to be, the bound alone decides.
No kernel may reach another device: no remote copies, remote signals or barrier semaphores. Data moves between devices by JAX's collectives and lax.ppermute only.
A program may use at most 64 MiB of HBM per device.

v0:
```python
import jax
import jax.numpy as jnp
from jax import lax
from jax.sharding import PartitionSpec as P


def passed_along(array, axis, by):
    devices = lax.axis_size(axis)
    return lax.ppermute(array, axis, [(i, (i + by) % devices) for i in range(devices)])


def bulk_fluxes(air, sea, surface_kind):
    wind_u, wind_v, air_temp, air_humid, radiation = (
        air[:, 0],
        air[:, 1],
        air[:, 2],
        air[:, 3],
        air[:, 4],
    )
    sea_temp, ice_conc, ice_temp, current_u, current_v = (
        sea[:, 0],
        sea[:, 1],
        sea[:, 2],
        sea[:, 3],
        sea[:, 4],
    )
    wet_cell = (surface_kind > 0).astype(air.dtype)
    ice_frac = jnp.clip(ice_conc, 0.0, 1.0) * (surface_kind == 2).astype(air.dtype)
    rel_u = wind_u - current_u
    rel_v = wind_v - current_v
    wind_speed = jnp.sqrt(rel_u * rel_u + rel_v * rel_v + 1.0)
    drag_coef = 0.8 * (1.0 - ice_frac) + 1.2 * ice_frac

    def surface_terms(surf_temp, sens_coef, albedo, latent):
        evaporation = 0.5 * wind_speed * (0.6 * jnp.exp(0.3 * surf_temp) - air_humid)
        heat_total = (
            sens_coef * wind_speed * (surf_temp - air_temp)
            + latent * evaporation
            - ((1.0 - albedo) * radiation - 0.25 * surf_temp)
        )
        return (heat_total, evaporation)

    heat_water, evap_water = surface_terms(sea_temp, 0.6, 0.07, 1.0)
    heat_ice, evap_ice = surface_terms(ice_temp, 0.4, 0.6, 1.2)
    stress_x = wet_cell * drag_coef * wind_speed * rel_u
    stress_y = wet_cell * drag_coef * wind_speed * rel_v
    heat_flux = wet_cell * ((1.0 - ice_frac) * heat_water + ice_frac * heat_ice)
    water_flux = wet_cell * ((1.0 - ice_frac) * evap_water + ice_frac * evap_ice)
    return jnp.stack([stress_x, stress_y, heat_flux, water_flux], axis=1)


def local(state, surface_kind, send_block, send_count, src_slot, src_count, remap_weight):
    tiles = lax.axis_size("comp")
    my_tile = lax.axis_index("comp")
    half_way = tiles // 2
    steps = state.shape[0]
    fields = state.shape[1]
    rows_all = steps * fields
    nblk = remap_weight.shape[0]
    width = remap_weight.shape[2]
    blocks_first = state.reshape(rows_all, nblk, width).transpose(1, 0, 2)
    chosen = send_block[0]
    counts = send_count[0]
    neigh = chosen.shape[0]
    capacity = chosen.shape[1]
    live_slot = lax.broadcasted_iota(jnp.int32, chosen.shape, 1) < counts[:, None]
    outgoing = jnp.where(live_slot[:, :, None, None], blocks_first[chosen], 0.0)
    steps_by = [half_way + neigh // 2 - offset for offset in range(neigh)]
    received = []
    for offset in range(neigh):
        received.append(passed_along(outgoing[offset], "comp", steps_by[offset]))
    arrived = jnp.stack(received)
    flat_slots = arrived.reshape(neigh * capacity, rows_all, width)
    taken = flat_slots[src_slot]
    slot_index = lax.broadcasted_iota(jnp.int32, src_slot.shape, 1)
    used_slot = (slot_index < src_count[:, None]).astype(jnp.float32)
    taken = taken * used_slot[:, :, None, None]
    remapped = jnp.einsum("bkci,bkit->cbt", taken, remap_weight, precision=lax.Precision.HIGHEST)
    remapped = remapped.reshape(steps, fields, nblk * width)
    is_air = my_tile < half_way
    air = jnp.where(is_air, state, remapped)
    sea = jnp.where(is_air, remapped, state)
    return bulk_fluxes(air, sea, surface_kind)


def solution(mesh):
    return jax.shard_map(
        local,
        mesh=mesh,
        in_specs=(
            P(None, None, ("group", "comp")),
            P("comp"),
            P("comp", None, None),
            P("comp", None),
            P("comp", None),
            P("comp"),
            P("comp", None, None, None),
        ),
        out_specs=P(None, None, ("group", "comp")),
        check_vma=False,
    )
```

profile of v0, /device:TPU:0, one launch (start us, length us, event | category | flops | bytes accessed | tf_op | source)
XLA Modules:
  0.0 88.7 jit_solution(16839022684332589764)
XLA Ops:
  0.0 1.0 %copy.16 = f32[2,5,5120]{2,1,0:T(8,128)S(1)} copy(f32[2,5,5120]{2,0,1:T(2,128)} %param.7) | data formatting | bytes 409600 | tf_op args[0]
  1.0 0.1 reshape.115
  1.1 0.1 copy.27
  1.1 0.7 compare_select_fusion
  1.8 0.1 reshape.120
  1.9 0.7 iota_compare_fusion.1
  2.7 1.0 %gather_fusion = f32[256,10,128]{2,1,0:T(8,128)S(1)} fusion(f32[40,10,128]{2,1,0:T(8,128)S(1)} %bitcast.49, s32[1024]{0:T(1024)S(1)} %pad_clamp_fusion.1), kind=kCustom, calls=%fused_computation | custom fusion | bytes 2622464 | tf_op jit(solution)/shard_map/gather | solution.py:67
  3.7 0.3 broadcast_select_fusion
  4.0 0.0 copy-start.3
  4.0 0.0 copy-start.1
  4.0 0.0 copy-start.2
  4.1 0.9 %slice_bitcast_fusion = (f32[32,10,128]{2,1,0:T(8,128)S(1)}, f32[32,10,128]{2,1,0:T(8,128)S(1)}, f32[32,10,128]{2,1,0:T(8,128)S(1)}, f32[32,10,128]{2,1,0:T(8,12...) fusion(f32[8,32,10,128]{3,2,1,0:T(8,128)S(1)} %broadcast_select, ...), kind=kLoop, calls=%fused_computation.8 | loop fusion | bytes 2621440 | tf_op jit(solution)/shard_map/squeeze | solution.py:71
  5.0 5.0 %collective-permute-start = (f32[32,10,128]{2,1,0:T(8,128)S(1)}, f32[32,10,128]{2,1,0:T(8,128)}, u32[]{:S(2)}, u32[]{:S(2)}) collective-permute-start(f32[32,10,128]{2,1,0:T(8,128)S(1)} %get-tuple-element.15), channel_id=1, source_target_pairs={{0,12},{1,13},{2,14},{3,15},{4,0},{5,1},{6,2},{7,3},{8,4},{9,5},{1... | collective-permute-start | bytes 491528 | tf_op jit(solution)/shard_map/ppermute | solution.py:9
  10.1 0.0 collective-permute-start.1
  10.1 0.4 collective-permute-start.2
  10.4 3.4 %collective-permute-start.3 = (f32[32,10,128]{2,1,0:T(8,128)S(1)}, f32[32,10,128]{2,1,0:T(8,128)}, u32[]{:S(2)}, u32[]{:S(2)}) collective-permute-start(f32[32,10,128]{2,1,0:T(8,128)S(1)} %get-tuple-element.12), channel_id=1, source_target_pairs={{0,9},{1,10},{2,11},{3,12},{4,13},{5,14},{6,15},{7,0},{8,1},{9,2},... | collective-permute-start | bytes 491528 | tf_op jit(solution)/shard_map/ppermute | solution.py:9
  13.8 0.1 collective-permute-start.4
  13.9 0.0 copy-done.3
  13.9 0.1 fusion.7
  14.0 0.0 copy-done.1
  14.0 0.0 copy-done.2
  14.1 0.1 copy.18
  14.1 0.1 reshape.128
  14.3 2.5 %collective-permute-done = f32[32,10,128]{2,1,0:T(8,128)} collective-permute-done((f32[32,10,128]{2,1,0:T(8,128)S(1)}, f32[32,10,128]{2,1,0:T(8,128)}, u32[]{:S(2)}, u32[]{:S(2)}) %collective-permute-start) | collective-permute-done | bytes 163872 | tf_op jit(solution)/shard_map/ppermute | solution.py:9
  16.8 0.0 collective-permute-start.5
  16.8 1.0 %bitcast_dynamic-update-slice_fusion.7 = f32[8,32,10,128]{3,2,1,0:T(8,128)S(1)} fusion(f32[32,10,128]{2,1,0:T(8,128)} %collective-permute-done), kind=kLoop, calls=%fused_computation.23 | loop fusion | bytes 425984
  17.8 4.7 %collective-permute-done.1 = f32[32,10,128]{2,1,0:T(8,128)} collective-permute-done((f32[32,10,128]{2,1,0:T(8,128)}, f32[32,10,128]{2,1,0:T(8,128)}, u32[]{:S(2)}, u32[]{:S(2)}) %collective-permute-start.1) | collective-permute-done | bytes 163872 | tf_op jit(solution)/shard_map/ppermute | solution.py:9
  22.5 0.0 collective-permute-start.6
  22.5 1.0 %bitcast_dynamic-update-slice_fusion.6 = f32[8,32,10,128]{3,2,1,0:T(8,128)S(1)} fusion(f32[8,32,10,128]{3,2,1,0:T(8,128)S(1)} %bitcast_dynamic-update-slice_fusion.7, f32[32,10,128]{2,1,0:T(8,128)} %collective-permute-done.1), kind=kLoop, calls=%fused_computation.22 | loop fusion | bytes 425984
  23.5 4.6 %collective-permute-done.2 = f32[32,10,128]{2,1,0:T(8,128)} collective-permute-done((f32[32,10,128]{2,1,0:T(8,128)}, f32[32,10,128]{2,1,0:T(8,128)}, u32[]{:S(2)}, u32[]{:S(2)}) %collective-permute-start.2) | collective-permute-done | bytes 163872 | tf_op jit(solution)/shard_map/ppermute | solution.py:9
  28.1 19.7 %collective-permute-start.7 = (f32[32,10,128]{2,1,0:T(8,128)S(1)}, f32[32,10,128]{2,1,0:T(8,128)S(1)}, u32[]{:S(2)}, u32[]{:S(2)}) collective-permute-start(f32[32,10,128]{2,1,0:T(8,128)S(1)} %get-tuple-element.8), channel_id=1, source_target_pairs={{0,5},{1,6},{2,7},{3,8},{4,9},{5,10},{6,11},{7,12},{8,13},{9,14},{... | collective-permute-start | bytes 491528 | tf_op jit(solution)/shard_map/ppermute | solution.py:9
  47.8 1.0 %bitcast_dynamic-update-slice_fusion.5 = f32[8,32,10,128]{3,2,1,0:T(8,128)S(1)} fusion(f32[8,32,10,128]{3,2,1,0:T(8,128)S(1)} %bitcast_dynamic-update-slice_fusion.6, f32[32,10,128]{2,1,0:T(8,128)} %collective-permute-done.2), kind=kLoop, calls=%fused_computation.21 | loop fusion | bytes 425984
  48.8 0.0 collective-permute-done.3
  48.8 1.0 %bitcast_dynamic-update-slice_fusion.4 = f32[8,32,10,128]{3,2,1,0:T(8,128)S(1)} fusion(f32[8,32,10,128]{3,2,1,0:T(8,128)S(1)} %bitcast_dynamic-update-slice_fusion.5, f32[32,10,128]{2,1,0:T(8,128)} %collective-permute-done.3), kind=kLoop, calls=%fused_computation.20 | loop fusion | bytes 425984
  49.8 26.0 %collective-permute-done.4 = f32[32,10,128]{2,1,0:T(8,128)} collective-permute-done((f32[32,10,128]{2,1,0:T(8,128)S(1)}, f32[32,10,128]{2,1,0:T(8,128)}, u32[]{:S(2)}, u32[]{:S(2)}) %collective-permute-start.4) | collective-permute-done | bytes 163872 | tf_op jit(solution)/shard_map/ppermute | solution.py:9
  75.7 1.0 %bitcast_dynamic-update-slice_fusion.3 = f32[8,32,10,128]{3,2,1,0:T(8,128)S(1)} fusion(f32[8,32,10,128]{3,2,1,0:T(8,128)S(1)} %bitcast_dynamic-update-slice_fusion.4, f32[32,10,128]{2,1,0:T(8,128)} %collective-permute-done.4), kind=kLoop, calls=%fused_computation.19 | loop fusion | bytes 425984
  76.7 0.6 collective-permute-done.5
  77.3 0.0 collective-permute-done.6
  77.4 0.9 %collective-permute-done.7 = f32[32,10,128]{2,1,0:T(8,128)S(1)} collective-permute-done((f32[32,10,128]{2,1,0:T(8,128)S(1)}, f32[32,10,128]{2,1,0:T(8,128)S(1)}, u32[]{:S(2)}, u32[]{:S(2)}) %collective-permute-start.7) | collective-permute-done | bytes 163872 | tf_op jit(solution)/shard_map/ppermute | solution.py:9
  78.3 0.8 gather_fusion.1
  79.1 0.0 copy-start
  79.1 8.0 %fusion.2 = f32[10,40,128]{2,0,1:T(8,128)S(1)} fusion(f32[40,4,128,128]{3,2,1,0:T(8,128)} %param.13, f32[40,4,10,128]{3,2,1,0:T(8,128)S(1)} %bitcast.51, f32[40,4]{1,0:T(8,128)S(1)} %fusion.7), kind=kOutput, calls=%fused_computation.4 | convolution fusion | flops 314777600 | bytes 11510400 | tf_op jit(solution)/shard_map/bkci,bkit->cbt/dot_general | solution.py:78
  87.1 0.1 copy.19
  87.2 0.0 copy-done
  87.2 0.3 broadcast_select_fusion.1
  87.5 0.2 fusion.8
  87.7 0.2 add_multiply_fusion.1
  87.9 0.1 pad_maximum_fusion
  88.0 0.7 copy.22
  (8 shorter events, 0.1 us)
Async XLA Ops:
  4.0 9.9 %copy-start.3 = (s32[40]{0:T(128)S(1)}, s32[40]{0:T(128)}, u32[]{:S(2)}) copy-start(s32[40]{0:T(128)} %param.12) | copy-start | bytes 484
  4.0 10.0 %copy-start.1 = (s32[5120]{0:T(1024)S(1)}, s32[5120]{0:T(1024)}, u32[]{:S(2)}) copy-start(s32[5120]{0:T(1024)} %param.8) | copy-start | bytes 61444
  4.0 10.0 %copy-start.2 = (s32[40,4]{0,1:T(4,128)S(1)}, s32[40,4]{0,1:T(4,128)}, u32[]{:S(2)}) copy-start(s32[40,4]{0,1:T(4,128)} %param.11) | copy-start | bytes 1924
  5.0 11.8 %collective-permute-start = (f32[32,10,128]{2,1,0:T(8,128)S(1)}, f32[32,10,128]{2,1,0:T(8,128)}, u32[]{:S(2)}, u32[]{:S(2)}) collective-permute-start(f32[32,10,128]{2,1,0:T(8,128)S(1)} %get-tuple-element.15), channel_id=1, source_target_pairs={{0,12},{1,13},{2,14},{3,15},{4,0},{5,1},{6,2},{7,3},{8,4},{9,5},{1... | collective-permute-start | bytes 491528 | tf_op jit(solution)/shard_map/ppermute | solution.py:9
  10.1 12.5 %collective-permute-start.1 = (f32[32,10,128]{2,1,0:T(8,128)}, f32[32,10,128]{2,1,0:T(8,128)}, u32[]{:S(2)}, u32[]{:S(2)}) collective-permute-start(f32[32,10,128]{2,1,0:T(8,128)} %get-tuple-element.14), channel_id=1, source_target_pairs={{0,11},{1,12},{2,13},{3,14},{4,15},{5,0},{6,1},{7,2},{8,3},{9,4},{... | collective-permute-start | bytes 491528 | tf_op jit(solution)/shard_map/ppermute | solution.py:9
  10.1 18.1 %collective-permute-start.2 = (f32[32,10,128]{2,1,0:T(8,128)}, f32[32,10,128]{2,1,0:T(8,128)}, u32[]{:S(2)}, u32[]{:S(2)}) collective-permute-start(f32[32,10,128]{2,1,0:T(8,128)} %get-tuple-element.13), channel_id=1, source_target_pairs={{0,10},{1,11},{2,12},{3,13},{4,14},{5,15},{6,0},{7,1},{8,2},{9,3},... | collective-permute-start | bytes 491528 | tf_op jit(solution)/shard_map/ppermute | solution.py:9
  10.4 38.4 %collective-permute-start.3 = (f32[32,10,128]{2,1,0:T(8,128)S(1)}, f32[32,10,128]{2,1,0:T(8,128)}, u32[]{:S(2)}, u32[]{:S(2)}) collective-permute-start(f32[32,10,128]{2,1,0:T(8,128)S(1)} %get-tuple-element.12), channel_id=1, source_target_pairs={{0,9},{1,10},{2,11},{3,12},{4,13},{5,14},{6,15},{7,0},{8,1},{9,2},... | collective-permute-start | bytes 491528 | tf_op jit(solution)/shard_map/ppermute | solution.py:9
  13.8 61.9 %collective-permute-start.4 = (f32[32,10,128]{2,1,0:T(8,128)S(1)}, f32[32,10,128]{2,1,0:T(8,128)}, u32[]{:S(2)}, u32[]{:S(2)}) collective-permute-start(f32[32,10,128]{2,1,0:T(8,128)S(1)} %get-tuple-element.11), channel_id=1, source_target_pairs={{0,8},{1,9},{2,10},{3,11},{4,12},{5,13},{6,14},{7,15},{8,0},{9,1},... | collective-permute-start | bytes 491528 | tf_op jit(solution)/shard_map/ppermute | solution.py:9
  16.8 60.5 %collective-permute-start.5 = (f32[32,10,128]{2,1,0:T(8,128)S(1)}, f32[32,10,128]{2,1,0:T(8,128)S(1)}, u32[]{:S(2)}, u32[]{:S(2)}) collective-permute-start(f32[32,10,128]{2,1,0:T(8,128)S(1)} %get-tuple-element.10), channel_id=1, source_target_pairs={{0,7},{1,8},{2,9},{3,10},{4,11},{5,12},{6,13},{7,14},{8,15},{9,0},... | collective-permute-start | bytes 491528 | tf_op jit(solution)/shard_map/ppermute | solution.py:9
  22.5 54.8 %collective-permute-start.6 = (f32[32,10,128]{2,1,0:T(8,128)S(1)}, f32[32,10,128]{2,1,0:T(8,128)S(1)}, u32[]{:S(2)}, u32[]{:S(2)}) collective-permute-start(f32[32,10,128]{2,1,0:T(8,128)S(1)} %get-tuple-element.9), channel_id=1, source_target_pairs={{0,6},{1,7},{2,8},{3,9},{4,10},{5,11},{6,12},{7,13},{8,14},{9,15},... | collective-permute-start | bytes 491528 | tf_op jit(solution)/shard_map/ppermute | solution.py:9
  28.1 50.1 %collective-permute-start.7 = (f32[32,10,128]{2,1,0:T(8,128)S(1)}, f32[32,10,128]{2,1,0:T(8,128)S(1)}, u32[]{:S(2)}, u32[]{:S(2)}) collective-permute-start(f32[32,10,128]{2,1,0:T(8,128)S(1)} %get-tuple-element.8), channel_id=1, source_target_pairs={{0,5},{1,6},{2,7},{3,8},{4,9},{5,10},{6,11},{7,12},{8,13},{9,14},{... | collective-permute-start | bytes 491528 | tf_op jit(solution)/shard_map/ppermute | solution.py:9
  79.1 8.1 %copy-start = (f32[2,5,5120]{2,0,1:T(2,128)S(1)}, f32[2,5,5120]{2,0,1:T(2,128)}, u32[]{:S(2)}) copy-start(f32[2,5,5120]{2,0,1:T(2,128)} %param.7) | copy-start | bytes 614404
where the time goes:
time: 89.1 us; the launch traced here: 88.7 us
  waiting for transfers between devices  39.4 us (44%)
  starting transfers between devices  28.6 us (32%)
  local copies, waits for them, and re-layouts  9.94 us (11%)
  matrix products  7.98 us (9%)
  other arithmetic  2.58 us (3%)
    ppermute x8, waiting for transfers between devices, passed_along(): lax.ppermute(array, axis, [(i, (i + by) % devices) for i in range(devices)])  39.4 us
    ppermute x8, starting transfers between devices, passed_along(): lax.ppermute(array, axis, [(i, (i + by) % devices) for i in range(devices)])  28.6 us
    dot_general x1, matrix products, local(): jnp.einsum('bkci,bkit->cbt', taken, remap_weight, precision=lax.Precision...  7.98 us
    unnamed x16, local copies, waits for them, and re-layouts  5.92 us
  transfers between devices with their start and end apart: 8, of which 6 were waited for; matrix products, arithmetic and copies ran while one was open for 6% of the time, Pallas kernels for 0%

commit v1 on v0

v1 whole, which is shorter than its diff:
```python
import jax
import jax.numpy as jnp
import numpy as np
from jax import lax
from jax.experimental import pallas as pl
from jax.experimental.pallas import tpu as pltpu
from jax.sharding import PartitionSpec as P


def exchange_plan(tiles, neigh):
    half = tiles // 2
    before, after = neigh // 2, neigh - 1 - neigh // 2
    wanted = set()
    for p in range(half):
        for s in range(max(0, p - before), min(half - 1, p + after) + 1):
            for core in (0, 1):
                if s // 2 != p // 2:
                    wanted.add((2 * (s // 2) + s % 2, 2 * (p // 2) + s % 2))
    reach = max((abs(s // 2 - p // 2) for s, p in wanted), default=0)
    passes, place = [], {}
    for p in range(half):
        place[p // 2, p // 2] = 0
    for d in range(1, reach + 1):
        for phase in (0, 1):
            pairs = []
            for s, p in sorted(wanted):
                low = min(s // 2, p // 2)
                if abs(s // 2 - p // 2) == d and (low // d) % 2 == phase:
                    pairs.append((s, p))
                    place[s // 2, p // 2] = len(passes) + 1
            if pairs:
                passes.append(pairs)
    held = 1 + len(passes)
    where = np.zeros((half, neigh), np.int32)
    for p in range(half):
        for n in range(neigh):
            s = p + n - before
            if 0 <= s < half:
                where[p, n] = place[s // 2, p // 2] + held * (s % 2 != p % 2)
    return passes, where, held


def split_kernel(chunks, w_hbm, out_ref, buf, sems):
    slots = w_hbm.shape[0]
    per = slots // chunks
    copies = [
        pltpu.make_async_copy(
            w_hbm.at[pl.ds(i * per, per)], buf.at[pl.ds(i * per, per)], sems.at[i]
        )
        for i in range(chunks)
    ]
    for copy in copies:
        copy.start()
    width = w_hbm.shape[2]
    for i in range(chunks):
        copies[i].wait()

        def one(j, carry):
            w = buf[j]
            high = w.astype(jnp.bfloat16)
            low = (w - high.astype(jnp.float32)).astype(jnp.bfloat16)
            out_ref[j, :, :width] = high
            out_ref[j, :, width:] = low
            return carry

        lax.fori_loop(i * per, (i + 1) * per, one, 0, unroll=2)


def split_weights(weight):
    slots, width, _ = weight.shape
    chunks = 10 if slots % 10 == 0 else 1
    return pl.pallas_call(
        lambda *refs: split_kernel(chunks, *refs),
        out_shape=pltpu.VMEM((slots, width, 2 * width), jnp.bfloat16),
        in_specs=[pl.BlockSpec(memory_space=pl.ANY)],
        out_specs=pl.BlockSpec(memory_space=pltpu.VMEM),
        scratch_shapes=[
            pltpu.VMEM(weight.shape, jnp.float32),
            pltpu.SemaphoreType.DMA((chunks,)),
        ],
        compiler_params=pltpu.CompilerParams(vmem_limit_bytes=32 * 2**20),
        cost_estimate=pl.CostEstimate(
            flops=slots * width * width * 4, bytes_accessed=weight.size * 8, transcendentals=0
        ),
        name="split_weights",
    )(weight)


def fluxes_of(air, sea, kind):
    wind_u, wind_v, air_temp, air_humid, radiation = air
    sea_temp, ice_conc, ice_temp, current_u, current_v = sea
    wet = (kind > 0).astype(jnp.float32)
    frac = jnp.clip(ice_conc, 0.0, 1.0) * (kind == 2).astype(jnp.float32)
    du = wind_u - current_u
    dv = wind_v - current_v
    speed = jnp.sqrt(du * du + dv * dv + 1.0)
    drag = 0.8 * (1.0 - frac) + 1.2 * frac

    def terms(ts, sens, albedo, latent):
        evap = 0.5 * speed * (0.6 * jnp.exp(0.3 * ts) - air_humid)
        heat = (
            sens * speed * (ts - air_temp)
            + latent * evap
            - ((1.0 - albedo) * radiation - 0.25 * ts)
        )
        return heat, evap

    heat_water, evap_water = terms(sea_temp, 0.6, 0.07, 1.0)
    heat_ice, evap_ice = terms(ice_temp, 0.4, 0.6, 1.2)
    pull = wet * drag * speed
    return (
        pull * du,
        pull * dv,
        wet * ((1.0 - frac) * heat_water + frac * heat_ice),
        wet * ((1.0 - frac) * evap_water + frac * evap_ice),
    )


def remap_kernel(dims, base_ref, slot_ref, count_ref, air_ref, x_ref, w_ref, state_ref, kind_ref, out_ref, acc):
    steps, fields, nblk, sources, zero_row = dims
    span = nblk * steps
    rows = 8
    width = w_ref.shape[1]

    def block(b, carry):
        count = count_ref[b]
        parts = []
        for k in range(sources):
            base = jnp.where(k < count, base_ref[slot_ref[b * sources + k]], zero_row)
            x = jnp.concatenate(
                [x_ref[pl.ds(base + m, rows, stride=span), :] for m in range(steps)], axis=0
            )
            high = x.astype(jnp.bfloat16)
            low = (x - high.astype(jnp.float32)).astype(jnp.bfloat16)
            parts.append(jnp.concatenate([high, low], axis=0))
        left = jnp.concatenate(parts, axis=1)
        right = w_ref[pl.ds(b * sources, sources)].reshape(sources * width, 2 * width)
        both = jnp.dot(left, right, preferred_element_type=jnp.float32)
        both = both[:, :width] + both[:, width:]
        n = rows * steps
        total = both[:n] + both[n:]
        for m in range(steps):
            acc[pl.ds(m * rows * nblk + b, rows, stride=nblk), :] = total[m * rows:(m + 1) * rows]
        return carry

    lax.fori_loop(0, nblk, block, 0, unroll=4)
    is_air = air_ref[0] > 0
    for m in range(steps):
        for j in range(nblk // 8):
            mapped = [acc[pl.ds((m * rows + f) * nblk + 8 * j, 8), :] for f in range(fields)]
            own = [
                state_ref[pl.ds(f * span + 8 * j * steps + m, 8, stride=steps), :]
                for f in range(fields)
            ]
            air = [jnp.where(is_air, s, r) for s, r in zip(own, mapped)]
            sea = [jnp.where(is_air, r, s) for s, r in zip(own, mapped)]
            for o, value in enumerate(fluxes_of(air, sea, kind_ref[pl.ds(8 * j, 8), :])):
                out_ref[pl.ds(m * 4 * nblk + 32 * j + o, 8, stride=4), :] = value


def remap_and_fluxes(base, slot, count, is_air, x, split, state, kind, dims):
    steps, fields, nblk, sources, zero_row = dims
    width = kind.shape[1]
    smem = pl.BlockSpec(memory_space=pltpu.SMEM)
    vmem = pl.BlockSpec(memory_space=pltpu.VMEM)
    return pl.pallas_call(
        lambda *refs: remap_kernel(dims, *refs),
        out_shape=jax.ShapeDtypeStruct((steps * nblk * 4, width), jnp.float32),
        in_specs=[smem] * 4 + [vmem] * 4,
        out_specs=vmem,
        scratch_shapes=[pltpu.VMEM((steps * 8 * nblk, width), jnp.float32)],
        compiler_params=pltpu.CompilerParams(vmem_limit_bytes=32 * 2**20),
        cost_estimate=pl.CostEstimate(
            flops=nblk * sources * 32 * width * width * 4,
            bytes_accessed=split.size * 2,
            transcendentals=2 * steps * nblk * width,
        ),
        name="remap_and_fluxes",
    )(base, slot, count, is_air, x, pltpu.with_memory_space_constraint(split, pltpu.VMEM), state, kind)


def local(state, surface_kind, send_block, send_count, src_slot, src_count, remap_weight):
    tiles = lax.axis_size("comp")
    tile = lax.axis_index("comp")
    half = tiles // 2
    position = tile % half
    steps, fields, _ = state.shape
    nblk, sources, width, _ = remap_weight.shape
    neigh, capacity = send_block.shape[1:]
    passes, where, held = exchange_plan(tiles, neigh)
    span = nblk * steps
    rows = fields * span

    def passed(array, pairs):
        return lax.ppermute(array, "comp", pairs)

    def both_halves(pairs):
        return pairs + [(s + half, t + half) for s, t in pairs]

    mine = state.reshape(steps, fields, nblk, width).transpose(1, 2, 0, 3).reshape(rows, width)
    across = passed(mine, [(i, (i + half) % tiles) for i in range(tiles)])
    near = [across] + [passed(across, both_halves(pairs)) for pairs in passes]
    near = jnp.concatenate(near)
    sibling = passed(near, [(i, i ^ 1) for i in range(tiles)])
    pad = 8 * span
    x = jnp.concatenate([near, sibling, jnp.zeros((pad, width), jnp.float32)])
    zero_row = 2 * held * rows

    live = lax.broadcasted_iota(jnp.int32, (neigh, capacity), 1) < send_count[0][:, None]
    coded = lax.all_gather(jnp.where(live, send_block[0], -1), "comp")
    offset = jnp.arange(neigh, dtype=jnp.int32)
    source = (tile + half - neigh // 2 + offset) % tiles
    picked = coded[source, offset]
    start = jnp.asarray(where)[position] * rows
    base = jnp.where(picked >= 0, start[:, None] + steps * picked, zero_row).reshape(-1)

    split = split_weights(remap_weight.reshape(nblk * sources, width, width))
    is_air = (tile < half).astype(jnp.int32).reshape(1)
    out = remap_and_fluxes(
        base, src_slot.reshape(-1), src_count, is_air, x, split, mine,
        surface_kind.reshape(nblk, width), (steps, fields, nblk, sources, zero_row),
    )
    out = out.reshape(steps, nblk, 4, width).transpose(0, 2, 1, 3)
    return out.reshape(steps, 4, nblk * width)


def solution(mesh):
    return jax.shard_map(
        local,
        mesh=mesh,
        in_specs=(
            P(None, None, ("group", "comp")),
            P("comp"),
            P("comp", None, None),
            P("comp", None),
            P("comp", None),
            P("comp"),
            P("comp", None, None, None),
        ),
        out_specs=P(None, None, ("group", "comp")),
        check_vma=False,
    )
```

time: 89.1 us -> 65.9 us (0.74)
  waiting for transfers between devices: 39.4 us -> 16.4 us
  blocking collectives: 0 us -> 22.6 us
  starting transfers between devices: 28.6 us -> 11.5 us
  matrix products: 7.98 us -> 0 us
  Pallas kernels: 0 us -> 7.04 us
  local copies, waits for them, and re-layouts: 9.94 us -> 6.35 us
  other arithmetic: 2.58 us -> 1.6 us
    ppermute x8 -> x5, waiting for transfers between devices: 39.4 us -> 16.4 us  [passed(): return lax.ppermute(array, 'comp', pairs)]
    all_gather x0 -> x1, blocking collectives: none -> 22.6 us  [local(): coded = lax.all_gather(jnp.where(live, send_block[0], -1), 'comp')]
    ppermute x8 -> x5, starting transfers between devices: 28.6 us -> 11.5 us  [passed(): return lax.ppermute(array, 'comp', pairs)]
    dot_general x1 -> x0, matrix products: 7.98 us -> none  [local(): jnp.einsum('bkci,bkit->cbt', taken, remap_weight, precision=lax.Precision...]
    pallas_call x0 -> x2, Pallas kernels: none -> 7.04 us  [the longest x1 4.3 us: remap_and_fluxes(): pl.pallas_call(lambda *refs: remap_kernel(dims, *refs), out_shape=jax.Sha...]
    gather x2 -> x1, local copies, waits for them, and re-layouts: 1.85 us -> 0.57 us  [local(): picked = coded[source, offset]]
    squeeze x1 -> x0, local copies, waits for them, and re-layouts: 0.95 us -> none  [local(): received.append(passed_along(outgoing[offset], 'comp', steps_by[offset]))]
    unnamed x16 -> x14, local copies, waits for them, and re-layouts: 5.92 us -> 5.58 us
  transfers between devices with their start and end apart: 8 -> 5, of which waited for: 6 -> 2; matrix products, arithmetic and copies ran while one was open for 6% -> 5% of each run, Pallas kernels for 0% -> 4%
where the time goes in v1:
time: 65.9 us; the launch traced here: 65.6 us
  blocking collectives  22.6 us (34%)
  waiting for transfers between devices  16.4 us (25%)
  starting transfers between devices  11.5 us (17%)
  Pallas kernels  7.04 us (11%)
  local copies, waits for them, and re-layouts  6.35 us (10%)
  other arithmetic  1.6 us (2%)
    all_gather x1, blocking collectives, local(): coded = lax.all_gather(jnp.where(live, send_block[0], -1), 'comp')  22.6 us
    ppermute x5, waiting for transfers between devices, passed(): return lax.ppermute(array, 'comp', pairs)  16.4 us
    ppermute x5, starting transfers between devices, passed(): return lax.ppermute(array, 'comp', pairs)  11.5 us
    unnamed x14, local copies, waits for them, and re-layouts  5.58 us
    pallas_call x1, Pallas kernels, remap_and_fluxes(): pl.pallas_call(lambda *refs: remap_kernel(dims, *refs), out_shape=jax.Sha...  4.3 us
    pallas_call x1, Pallas kernels, split_weights(): pl.pallas_call(lambda *refs: split_kernel(chunks, *refs), out_shape=pltpu...  2.74 us
  transfers between devices with their start and end apart: 5, of which 2 were waited for; matrix products, arithmetic and copies ran while one was open for 5% of the time, Pallas kernels for 4%

profile of v1, /device:TPU:0, one launch (start us, length us, event | category | flops | bytes accessed | tf_op | source)
XLA Modules:
  0.0 65.6 jit_solution(13895203718143954021)
XLA Ops:
  0.0 4.0 %collective-permute-start = (f32[400,128]{1,0:T(8,128)}, f32[400,128]{1,0:T(8,128)S(1)}, u32[]{:S(2)}, u32[]{:S(2)}) collective-permute-start(f32[400,128]{1,0:T(8,128)} %bitcast.19), channel_id=1, source_target_pairs={{0,8},{1,9},{2,10},{3,11},{4,12},{5,13},{6,14},{7,15},{8,0},{9,1},... | collective-permute-start | bytes 614408 | tf_op jit(solution)/shard_map/ppermute | solution.py:195
  4.0 9.7 %collective-permute-done = f32[400,128]{1,0:T(8,128)S(1)} collective-permute-done((f32[400,128]{1,0:T(8,128)}, f32[400,128]{1,0:T(8,128)S(1)}, u32[]{:S(2)}, u32[]{:S(2)}) %collective-permute-start) | collective-permute-done | bytes 204832 | tf_op jit(solution)/shard_map/ppermute | solution.py:195
  13.7 2.7 %collective-permute-start.3 = (f32[400,128]{1,0:T(8,128)S(1)}, f32[400,128]{1,0:T(8,128)S(1)}, u32[]{:S(2)}, u32[]{:S(2)}) collective-permute-start(f32[400,128]{1,0:T(8,128)S(1)} %collective-permute-done), channel_id=1, source_target_pairs={{0,4},{1,5},{2,6},{3,7},{4,0},{6,2},{8,12},{9,13},{10,14},{11,15},... | collective-permute-start | bytes 614408 | tf_op jit(solution)/shard_map/ppermute | solution.py:195
  16.4 0.7 %collective-permute-start.2 = (f32[400,128]{1,0:T(8,128)S(1)}, f32[400,128]{1,0:T(8,128)S(1)}, u32[]{:S(2)}, u32[]{:S(2)}) collective-permute-start(f32[400,128]{1,0:T(8,128)S(1)} %collective-permute-done), channel_id=1, source_target_pairs={{2,4},{3,5},{4,2},{5,3},{10,12},{11,13},{12,10},{13,11},{18,20},{1... | collective-permute-start | bytes 614408 | tf_op jit(solution)/shard_map/ppermute | solution.py:195
  17.1 4.0 %collective-permute-start.1 = (f32[400,128]{1,0:T(8,128)S(1)}, f32[400,128]{1,0:T(8,128)S(1)}, u32[]{:S(2)}, u32[]{:S(2)}) collective-permute-start(f32[400,128]{1,0:T(8,128)S(1)} %collective-permute-done), channel_id=1, source_target_pairs={{0,2},{1,3},{2,0},{3,1},{4,6},{5,7},{6,4},{7,5},{8,10},{9,11},{10,... | collective-permute-start | bytes 614408 | tf_op jit(solution)/shard_map/ppermute | solution.py:195
  21.1 0.8 %fusion = s32[1,8,32]{2,1,0:T(8,128)S(1)} fusion(s32[1,8,32]{2,1,0:T(8,128)} %param.10, s32[8]{0:T(128)} %bitcast.22), kind=kLoop, calls=%fused_computation.10 | loop fusion | flops 512 | bytes 2080 | tf_op jit(solution)/shard_map/jit(_where)/select_n | solution.py:210
  21.8 0.0 collective-permute-done.3
  21.8 0.0 collective-permute-done.2
  21.9 6.7 %collective-permute-done.1 = f32[400,128]{1,0:T(8,128)S(1)} collective-permute-done((f32[400,128]{1,0:T(8,128)S(1)}, f32[400,128]{1,0:T(8,128)S(1)}, u32[]{:S(2)}, u32[]{:S(2)}) %collective-permute-start.1) | collective-permute-done | bytes 204832 | tf_op jit(solution)/shard_map/ppermute | solution.py:195
  28.6 0.1 pad_maximum_fusion
  28.7 0.1 collective-permute-start.4
  28.8 0.8 %copy.14 = s32[40,4]{1,0:T(8,128)S(1)} copy(s32[40,4]{0,1:T(4,128)} %param.12) | data formatting | bytes 1280 | tf_op args[4]
  29.5 0.1 reshape.124.refs_1_
  29.6 22.6 %all_gather.4 = s32[16,8,32]{2,1,0:T(8,128)S(1)} all-gather(s32[1,8,32]{2,1,0:T(8,128)S(1)} %fusion), channel_id=1, replica_groups=mesh['group'=2,'comp'=16] {'comp'}, dimensions={0}, use_global_device_ids=true | all-gather | bytes 17408 | tf_op jit(solution)/shard_map/all_gather | solution.py:210
  52.2 0.6 gather_fusion
  52.8 0.7 %multiply_bitcast_fusion = s32[8]{0:T(128)S(1)} fusion(s32[8,8]{1,0:T(8,128)} %constant.53.clone, s32[]{:T(128)S(6)} %select_n.50), kind=kLoop, calls=%fused_computation.19 | loop fusion | flops 8 | bytes 68 | tf_op jit(solution)/shard_map/mul | solution.py:214
  53.5 0.1 add_select_fusion
  53.6 0.1 select_n.52.refs_0_
  53.7 0.0 copy-start
  53.7 4.0 %copy-done = f32[40,4,128,128]{3,2,1,0:T(8,128)S(1)} copy-done((f32[40,4,128,128]{3,2,1,0:T(8,128)S(1)}, f32[40,4,128,128]{3,2,1,0:T(8,128)}, u32[]{:S(2)}) %copy-start) | copy-done | bytes 10485784
  57.6 2.7 %split_weights.1.refs_5_ = bf16[160,128,256]{2,1,0:T(8,128)(2,1)S(1)} custom-call(f32[160,128,128]{2,1,0:T(8,128)S(1)} %bitcast.18), custom_call_target="tpu_custom_call" | custom-call | flops 10485760 | bytes 20971520 | tf_op jit(solution)/shard_map/split_weights/pallas_call | solution.py:72
  60.4 0.0 copy-start.1
  60.4 0.0 copy-start.2
  60.4 0.0 copy-start.3
  60.5 0.0 collective-permute-done.4
  60.5 0.1 constant_dynamic-update-slice_fusion
  60.6 0.7 %copy-done.1 = f32[2,5,5120]{2,0,1:T(2,128)S(1)} copy-done((f32[2,5,5120]{2,0,1:T(2,128)S(1)}, f32[2,5,5120]{2,0,1:T(2,128)}, u32[]{:S(2)}) %copy-start.1) | copy-done | bytes 204824
  61.3 0.0 copy-done.2
  61.3 0.0 copy-done.3
  61.3 4.3 %remap_and_fluxes.1 = f32[320,128]{1,0:T(8,128)} custom-call(s32[256]{0:T(256)S(1)} %select_n.52.refs_0_, s32[160]{0:T(256)S(1)} %reshape.124.refs_1_, s32[40]{0:T(128)S(1)} %copy-done.3, s32[1]{0:T(128)} %bitcast.3.refs_3_, f32[3840,128]{1,0:T(8,128)S(1)} %broadcast_dynamic-update-slice_fusion.refs_4_, bf16[160,128,256]{2,1,0:T(8,128)(2,1)S(1)} %split_weights.1.refs_5_, ...), custom_call_target="tpu_custom_call" | custom-call | flops 335544320 | bytes 10485760 | tf_op jit(solution)/shard_map/remap_and_fluxes/pallas_call | solution.py:166
  (6 shorter events, 0.1 us)
Async XLA Ops:
  0.0 13.7 %collective-permute-start = (f32[400,128]{1,0:T(8,128)}, f32[400,128]{1,0:T(8,128)S(1)}, u32[]{:S(2)}, u32[]{:S(2)}) collective-permute-start(f32[400,128]{1,0:T(8,128)} %bitcast.19), channel_id=1, source_target_pairs={{0,8},{1,9},{2,10},{3,11},{4,12},{5,13},{6,14},{7,15},{8,0},{9,1},... | collective-permute-start | bytes 614408 | tf_op jit(solution)/shard_map/ppermute | solution.py:195
  13.7 8.1 %collective-permute-start.3 = (f32[400,128]{1,0:T(8,128)S(1)}, f32[400,128]{1,0:T(8,128)S(1)}, u32[]{:S(2)}, u32[]{:S(2)}) collective-permute-start(f32[400,128]{1,0:T(8,128)S(1)} %collective-permute-done), channel_id=1, source_target_pairs={{0,4},{1,5},{2,6},{3,7},{4,0},{6,2},{8,12},{9,13},{10,14},{11,15},... | collective-permute-start | bytes 614408 | tf_op jit(solution)/shard_map/ppermute | solution.py:195
  16.4 5.4 %collective-permute-start.2 = (f32[400,128]{1,0:T(8,128)S(1)}, f32[400,128]{1,0:T(8,128)S(1)}, u32[]{:S(2)}, u32[]{:S(2)}) collective-permute-start(f32[400,128]{1,0:T(8,128)S(1)} %collective-permute-done), channel_id=1, source_target_pairs={{2,4},{3,5},{4,2},{5,3},{10,12},{11,13},{12,10},{13,11},{18,20},{1... | collective-permute-start | bytes 614408 | tf_op jit(solution)/shard_map/ppermute | solution.py:195
  17.1 11.5 %collective-permute-start.1 = (f32[400,128]{1,0:T(8,128)S(1)}, f32[400,128]{1,0:T(8,128)S(1)}, u32[]{:S(2)}, u32[]{:S(2)}) collective-permute-start(f32[400,128]{1,0:T(8,128)S(1)} %collective-permute-done), channel_id=1, source_target_pairs={{0,2},{1,3},{2,0},{3,1},{4,6},{5,7},{6,4},{7,5},{8,10},{9,11},{10,... | collective-permute-start | bytes 614408 | tf_op jit(solution)/shard_map/ppermute | solution.py:195
  28.7 31.9 %collective-permute-start.4 = (f32[1600,128]{1,0:T(8,128)S(1)}, f32[1600,128]{1,0:T(8,128)S(1)}, u32[]{:S(2)}, u32[]{:S(2)}) collective-permute-start(f32[1600,128]{1,0:T(8,128)S(1)} %pad_maximum_fusion), channel_id=1, source_target_pairs={{0,1},{1,0},{2,3},{3,2},{4,5},{5,4},{6,7},{7,6},{8,9},{9,8},{10,11... | collective-permute-start | bytes 2457608 | tf_op jit(solution)/shard_map/ppermute | solution.py:195
  53.7 4.0 %copy-start = (f32[40,4,128,128]{3,2,1,0:T(8,128)S(1)}, f32[40,4,128,128]{3,2,1,0:T(8,128)}, u32[]{:S(2)}) copy-start(f32[40,4,128,128]{3,2,1,0:T(8,128)} %param.14) | copy-start | bytes 31457284
  60.4 0.9 %copy-start.1 = (f32[2,5,5120]{2,0,1:T(2,128)S(1)}, f32[2,5,5120]{2,0,1:T(2,128)}, u32[]{:S(2)}) copy-start(f32[2,5,5120]{2,0,1:T(2,128)} %param.8) | copy-start | bytes 614404
  60.4 0.9 %copy-start.2 = (s32[5120]{0:T(1024)S(1)}, s32[5120]{0:T(1024)}, u32[]{:S(2)}) copy-start(s32[5120]{0:T(1024)} %param.9) | copy-start | bytes 61444
  60.4 0.9 %copy-start.3 = (s32[40]{0:T(128)S(1)}, s32[40]{0:T(128)}, u32[]{:S(2)}) copy-start(s32[40]{0:T(128)} %refs_2_.1) | copy-start | bytes 484

commit v2 on v1

--- a/solution.py
+++ b/solution.py
@@ -83,7 +83,7 @@
             flops=slots * width * width * 4, bytes_accessed=weight.size * 8, transcendentals=0
         ),
         name="split_weights",
-    )(weight)
+    )(pltpu.with_memory_space_constraint(weight, pltpu.HBM))
 
 
 def fluxes_of(air, sea, kind):
@@ -116,17 +116,31 @@
     )
 
 
-def remap_kernel(dims, base_ref, slot_ref, count_ref, air_ref, x_ref, w_ref, state_ref, kind_ref, out_ref, acc):
-    steps, fields, nblk, sources, zero_row = dims
+def remap_kernel(
+    dims, place_ref, slot_ref, count_ref, air_ref, x_ref, w_ref, state_ref, kind_ref, out_ref,
+    acc, starts, base_ref, sem,
+):
+    steps, fields, nblk, sources, capacity, stride, zero_row = dims
     span = nblk * steps
     rows = 8
     width = w_ref.shape[1]
+
+    lines = starts.shape[1]
+    for i in range(starts.shape[0]):
+        code = x_ref[pl.ds(i * stride + stride - lines, lines), :]
+        at = (code * steps + i * stride).astype(jnp.int32)
+        starts[i] = jnp.where(code >= 0.0, at, zero_row)
+    copy = pltpu.make_async_copy(starts, base_ref, sem)
+    copy.start()
+    copy.wait()
 
     def block(b, carry):
         count = count_ref[b]
         parts = []
         for k in range(sources):
-            base = jnp.where(k < count, base_ref[slot_ref[b * sources + k]], zero_row)
+            slot = slot_ref[b * sources + k]
+            base = base_ref[place_ref[slot // capacity], slot // width, slot % width]
+            base = jnp.where(k < count, base, zero_row)
             x = jnp.concatenate(
                 [x_ref[pl.ds(base + m, rows, stride=span), :] for m in range(steps)], axis=0
             )
@@ -158,9 +172,10 @@
                 out_ref[pl.ds(m * 4 * nblk + 32 * j + o, 8, stride=4), :] = value
 
 
-def remap_and_fluxes(base, slot, count, is_air, x, split, state, kind, dims):
-    steps, fields, nblk, sources, zero_row = dims
+def remap_and_fluxes(place, slot, count, is_air, x, split, state, kind, dims):
+    steps, fields, nblk, sources, capacity, stride, zero_row = dims
     width = kind.shape[1]
+    table = (zero_row // stride, stride - steps * fields * nblk, width)
     smem = pl.BlockSpec(memory_space=pltpu.SMEM)
     vmem = pl.BlockSpec(memory_space=pltpu.VMEM)
     return pl.pallas_call(
@@ -168,7 +183,12 @@
         out_shape=jax.ShapeDtypeStruct((steps * nblk * 4, width), jnp.float32),
         in_specs=[smem] * 4 + [vmem] * 4,
         out_specs=vmem,
-        scratch_shapes=[pltpu.VMEM((steps * 8 * nblk, width), jnp.float32)],
+        scratch_shapes=[
+            pltpu.VMEM((steps * 8 * nblk, width), jnp.float32),
+            pltpu.VMEM(table, jnp.int32),
+            pltpu.SMEM(table, jnp.int32),
+            pltpu.SemaphoreType.DMA,
+        ],
         compiler_params=pltpu.CompilerParams(vmem_limit_bytes=32 * 2**20),
         cost_estimate=pl.CostEstimate(
             flops=nblk * sources * 32 * width * width * 4,
@@ -176,7 +196,7 @@
             transcendentals=2 * steps * nblk * width,
         ),
         name="remap_and_fluxes",
-    )(base, slot, count, is_air, x, pltpu.with_memory_space_constraint(split, pltpu.VMEM), state, kind)
+    )(place, slot, count, is_air, x, pltpu.with_memory_space_constraint(split, pltpu.VMEM), state, kind)
 
 
 def local(state, surface_kind, send_block, send_count, src_slot, src_count, remap_weight):
@@ -198,27 +218,25 @@
         return pairs + [(s + half, t + half) for s, t in pairs]
 
     mine = state.reshape(steps, fields, nblk, width).transpose(1, 2, 0, 3).reshape(rows, width)
-    across = passed(mine, [(i, (i + half) % tiles) for i in range(tiles)])
+    live = lax.broadcasted_iota(jnp.int32, (neigh, capacity), 1) < send_count[0][:, None]
+    table = jnp.where(live, send_block[0], -1).astype(jnp.float32).reshape(-1, width)
+    table = jnp.pad(table, ((0, -table.shape[0] % 8), (0, 0)))
+    across_pairs = [(i, (i + half) % tiles) for i in range(tiles)]
+    across = jnp.concatenate([passed(mine, across_pairs), passed(table, across_pairs)])
     near = [across] + [passed(across, both_halves(pairs)) for pairs in passes]
     near = jnp.concatenate(near)
     sibling = passed(near, [(i, i ^ 1) for i in range(tiles)])
-    pad = 8 * span
-    x = jnp.concatenate([near, sibling, jnp.zeros((pad, width), jnp.float32)])
-    zero_row = 2 * held * rows
-
-    live = lax.broadcasted_iota(jnp.int32, (neigh, capacity), 1) < send_count[0][:, None]
-    coded = lax.all_gather(jnp.where(live, send_block[0], -1), "comp")
-    offset = jnp.arange(neigh, dtype=jnp.int32)
-    source = (tile + half - neigh // 2 + offset) % tiles
-    picked = coded[source, offset]
-    start = jnp.asarray(where)[position] * rows
-    base = jnp.where(picked >= 0, start[:, None] + steps * picked, zero_row).reshape(-1)
+    stride = rows + table.shape[0]
+    zero_row = 2 * held * stride
+    x = jnp.concatenate([near, sibling, jnp.zeros((8 * span, width), jnp.float32)])
+    place = jnp.asarray(where)[position]
 
     split = split_weights(remap_weight.reshape(nblk * sources, width, width))
     is_air = (tile < half).astype(jnp.int32).reshape(1)
     out = remap_and_fluxes(
-        base, src_slot.reshape(-1), src_count, is_air, x, split, mine,
-        surface_kind.reshape(nblk, width), (steps, fields, nblk, sources, zero_row),
+        place, src_slot.reshape(-1), src_count, is_air, x, split, mine,
+        surface_kind.reshape(nblk, width),
+        (steps, fields, nblk, sources, capacity, stride, zero_row),
     )
     out = out.reshape(steps, nblk, 4, width).transpose(0, 2, 1, 3)
     return out.reshape(steps, 4, nblk * width)

time: 65.9 us -> 41.2 us (0.63)
  the two profiles are of different devices: /device:TPU:0 before, /device:TPU:29 now
where the time goes in v2:
time: 41.2 us; the launch traced here: 40.9 us
  waiting for transfers between devices  17 us (41%)
  Pallas kernels  10.1 us (25%)
  starting transfers between devices  6.27 us (15%)
  local copies, waits for them, and re-layouts  6.16 us (15%)
  other arithmetic  1.33 us (3%)
    ppermute x6, waiting for transfers between devices, passed(): return lax.ppermute(array, 'comp', pairs)  17 us
    ppermute x6, starting transfers between devices, passed(): return lax.ppermute(array, 'comp', pairs)  6.27 us
    pallas_call x1, Pallas kernels, remap_and_fluxes(): pl.pallas_call(lambda *refs: remap_kernel(dims, *refs), out_shape=jax.Sha...  5.81 us
    pallas_call x1, Pallas kernels, split_weights(): pl.pallas_call(lambda *refs: split_kernel(chunks, *refs), out_shape=pltpu...  4.28 us
    unnamed x15, local copies, waits for them, and re-layouts  3.46 us
    unnamed x1, other arithmetic  1.32 us
  transfers between devices with their start and end apart: 6, of which 3 were waited for; matrix products, arithmetic and copies ran while one was open for 15% of the time, Pallas kernels for 10%

profile of v2, /device:TPU:29, one launch (start us, length us, event | category | flops | bytes accessed | tf_op | source)
XLA Modules:
  0.0 40.9 jit_solution(6731741462436889509)
XLA Ops:
  0.0 0.0 copy-start.3
  0.0 0.1 collective-permute-start
  0.1 0.5 %broadcast.11 = s32[]{:T(128)} broadcast(s32[]{:T(128)} %constant.20.clone.1), dimensions={} | broadcast | bytes 8 | tf_op args[3]
  0.6 1.3 %reduce.3 = s32[8]{0:T(128)S(1)} reduce(s32[1,8]{1,0:T(1,128)} %param.11, s32[]{:T(128)} %broadcast.11), dimensions={0}, to_apply=%param.11.reduce_sub_computation.3 | reduce | bytes 68 | tf_op args[3]
  1.9 0.1 lt.28
  2.0 0.8 %squeeze.7 = s32[2,128]{1,0:T(2,128)S(1)} reshape(s32[1,8,32]{2,1,0:T(8,128)} %param.10) | data formatting | bytes 2048 | tf_op jit(solution)/shard_map/squeeze | solution.py:222
  2.7 0.1 iota.12
  2.8 0.1 lt.29
  2.9 0.1 lt.30
  3.0 2.4 %collective-permute-start.1 = (f32[8,128]{1,0:T(8,128)S(1)}, f32[8,128]{1,0:T(8,128)S(1)}, u32[]{:S(2)}, u32[]{:S(2)}) collective-permute-start(f32[8,128]{1,0:T(8,128)S(1)} %pad.4), channel_id=1, source_target_pairs={{0,8},{1,9},{2,10},{3,11},{4,12},{5,13},{6,14},{7,15},{8,0},{9,1},... | collective-permute-start | bytes 12296 | tf_op jit(solution)/shard_map/ppermute | solution.py:215
  5.4 7.1 %collective-permute-done = f32[400,128]{1,0:T(8,128)S(1)} collective-permute-done((f32[400,128]{1,0:T(8,128)}, f32[400,128]{1,0:T(8,128)S(1)}, u32[]{:S(2)}, u32[]{:S(2)}) %collective-permute-start) | collective-permute-done | bytes 204832 | tf_op jit(solution)/shard_map/ppermute | solution.py:215
  12.5 0.7 %constant_dynamic-update-slice_fusion.6 = (f32[1632,128]{1,0:T(8,128)}, f32[3904,128]{1,0:T(8,128)S(1)}, f32[408,128]{1,0:T(8,128)S(1)}) fusion(f32[400,128]{1,0:T(8,128)S(1)} %collective-permute-done), kind=kLoop, calls=%fused_computation.7 | loop fusion | bytes 819200
  13.2 0.0 collective-permute-done.1
  13.2 0.6 %constant_dynamic-update-slice_fusion.5 = (f32[1632,128]{1,0:T(8,128)}, f32[3904,128]{1,0:T(8,128)S(1)}, f32[408,128]{1,0:T(8,128)S(1)}) fusion(f32[1632,128]{1,0:T(8,128)} %get-tuple-element.11, f32[8,128]{1,0:T(8,128)S(1)} %collective-permute-done.1, f32[3904,128]{1,0:T(8,128)S(1)} %get-tuple-element.12, f32[408,128]{1,0:T(8,128)S(1)} %get-tuple-element.13), kind=kLoop, calls=%fused_computation.6 | loop fusion | bytes 16384
  13.8 0.2 collective-permute-start.2
  14.0 0.7 %collective-permute-start.3 = (f32[408,128]{1,0:T(8,128)S(1)}, f32[408,128]{1,0:T(8,128)S(1)}, u32[]{:S(2)}, u32[]{:S(2)}) collective-permute-start(f32[408,128]{1,0:T(8,128)S(1)} %get-tuple-element.16), channel_id=1, source_target_pairs={{2,4},{3,5},{4,2},{5,3},{10,12},{11,13},{12,10},{13,11},{18,20},{1... | collective-permute-start | bytes 626696 | tf_op jit(solution)/shard_map/ppermute | solution.py:215
  14.7 1.3 %collective-permute-start.4 = (f32[408,128]{1,0:T(8,128)S(1)}, f32[408,128]{1,0:T(8,128)S(1)}, u32[]{:S(2)}, u32[]{:S(2)}) collective-permute-start(f32[408,128]{1,0:T(8,128)S(1)} %get-tuple-element.16), channel_id=1, source_target_pairs={{0,4},{1,5},{2,6},{3,7},{4,0},{6,2},{8,12},{9,13},{10,14},{11,15},... | collective-permute-start | bytes 626696 | tf_op jit(solution)/shard_map/ppermute | solution.py:215
  16.0 4.0 %collective-permute-done.2 = f32[408,128]{1,0:T(8,128)S(1)} collective-permute-done((f32[408,128]{1,0:T(8,128)S(1)}, f32[408,128]{1,0:T(8,128)S(1)}, u32[]{:S(2)}, u32[]{:S(2)}) %collective-permute-start.2) | collective-permute-done | bytes 208928 | tf_op jit(solution)/shard_map/ppermute | solution.py:215
  20.0 0.7 %constant_dynamic-update-slice_fusion.4 = (f32[1632,128]{1,0:T(8,128)}, f32[3904,128]{1,0:T(8,128)S(1)}) fusion(f32[1632,128]{1,0:T(8,128)} %get-tuple-element.14, f32[408,128]{1,0:T(8,128)S(1)} %collective-permute-done.2, f32[3904,128]{1,0:T(8,128)S(1)} %get-tuple-element.15), kind=kLoop, calls=%fused_computation.5 | loop fusion | bytes 626688
  20.7 0.0 collective-permute-done.3
  20.7 0.7 %constant_dynamic-update-slice_fusion.3 = (f32[1632,128]{1,0:T(8,128)}, f32[3904,128]{1,0:T(8,128)S(1)}) fusion(f32[1632,128]{1,0:T(8,128)} %get-tuple-element.9, f32[408,128]{1,0:T(8,128)S(1)} %collective-permute-done.3, f32[3904,128]{1,0:T(8,128)S(1)} %get-tuple-element.10), kind=kLoop, calls=%fused_computation.4 | loop fusion | bytes 626688
  21.4 5.9 %collective-permute-done.4 = f32[408,128]{1,0:T(8,128)S(1)} collective-permute-done((f32[408,128]{1,0:T(8,128)S(1)}, f32[408,128]{1,0:T(8,128)S(1)}, u32[]{:S(2)}, u32[]{:S(2)}) %collective-permute-start.4) | collective-permute-done | bytes 208928 | tf_op jit(solution)/shard_map/ppermute | solution.py:215
  27.3 0.7 %constant_dynamic-update-slice_fusion.2 = (f32[1632,128]{1,0:T(8,128)}, f32[3904,128]{1,0:T(8,128)S(1)}) fusion(f32[1632,128]{1,0:T(8,128)} %get-tuple-element.7, f32[408,128]{1,0:T(8,128)S(1)} %collective-permute-done.4, f32[3904,128]{1,0:T(8,128)S(1)} %get-tuple-element.8), kind=kLoop, calls=%fused_computation.3 | loop fusion | bytes 626688 | tf_op jit(solution)/shard_map/concatenate | solution.py:227
  28.0 1.7 %collective-permute-start.5 = (f32[1632,128]{1,0:T(8,128)}, f32[1632,128]{1,0:T(8,128)S(1)}, u32[]{:S(2)}, u32[]{:S(2)}) collective-permute-start(f32[1632,128]{1,0:T(8,128)} %get-tuple-element.5), channel_id=1, source_target_pairs={{0,1},{1,0},{2,3},{3,2},{4,5},{5,4},{6,7},{7,6},{8,9},{9,8},{10,11... | collective-permute-start | bytes 2506760 | tf_op jit(solution)/shard_map/ppermute | solution.py:215
  29.7 0.0 copy-done.3
  29.7 0.1 copy.11
  29.8 0.1 reshape.33.refs_1_
  29.9 4.3 %split_weights.1.refs_5_ = bf16[160,128,256]{2,1,0:T(8,128)(2,1)S(1)} custom-call(f32[160,128,128]{2,1,0:T(8,128)} %bitcast.18), custom_call_target="tpu_custom_call" | custom-call | flops 10485760 | bytes 20971520 | tf_op jit(solution)/shard_map/split_weights/pallas_call | solution.py:72
  34.2 0.0 copy-start
  34.2 0.0 copy-start.1
  34.2 0.0 copy-start.2
  34.2 0.8 %dynamic-slice_bitcast_fusion.refs_0_ = s32[8]{0:T(128)S(1)} fusion(s32[8,8]{1,0:T(8,128)} %constant.25.clone, s32[]{:T(128)S(6)} %select_n.16), kind=kLoop, calls=%fused_computation.16 | loop fusion | bytes 68 | tf_op jit(solution)/shard_map/squeeze | solution.py:232
  35.0 0.0 collective-permute-done.5
  35.0 0.1 constant_dynamic-update-slice_fusion.7
  35.1 0.1 copy-done
  35.1 0.0 copy-done.1
  35.1 0.0 copy-done.2
  35.1 5.8 %remap_and_fluxes.1 = f32[320,128]{1,0:T(8,128)} custom-call(s32[8]{0:T(128)S(1)} %dynamic-slice_bitcast_fusion.refs_0_, s32[160]{0:T(256)S(1)} %reshape.33.refs_1_, s32[40]{0:T(128)S(1)} %copy-done.2, s32[1]{0:T(128)} %bitcast.1.refs_3_, f32[3904,128]{1,0:T(8,128)S(1)} %broadcast_dynamic-update-slice_fusion.refs_4_, ...), custom_call_target="tpu_custom_call" | custom-call | flops 335544320 | bytes 10485760 | tf_op jit(solution)/shard_map/remap_and_fluxes/pallas_call | solution.py:181
  (4 shorter events, 0.0 us)
Async XLA Ops:
  0.0 29.7 %copy-start.3 = (s32[40,4]{0,1:T(4,128)S(1)}, s32[40,4]{0,1:T(4,128)}, u32[]{:S(2)}) copy-start(s32[40,4]{0,1:T(4,128)} %param.12) | copy-start | bytes 1924
  0.0 12.5 %collective-permute-start = (f32[400,128]{1,0:T(8,128)}, f32[400,128]{1,0:T(8,128)S(1)}, u32[]{:S(2)}, u32[]{:S(2)}) collective-permute-start(f32[400,128]{1,0:T(8,128)} %bitcast.15), channel_id=1, source_target_pairs={{0,8},{1,9},{2,10},{3,11},{4,12},{5,13},{6,14},{7,15},{8,0},{9,1},... | collective-permute-start | bytes 614408 | tf_op jit(solution)/shard_map/ppermute | solution.py:215
  3.0 10.2 %collective-permute-start.1 = (f32[8,128]{1,0:T(8,128)S(1)}, f32[8,128]{1,0:T(8,128)S(1)}, u32[]{:S(2)}, u32[]{:S(2)}) collective-permute-start(f32[8,128]{1,0:T(8,128)S(1)} %pad.4), channel_id=1, source_target_pairs={{0,8},{1,9},{2,10},{3,11},{4,12},{5,13},{6,14},{7,15},{8,0},{9,1},... | collective-permute-start | bytes 12296 | tf_op jit(solution)/shard_map/ppermute | solution.py:215
  13.8 6.2 %collective-permute-start.2 = (f32[408,128]{1,0:T(8,128)S(1)}, f32[408,128]{1,0:T(8,128)S(1)}, u32[]{:S(2)}, u32[]{:S(2)}) collective-permute-start(f32[408,128]{1,0:T(8,128)S(1)} %get-tuple-element.16), channel_id=1, source_target_pairs={{0,2},{1,3},{2,0},{3,1},{4,6},{5,7},{6,4},{7,5},{8,10},{9,11},{10,... | collective-permute-start | bytes 626696 | tf_op jit(solution)/shard_map/ppermute | solution.py:215
  14.0 6.7 %collective-permute-start.3 = (f32[408,128]{1,0:T(8,128)S(1)}, f32[408,128]{1,0:T(8,128)S(1)}, u32[]{:S(2)}, u32[]{:S(2)}) collective-permute-start(f32[408,128]{1,0:T(8,128)S(1)} %get-tuple-element.16), channel_id=1, source_target_pairs={{2,4},{3,5},{4,2},{5,3},{10,12},{11,13},{12,10},{13,11},{18,20},{1... | collective-permute-start | bytes 626696 | tf_op jit(solution)/shard_map/ppermute | solution.py:215
  14.7 12.6 %collective-permute-start.4 = (f32[408,128]{1,0:T(8,128)S(1)}, f32[408,128]{1,0:T(8,128)S(1)}, u32[]{:S(2)}, u32[]{:S(2)}) collective-permute-start(f32[408,128]{1,0:T(8,128)S(1)} %get-tuple-element.16), channel_id=1, source_target_pairs={{0,4},{1,5},{2,6},{3,7},{4,0},{6,2},{8,12},{9,13},{10,14},{11,15},... | collective-permute-start | bytes 626696 | tf_op jit(solution)/shard_map/ppermute | solution.py:215
  28.0 7.0 %collective-permute-start.5 = (f32[1632,128]{1,0:T(8,128)}, f32[1632,128]{1,0:T(8,128)S(1)}, u32[]{:S(2)}, u32[]{:S(2)}) collective-permute-start(f32[1632,128]{1,0:T(8,128)} %get-tuple-element.5), channel_id=1, source_target_pairs={{0,1},{1,0},{2,3},{3,2},{4,5},{5,4},{6,7},{7,6},{8,9},{9,8},{10,11... | collective-permute-start | bytes 2506760 | tf_op jit(solution)/shard_map/ppermute | solution.py:215
  34.2 0.9 %copy-start = (f32[2,5,5120]{2,0,1:T(2,128)S(1)}, f32[2,5,5120]{2,0,1:T(2,128)}, u32[]{:S(2)}) copy-start(f32[2,5,5120]{2,0,1:T(2,128)} %param.8) | copy-start | bytes 614404
  34.2 0.9 %copy-start.1 = (s32[5120]{0:T(1024)S(1)}, s32[5120]{0:T(1024)}, u32[]{:S(2)}) copy-start(s32[5120]{0:T(1024)} %param.9) | copy-start | bytes 61444
  34.2 0.9 %copy-start.2 = (s32[40]{0:T(128)S(1)}, s32[40]{0:T(128)}, u32[]{:S(2)}) copy-start(s32[40]{0:T(128)} %refs_2_.1) | copy-start | bytes 484

commit v3 on v2

v3 whole, which is shorter than its diff:
```python
import jax
import jax.numpy as jnp
import numpy as np
from jax import lax
from jax.experimental import pallas as pl
from jax.experimental.pallas import tpu as pltpu
from jax.sharding import PartitionSpec as P


def exchange_plan(tiles, neigh):
    half = tiles // 2
    before, after = neigh // 2, neigh - 1 - neigh // 2
    where = np.zeros((half, neigh), np.int32)
    offsets = [
        (p, n, p + n - before)
        for p in range(half)
        for n in range(neigh)
        if 0 <= p + n - before < half
    ]
    if half == 8:
        passes = [[(p, p ^ 2) for p in range(half)], [(p, p ^ 4) for p in range(half)]]
        land = 0
        for p, n, s in offsets:
            chip, other = (s ^ p ^ land) // 2, (s ^ p) % 2
            where[p, n] = 2 * 16 + other if chip == 3 else other * 16 + chip
        return passes, True, land, where
    wanted = set()
    for p, n, s in offsets:
        for core in (0, 1):
            if s // 2 != p // 2:
                wanted.add((2 * (s // 2) + s % 2, 2 * (p // 2) + s % 2))
    reach = max((abs(s // 2 - p // 2) for s, p in wanted), default=0)
    passes, place = [], {(c, c): 0 for c in range(half // 2)}
    for d in range(1, reach + 1):
        for phase in (0, 1):
            pairs = []
            for s, p in sorted(wanted):
                low = min(s // 2, p // 2)
                if abs(s // 2 - p // 2) == d and (low // d) % 2 == phase:
                    pairs.append((s, p))
                    place[s // 2, p // 2] = len(passes) + 1
            if pairs:
                passes.append(pairs)
    for p, n, s in offsets:
        where[p, n] = place[s // 2, p // 2] + 16 * (s % 2 != p % 2)
    return passes, False, 0, where


def tile_facts(tiles, where):
    half = tiles // 2
    return np.array(
        [[*where[t % half], t % 2 == 0, t < half] for t in range(tiles)], np.int32
    )


def encode_kernel(block_ref, count_ref, out_ref):
    neigh, capacity = block_ref.shape
    slot = lax.broadcasted_iota(jnp.int32, (1, capacity), 1)
    out_ref[...] = jnp.full(out_ref.shape, -1.0, jnp.float32)
    for n in range(neigh):
        code = jnp.where(slot < count_ref[0, n], block_ref[n:n + 1, :], -1)
        out_ref[n:n + 1, :capacity] = code.astype(jnp.float32)


def encode(block, count, width):
    neigh = block.shape[0]
    return pl.pallas_call(
        encode_kernel,
        out_shape=jax.ShapeDtypeStruct((neigh + -neigh % 8, width), jnp.float32),
        in_specs=[pl.BlockSpec(memory_space=pltpu.VMEM), pl.BlockSpec(memory_space=pltpu.SMEM)],
        out_specs=pl.BlockSpec(memory_space=pltpu.VMEM),
        cost_estimate=pl.CostEstimate(flops=4096, bytes_accessed=8192, transcendentals=0),
        name="encode",
    )(block, count)


def power(n):
    return 1 << (n - 1).bit_length()


UNROLL = 8


def prepare_kernel(dims, chunks, slot_ref, count_ref, facts_ref, w_hbm, split_ref, list_ref, total_ref, even_ref, buf, sems):
    nblk, sources, capacity, groups, received = dims
    tile = lax.axis_index("comp")
    neigh = received // capacity
    slots, width = w_hbm.shape[:2]
    per = slots // chunks
    copies = [
        pltpu.make_async_copy(
            w_hbm.at[pl.ds(i * per, per)], buf.at[pl.ds(i * per, per)], sems.at[i]
        )
        for i in range(chunks)
    ]
    for copy in copies:
        copy.start()

    room = slots + UNROLL
    low, high = power(slots + 1), power(received)
    for g in range(groups):
        total_ref[g] = 0

    def block(b, carry):
        count = count_ref[b]
        for k in range(sources):
            slot = slot_ref[k, b]
            place = facts_ref[tile, slot // capacity]
            g = place // 16
            n = total_ref[g]
            list_ref[g * room + n] = ((place % 16) * high + slot) * low + b * sources + k
            total_ref[g] = n + (k < count).astype(jnp.int32)
        return carry

    lax.fori_loop(0, nblk, block, 0)
    total_ref[groups] = facts_ref[tile, neigh + 1]
    even_ref[...] = jnp.full(even_ref.shape, facts_ref[tile, neigh])
    for g in range(groups):
        n = total_ref[g]
        for u in range(UNROLL):
            list_ref[g * room + n + u] = slots

    split_ref[slots] = jnp.zeros(split_ref.shape[1:], split_ref.dtype)
    for i in range(chunks):
        copies[i].wait()

        def one(j, carry):
            w = buf[j]
            first = w.astype(jnp.bfloat16)
            rest = (w - first.astype(jnp.float32)).astype(jnp.bfloat16)
            split_ref[j, :, :width] = first
            split_ref[j, :, width:] = rest
            return carry

        lax.fori_loop(i * per, (i + 1) * per, one, 0, unroll=2)


def prepare(slot, count, facts, weight, dims):
    nblk, sources, capacity, groups, received = dims
    slots, width, _ = weight.shape
    chunks = 10 if slots % 10 == 0 else 1
    smem = pl.BlockSpec(memory_space=pltpu.SMEM)
    vmem = pl.BlockSpec(memory_space=pltpu.VMEM)
    return pl.pallas_call(
        lambda *refs: prepare_kernel(dims, chunks, *refs),
        out_shape=(
            pltpu.VMEM((slots + 1, width, 2 * width), jnp.bfloat16),
            jax.ShapeDtypeStruct((groups * (slots + UNROLL),), jnp.int32),
            jax.ShapeDtypeStruct((groups + 1,), jnp.int32),
            jax.ShapeDtypeStruct((8, width), jnp.int32),
        ),
        in_specs=[smem, smem, smem, pl.BlockSpec(memory_space=pl.ANY)],
        out_specs=(vmem, smem, smem, vmem),
        scratch_shapes=[
            pltpu.VMEM(weight.shape, jnp.float32),
            pltpu.SemaphoreType.DMA((chunks,)),
        ],
        compiler_params=pltpu.CompilerParams(vmem_limit_bytes=16 * 2**20),
        cost_estimate=pl.CostEstimate(
            flops=slots * width * width * 4, bytes_accessed=weight.size * 8, transcendentals=0
        ),
        name="prepare",
    )(slot, count, facts, pltpu.with_memory_space_constraint(weight, pltpu.HBM))


def fluxes_of(air, sea, kind):
    wind_u, wind_v, air_temp, air_humid, radiation = air
    sea_temp, ice_conc, ice_temp, current_u, current_v = sea
    wet = (kind > 0).astype(jnp.float32)
    frac = jnp.clip(ice_conc, 0.0, 1.0) * (kind == 2).astype(jnp.float32)
    du = wind_u - current_u
    dv = wind_v - current_v
    speed = jnp.sqrt(du * du + dv * dv + 1.0)
    drag = 0.8 * (1.0 - frac) + 1.2 * frac

    def terms(ts, sens, albedo, latent):
        evap = 0.5 * speed * (0.6 * jnp.exp(0.3 * ts) - air_humid)
        heat = (
            sens * speed * (ts - air_temp)
            + latent * evap
            - ((1.0 - albedo) * radiation - 0.25 * ts)
        )
        return heat, evap

    heat_water, evap_water = terms(sea_temp, 0.6, 0.07, 1.0)
    heat_ice, evap_ice = terms(ice_temp, 0.4, 0.6, 1.2)
    pull = wet * drag * speed
    return (
        pull * du,
        pull * dv,
        wet * ((1.0 - frac) * heat_water + frac * heat_ice),
        wet * ((1.0 - frac) * evap_water + frac * evap_ice),
    )


def remap_group(dims, group, list_ref, total_ref, x_ref, split_ref, acc, starts, base_ref, sem):
    steps, fields, nblk, sources, received, capacity, stride = dims
    span = nblk * steps
    rows = 8
    slots, width = nblk * sources, split_ref.shape[1]
    room = slots + UNROLL
    low, high = power(slots + 1), power(received)

    lines = starts.shape[1]
    for i in range(starts.shape[0]):
        code = x_ref[pl.ds(i * stride + stride - lines, lines), :]
        at = (code * steps + i * stride).astype(jnp.int32)
        starts[i] = jnp.where(code >= 0.0, at, -1)
    copy = pltpu.make_async_copy(starts, base_ref, sem)
    copy.start()
    copy.wait()

    def batch(i, carry):
        for u in range(UNROLL):
            entry = list_ref[group * room + i * UNROLL + u]
            j = entry % low
            slot = (entry // low) % high
            base = base_ref[entry // (low * high), slot // capacity, slot % capacity]
            j = jnp.where(base < 0, slots, j)
            base = jnp.maximum(base, 0)
            x = jnp.concatenate(
                [x_ref[pl.ds(base + m, rows, stride=span), :] for m in range(steps)], axis=0
            )
            first = x.astype(jnp.bfloat16)
            rest = (x - first.astype(jnp.float32)).astype(jnp.bfloat16)
            both = jnp.dot(
                jnp.concatenate([first, rest], axis=0), split_ref[j],
                preferred_element_type=jnp.float32,
            )
            both = both[:, :width] + both[:, width:]
            n = rows * steps
            both = both[:n] + both[n:]
            for m in range(steps):
                at = pl.ds(m * rows * nblk + j // sources, rows, stride=nblk)
                acc[at, :] += both[m * rows:(m + 1) * rows]
        return carry

    lax.fori_loop(0, (total_ref[group] + UNROLL - 1) // UNROLL, batch, 0)


def remap_kernel(dims, group, first, list_ref, total_ref, x_ref, split_ref, *refs):
    if first:
        acc, starts, base_ref, sem = refs
        acc[...] = jnp.zeros_like(acc)
    else:
        before, acc, starts, base_ref, sem = refs
        acc[...] = before[...]
    remap_group(dims, group, list_ref, total_ref, x_ref, split_ref, acc, starts, base_ref, sem)


def last_kernel(dims, group, groups, list_ref, total_ref, x_ref, split_ref, before, state_ref, kind_ref, out_ref, acc, starts, base_ref, sem):
    steps, fields, nblk = dims[:3]
    span = nblk * steps
    acc[...] = before[...]
    remap_group(dims, group, list_ref, total_ref, x_ref, split_ref, acc, starts, base_ref, sem)
    is_air = total_ref[groups] > 0
    for m in range(steps):
        for j in range(nblk // 8):
            mapped = [acc[pl.ds((m * 8 + f) * nblk + 8 * j, 8), :] for f in range(fields)]
            own = [
                state_ref[pl.ds(f * span + 8 * j * steps + m, 8, stride=steps), :]
                for f in range(fields)
            ]
            air = [jnp.where(is_air, s, r) for s, r in zip(own, mapped)]
            sea = [jnp.where(is_air, r, s) for s, r in zip(own, mapped)]
            for o, value in enumerate(fluxes_of(air, sea, kind_ref[pl.ds(8 * j, 8), :])):
                out_ref[pl.ds(m * 4 * nblk + 32 * j + o, 8, stride=4), :] = value


def remap(dims, group, lists, totals, x, tiles, split, before=None, last=None):
    steps, fields, nblk, sources, received, capacity, stride = dims
    width = x.shape[1]
    groups = totals.shape[0] - 1
    table = (tiles, stride - steps * fields * nblk, width)
    sums = (steps * 8 * nblk + 8, width)
    smem = pl.BlockSpec(memory_space=pltpu.SMEM)
    vmem = pl.BlockSpec(memory_space=pltpu.VMEM)
    scratch = [pltpu.VMEM(table, jnp.int32), pltpu.SMEM(table, jnp.int32), pltpu.SemaphoreType.DMA]
    args = [lists, totals, x, pltpu.with_memory_space_constraint(split, pltpu.VMEM)]
    specs = [smem, smem, vmem, vmem]
    if before is not None:
        args.append(before)
        specs.append(vmem)
    if last is None:
        out = jax.ShapeDtypeStruct(sums, jnp.float32)
        body = lambda *refs: remap_kernel(dims, group, before is None, *refs)
    else:
        args += list(last)
        specs += [vmem, vmem]
        out = jax.ShapeDtypeStruct((steps * nblk * 4, width), jnp.float32)
        scratch = [pltpu.VMEM(sums, jnp.float32)] + scratch
        body = lambda *refs: last_kernel(dims, group, groups, *refs)
    return pl.pallas_call(
        body,
        out_shape=out,
        in_specs=specs,
        out_specs=vmem,
        scratch_shapes=scratch,
        compiler_params=pltpu.CompilerParams(vmem_limit_bytes=16 * 2**20),
        cost_estimate=pl.CostEstimate(
            flops=nblk * sources * 32 * width * width,
            bytes_accessed=split.size,
            transcendentals=0 if last is None else 2 * steps * nblk * width,
        ),
        name="remap_last" if last is not None else "remap_%d" % group,
    )(*args)


def local(state, surface_kind, send_block, send_count, src_slot, src_count, remap_weight):
    tiles = lax.axis_size("comp")
    half = tiles // 2
    steps, fields, _ = state.shape
    nblk, sources, width, _ = remap_weight.shape
    neigh, capacity = send_block.shape[1:]
    passes, relayed, land, where = exchange_plan(tiles, neigh)
    span = nblk * steps
    rows = fields * span

    def passed(array, pairs):
        return lax.ppermute(array, "comp", pairs)

    def within(pairs):
        return pairs + [(s + half, t + half) for s, t in pairs]

    def ahead(early, late):
        return lax.optimization_barrier((early, late))

    siblings = [(i, i ^ 1) for i in range(tiles)]

    mine = state.reshape(steps, fields, nblk, width).transpose(1, 2, 0, 3).reshape(rows, width)
    table = encode(send_block[0], send_count, width)
    stride = rows + table.shape[0]
    over = [(i, (i % half ^ land) + (half if i < half else 0)) for i in range(tiles)]
    across = jnp.concatenate([passed(mine, over), passed(table, over)])

    groups = 3 if relayed else 2
    received = neigh * capacity
    split, lists, totals, even = prepare(
        src_slot.T, src_count, jnp.asarray(tile_facts(tiles, where)),
        remap_weight.reshape(nblk * sources, width, width),
        (nblk, sources, capacity, groups, received),
    )
    across, lists = ahead(across, lists)

    spare = jnp.zeros(((8 - fields) * span, width), jnp.float32)
    others = [passed(across, within(pairs)) for pairs in passes]
    near = jnp.concatenate([across] + others + [spare])
    held = 1 + len(passes)
    sibling = passed(near, siblings)

    dims = (steps, fields, nblk, sources, received, capacity, stride)
    last = (mine, surface_kind.reshape(nblk, width))
    sums = remap(dims, 0, lists, totals, near, held, split)
    if relayed:
        by_eight = [o.reshape(-1, 8, width) for o in others]
        relay = passed(
            jnp.where(even[None] > 0, by_eight[1], by_eight[0]).reshape(stride, width),
            within([(p, p ^ 2) if p % 2 == 0 else (p, p ^ 4) for p in range(half)]),
        )
        sums = remap(dims, 1, lists, totals, sibling, held, split, sums)
        relay, sums = ahead(relay, sums)
        extra = jnp.concatenate([relay, passed(relay, siblings), spare])
        out = remap(dims, 2, lists, totals, extra, 2, split, sums, last)
    else:
        out = remap(dims, 1, lists, totals, sibling, held, split, sums, last)
    out = out.reshape(steps, nblk, 4, width).transpose(0, 2, 1, 3)
    return out.reshape(steps, 4, nblk * width)


def solution(mesh):
    return jax.shard_map(
        local,
        mesh=mesh,
        in_specs=(
            P(None, None, ("group", "comp")),
            P("comp"),
            P("comp", None, None),
            P("comp", None),
            P("comp", None),
            P("comp"),
            P("comp", None, None, None),
        ),
        out_specs=P(None, None, ("group", "comp")),
        check_vma=False,
    )
```

time: 41.2 us -> 34.6 us (0.84)
  the two profiles are of different devices: /device:TPU:29 before, /device:TPU:0 now
where the time goes in v3:
time: 34.6 us; the launch traced here: 34.1 us
  Pallas kernels  16.6 us (48%)
  starting transfers between devices  9.08 us (26%)
  waiting for transfers between devices  6.2 us (18%)
  local copies, waits for them, and re-layouts  2.05 us (6%)
    ppermute x7, starting transfers between devices, passed(): return lax.ppermute(array, 'comp', pairs)  9.08 us
    pallas_call x3, Pallas kernels, remap(): pl.pallas_call(body, out_shape=out, in_specs=specs, out_specs=vmem, scrat...  8.97 us
    pallas_call x1, Pallas kernels, prepare(): pl.pallas_call(lambda *refs: prepare_kernel(dims, chunks, *refs), out_sha...  6.21 us
    ppermute x7, waiting for transfers between devices, passed(): return lax.ppermute(array, 'comp', pairs)  6.2 us
    unnamed x10, local copies, waits for them, and re-layouts  2.04 us
    pallas_call x1, Pallas kernels, encode(): pl.pallas_call(encode_kernel, out_shape=jax.ShapeDtypeStruct((neigh + -ne...  1.4 us
  transfers between devices with their start and end apart: 7, of which 4 were waited for; matrix products, arithmetic and copies ran while one was open for 0% of the time, Pallas kernels for 42%

profile of v3, /device:TPU:0, one launch (start us, length us, event | category | flops | bytes accessed | tf_op | source)
XLA Modules:
  0.0 34.1 jit_solution(306302942516797463)
XLA Ops:
  0.0 4.0 %collective-permute-start = (f32[400,128]{1,0:T(8,128)}, f32[400,128]{1,0:T(8,128)S(1)}, u32[]{:S(2)}, u32[]{:S(2)}) collective-permute-start(f32[400,128]{1,0:T(8,128)} %bitcast.16), channel_id=1, source_target_pairs={{0,8},{1,9},{2,10},{3,11},{4,12},{5,13},{6,14},{7,15},{8,0},{9,1},... | collective-permute-start | bytes 614408 | tf_op jit(solution)/shard_map/ppermute | solution.py:320
  4.0 1.4 %encode.1 = f32[8,128]{1,0:T(8,128)} custom-call(s32[8,32]{1,0:T(8,128)} %bitcast.21, s32[1,8]{1,0:T(1,128)} %count_ref.1), custom_call_target="tpu_custom_call" | custom-call | flops 4096 | bytes 8192 | tf_op jit(solution)/shard_map/encode/pallas_call | solution.py:67
  5.4 0.0 collective-permute-start.1
  5.4 0.0 copy-start.2
  5.4 0.7 %copy-done.2 = s32[16,10]{1,0:T(8,128)S(1)} copy-done((s32[16,10]{1,0:T(8,128)S(1)}, s32[16,10]{1,0:T(8,128)}, u32[]{:S(2)}) %copy-start.2) | copy-done | bytes 664
  6.1 0.0 copy-start.3
  6.1 0.7 %copy-done.3 = s32[40,4]{0,1:T(4,128)S(1)} copy-done((s32[40,4]{0,1:T(4,128)S(1)}, s32[40,4]{0,1:T(4,128)}, u32[]{:S(2)}) %copy-start.3) | copy-done | bytes 664
  6.8 0.0 copy-start.4
  6.8 0.7 %copy-done.4 = s32[40]{0:T(128)S(1)} copy-done((s32[40]{0:T(128)S(1)}, s32[40]{0:T(128)}, u32[]{:S(2)}) %copy-start.4) | copy-done | bytes 184
  7.5 6.2 %prepare.1 = (bf16[161,128,256]{2,1,0:T(8,128)(2,1)S(1)}, s32[504]{0:T(512)S(1)}, s32[4]{0:T(128)S(1)}, s32[8,128]{1,0:T(8,128)S(1)}) custom-call(s32[4,40]{1,0:T(4,128)S(1)} %bitcast.19, s32[40]{0:T(128)S(1)} %copy-done.4, s32[16,10]{1,0:T(8,128)S(1)} %copy-done.2, f32[160,128,128]{2,1,0:T(8,128)} %bitcast.20), custom_call_target="tpu_custom_call" | custom-call | flops 10485760 | bytes 20971520 | tf_op jit(solution)/shard_map/prepare/pallas_call | solution.py:144
  13.7 0.2 collective-permute-done.1
  13.9 0.0 collective-permute-done
  13.9 1.8 %collective-permute-start.2 = (f32[408,128]{1,0:T(8,128)S(1)}, f32[408,128]{1,0:T(8,128)S(1)}, u32[]{:S(2)}, u32[]{:S(2)}) collective-permute-start(f32[408,128]{1,0:T(8,128)S(1)} %pad_maximum_fusion.2), channel_id=1, source_target_pairs={{0,4},{1,5},{2,6},{3,7},{4,0},{5,1},{6,2},{7,3},{8,12},{9,13},{10,... | collective-permute-start | bytes 626696 | tf_op jit(solution)/shard_map/ppermute | solution.py:320
  15.7 1.5 %collective-permute-start.3 = (f32[408,128]{1,0:T(8,128)S(1)}, f32[408,128]{1,0:T(8,128)S(1)}, u32[]{:S(2)}, u32[]{:S(2)}) collective-permute-start(f32[408,128]{1,0:T(8,128)S(1)} %pad_maximum_fusion.2), channel_id=1, source_target_pairs={{0,2},{1,3},{2,0},{3,1},{4,6},{5,7},{6,4},{7,5},{8,10},{9,11},{10,... | collective-permute-start | bytes 626696 | tf_op jit(solution)/shard_map/ppermute | solution.py:320
  17.2 3.2 %collective-permute-done.2 = f32[408,128]{1,0:T(8,128)S(1)} collective-permute-done((f32[408,128]{1,0:T(8,128)S(1)}, f32[408,128]{1,0:T(8,128)S(1)}, u32[]{:S(2)}, u32[]{:S(2)}) %collective-permute-start.2) | collective-permute-done | bytes 208928 | tf_op jit(solution)/shard_map/ppermute | solution.py:320
  20.4 1.3 %collective-permute-done.3 = f32[408,128]{1,0:T(8,128)S(1)} collective-permute-done((f32[408,128]{1,0:T(8,128)S(1)}, f32[408,128]{1,0:T(8,128)S(1)}, u32[]{:S(2)}, u32[]{:S(2)}) %collective-permute-start.3) | collective-permute-done | bytes 208928 | tf_op jit(solution)/shard_map/ppermute | solution.py:320
  21.8 0.1 pad_maximum_fusion.refs_2_
  21.8 0.1 collective-permute-start.5
  22.0 1.6 %collective-permute-start.4 = (f32[408,128]{1,0:T(8,128)S(1)}, f32[408,128]{1,0:T(8,128)S(1)}, u32[]{:S(2)}, u32[]{:S(2)}) collective-permute-start(f32[408,128]{1,0:T(8,128)S(1)} %bitcast_select_fusion), channel_id=1, source_target_pairs={{0,2},{1,5},{2,0},{3,7},{4,6},{5,1},{6,4},{7,3},{8,10},{9,13},{10,... | collective-permute-start | bytes 626696 | tf_op jit(solution)/shard_map/ppermute | solution.py:320
  23.6 0.0 copy-start
  23.6 0.0 copy-start.1
  23.6 3.3 %remap_0.1.refs_4_ = f32[648,128]{1,0:T(8,128)S(1)} custom-call(s32[504]{0:T(512)S(1)} %get-tuple-element.14.refs_0_, s32[4]{0:T(128)S(1)} %get-tuple-element.15.refs_1_, f32[1464,128]{1,0:T(8,128)S(1)} %pad_maximum_fusion.refs_2_, bf16[161,128,256]{2,1,0:T(8,128)(2,1)S(1)} %get-tuple-element.18.refs_3_), custom_call_target="tpu_custom_call" | custom-call | flops 83886080 | bytes 5275648 | tf_op jit(solution)/shard_map/remap_0/pallas_call | solution.py:293
  26.9 0.0 collective-permute-done.5.refs_2_
  26.9 3.6 %remap_1.1.refs_4_ = f32[648,128]{1,0:T(8,128)S(1)} custom-call(s32[504]{0:T(512)S(1)} %get-tuple-element.14.refs_0_, s32[4]{0:T(128)S(1)} %get-tuple-element.15.refs_1_, f32[1464,128]{1,0:T(8,128)S(1)} %collective-permute-done.5.refs_2_, bf16[161,128,256]{2,1,0:T(8,128)(2,1)S(1)} %get-tuple-element.18.refs_3_, f32[648,128]{1,0:T(8,128)S(1)} %remap_0.1.refs_4_), custom_call_target="tpu_custom_call" | custom-call | flops 83886080 | bytes 5275648 | tf_op jit(solution)/shard_map/remap_1/pallas_call | solution.py:293
  30.5 0.0 collective-permute-done.4
  30.5 0.1 collective-permute-start.6
  30.6 1.4 %collective-permute-done.6 = f32[408,128]{1,0:T(8,128)S(1)} collective-permute-done((f32[408,128]{1,0:T(8,128)S(1)}, f32[408,128]{1,0:T(8,128)S(1)}, u32[]{:S(2)}, u32[]{:S(2)}) %collective-permute-start.6) | collective-permute-done | bytes 208928 | tf_op jit(solution)/shard_map/ppermute | solution.py:320
  32.1 0.0 copy-done
  32.1 0.0 copy-done.1
  32.1 2.0 %remap_last.1 = f32[320,128]{1,0:T(8,128)} custom-call(s32[504]{0:T(512)S(1)} %get-tuple-element.14.refs_0_, s32[4]{0:T(128)S(1)} %get-tuple-element.15.refs_1_, f32[1056,128]{1,0:T(8,128)S(1)} %pad_maximum_fusion.1.refs_2_, bf16[161,128,256]{2,1,0:T(8,128)(2,1)S(1)} %get-tuple-element.18.refs_3_, f32[648,128]{1,0:T(8,128)S(1)} %remap_1.1.refs_4_, ...), custom_call_target="tpu_custom_call" | custom-call | flops 83886080 | bytes 5275648 | tf_op jit(solution)/shard_map/remap_last/pallas_call | solution.py:293
  (5 shorter events, 0.1 us)
Async XLA Ops:
  0.0 13.9 %collective-permute-start = (f32[400,128]{1,0:T(8,128)}, f32[400,128]{1,0:T(8,128)S(1)}, u32[]{:S(2)}, u32[]{:S(2)}) collective-permute-start(f32[400,128]{1,0:T(8,128)} %bitcast.16), channel_id=1, source_target_pairs={{0,8},{1,9},{2,10},{3,11},{4,12},{5,13},{6,14},{7,15},{8,0},{9,1},... | collective-permute-start | bytes 614408 | tf_op jit(solution)/shard_map/ppermute | solution.py:320
  5.4 8.5 %collective-permute-start.1 = (f32[8,128]{1,0:T(8,128)}, f32[8,128]{1,0:T(8,128)S(1)}, u32[]{:S(2)}, u32[]{:S(2)}) collective-permute-start(f32[8,128]{1,0:T(8,128)} %encode.1), channel_id=1, source_target_pairs={{0,8},{1,9},{2,10},{3,11},{4,12},{5,13},{6,14},{7,15},{8,0},{9,1},... | collective-permute-start | bytes 12296 | tf_op jit(solution)/shard_map/ppermute | solution.py:320
  5.4 0.7 %copy-start.2 = (s32[16,10]{1,0:T(8,128)S(1)}, s32[16,10]{1,0:T(8,128)}, u32[]{:S(2)}) copy-start(s32[16,10]{1,0:T(8,128)} %constant.6.clone.refs_2_) | copy-start | bytes 1924
  6.1 0.7 %copy-start.3 = (s32[40,4]{0,1:T(4,128)S(1)}, s32[40,4]{0,1:T(4,128)}, u32[]{:S(2)}) copy-start(s32[40,4]{0,1:T(4,128)} %param.12) | copy-start | bytes 1924
  6.8 0.7 %copy-start.4 = (s32[40]{0:T(128)S(1)}, s32[40]{0:T(128)}, u32[]{:S(2)}) copy-start(s32[40]{0:T(128)} %refs_1_.1) | copy-start | bytes 484
  13.9 6.5 %collective-permute-start.2 = (f32[408,128]{1,0:T(8,128)S(1)}, f32[408,128]{1,0:T(8,128)S(1)}, u32[]{:S(2)}, u32[]{:S(2)}) collective-permute-start(f32[408,128]{1,0:T(8,128)S(1)} %pad_maximum_fusion.2), channel_id=1, source_target_pairs={{0,4},{1,5},{2,6},{3,7},{4,0},{5,1},{6,2},{7,3},{8,12},{9,13},{10,... | collective-permute-start | bytes 626696 | tf_op jit(solution)/shard_map/ppermute | solution.py:320
  15.7 6.1 %collective-permute-start.3 = (f32[408,128]{1,0:T(8,128)S(1)}, f32[408,128]{1,0:T(8,128)S(1)}, u32[]{:S(2)}, u32[]{:S(2)}) collective-permute-start(f32[408,128]{1,0:T(8,128)S(1)} %pad_maximum_fusion.2), channel_id=1, source_target_pairs={{0,2},{1,3},{2,0},{3,1},{4,6},{5,7},{6,4},{7,5},{8,10},{9,11},{10,... | collective-permute-start | bytes 626696 | tf_op jit(solution)/shard_map/ppermute | solution.py:320
  21.8 5.0 %collective-permute-start.5 = (f32[1464,128]{1,0:T(8,128)S(1)}, f32[1464,128]{1,0:T(8,128)S(1)}, u32[]{:S(2)}, u32[]{:S(2)}) collective-permute-start(f32[1464,128]{1,0:T(8,128)S(1)} %pad_maximum_fusion.refs_2_), channel_id=1, source_target_pairs={{0,1},{1,0},{2,3},{3,2},{4,5},{5,4},{6,7},{7,6},{8,9},{9,8},{10,11... | collective-permute-start | bytes 2248712 | tf_op jit(solution)/shard_map/ppermute | solution.py:320
  22.0 8.5 %collective-permute-start.4 = (f32[408,128]{1,0:T(8,128)S(1)}, f32[408,128]{1,0:T(8,128)S(1)}, u32[]{:S(2)}, u32[]{:S(2)}) collective-permute-start(f32[408,128]{1,0:T(8,128)S(1)} %bitcast_select_fusion), channel_id=1, source_target_pairs={{0,2},{1,5},{2,0},{3,7},{4,6},{5,1},{6,4},{7,3},{8,10},{9,13},{10,... | collective-permute-start | bytes 626696 | tf_op jit(solution)/shard_map/ppermute | solution.py:320
  23.6 8.5 %copy-start = (f32[2,5,5120]{2,0,1:T(2,128)S(1)}, f32[2,5,5120]{2,0,1:T(2,128)}, u32[]{:S(2)}) copy-start(f32[2,5,5120]{2,0,1:T(2,128)} %param.8) | copy-start | bytes 614404
  23.6 8.5 %copy-start.1 = (s32[5120]{0:T(1024)S(1)}, s32[5120]{0:T(1024)}, u32[]{:S(2)}) copy-start(s32[5120]{0:T(1024)} %param.9) | copy-start | bytes 61444
  30.5 1.5 %collective-permute-start.6 = (f32[408,128]{1,0:T(8,128)S(1)}, f32[408,128]{1,0:T(8,128)S(1)}, u32[]{:S(2)}, u32[]{:S(2)}) collective-permute-start(f32[408,128]{1,0:T(8,128)S(1)} %collective-permute-done.4), channel_id=1, source_target_pairs={{0,1},{1,0},{2,3},{3,2},{4,5},{5,4},{6,7},{7,6},{8,9},{9,8},{10,11... | collective-permute-start | bytes 626696 | tf_op jit(solution)/shard_map/ppermute | solution.py:320

commit v4 on v3

--- a/solution.py
+++ b/solution.py
@@ -19,7 +19,7 @@
     ]
     if half == 8:
         passes = [[(p, p ^ 2) for p in range(half)], [(p, p ^ 4) for p in range(half)]]
-        land = 0
+        land = 4
         for p, n, s in offsets:
             chip, other = (s ^ p ^ land) // 2, (s ^ p) % 2
             where[p, n] = 2 * 16 + other if chip == 3 else other * 16 + chip
@@ -78,26 +78,38 @@
     return 1 << (n - 1).bit_length()
 
 
-UNROLL = 8
-
-
-def prepare_kernel(dims, chunks, slot_ref, count_ref, facts_ref, w_hbm, split_ref, list_ref, total_ref, even_ref, buf, sems):
+UNROLL = 16
+
+
+def prepare_kernel(
+    dims, chunks, slot_hbm, count_hbm, facts_hbm, w_hbm, split_ref, list_ref, total_ref, even_ref,
+    buf, slot_ref, count_ref, facts_ref, sems, small_sems,
+):
     nblk, sources, capacity, groups, received = dims
     tile = lax.axis_index("comp")
     neigh = received // capacity
     slots, width = w_hbm.shape[:2]
     per = slots // chunks
+    small = [
+        pltpu.make_async_copy(src, dst, small_sems.at[i])
+        for i, (src, dst) in enumerate(
+            [(slot_hbm, slot_ref), (count_hbm, count_ref), (facts_hbm, facts_ref)]
+        )
+    ]
     copies = [
         pltpu.make_async_copy(
             w_hbm.at[pl.ds(i * per, per)], buf.at[pl.ds(i * per, per)], sems.at[i]
         )
         for i in range(chunks)
     ]
-    for copy in copies:
+    for copy in small + copies:
         copy.start()
+    for copy in small:
+        copy.wait()
 
     room = slots + UNROLL
-    low, high = power(slots + 1), power(received)
+    low = power(slots + 1)
+    lines = neigh + -neigh % 8
     for g in range(groups):
         total_ref[g] = 0
 
@@ -108,7 +120,8 @@
             place = facts_ref[tile, slot // capacity]
             g = place // 16
             n = total_ref[g]
-            list_ref[g * room + n] = ((place % 16) * high + slot) * low + b * sources + k
+            at = ((place % 16) * lines + slot // capacity) * width + slot % capacity
+            list_ref[g * room + n] = at * low + b * sources + k
             total_ref[g] = n + (k < count).astype(jnp.int32)
         return carry
 
@@ -141,6 +154,7 @@
     chunks = 10 if slots % 10 == 0 else 1
     smem = pl.BlockSpec(memory_space=pltpu.SMEM)
     vmem = pl.BlockSpec(memory_space=pltpu.VMEM)
+    args = [pltpu.with_memory_space_constraint(a, pltpu.HBM) for a in (slot, count, facts, weight)]
     return pl.pallas_call(
         lambda *refs: prepare_kernel(dims, chunks, *refs),
         out_shape=(
@@ -149,18 +163,22 @@
             jax.ShapeDtypeStruct((groups + 1,), jnp.int32),
             jax.ShapeDtypeStruct((8, width), jnp.int32),
         ),
-        in_specs=[smem, smem, smem, pl.BlockSpec(memory_space=pl.ANY)],
+        in_specs=[pl.BlockSpec(memory_space=pl.ANY)] * 4,
         out_specs=(vmem, smem, smem, vmem),
         scratch_shapes=[
             pltpu.VMEM(weight.shape, jnp.float32),
+            pltpu.SMEM(slot.shape, jnp.int32),
+            pltpu.SMEM(count.shape, jnp.int32),
+            pltpu.SMEM(facts.shape, jnp.int32),
             pltpu.SemaphoreType.DMA((chunks,)),
+            pltpu.SemaphoreType.DMA((3,)),
         ],
         compiler_params=pltpu.CompilerParams(vmem_limit_bytes=16 * 2**20),
         cost_estimate=pl.CostEstimate(
             flops=slots * width * width * 4, bytes_accessed=weight.size * 8, transcendentals=0
         ),
         name="prepare",
-    )(slot, count, facts, pltpu.with_memory_space_constraint(weight, pltpu.HBM))
+    )(*args)
 
 
 def fluxes_of(air, sea, kind):
@@ -193,29 +211,29 @@
     )
 
 
-def remap_group(dims, group, list_ref, total_ref, x_ref, split_ref, acc, starts, base_ref, sem):
+def remap_group(dims, group, list_ref, total_ref, x_ref, split_ref, before, acc, starts, base_ref, sem):
     steps, fields, nblk, sources, received, capacity, stride = dims
     span = nblk * steps
     rows = 8
     slots, width = nblk * sources, split_ref.shape[1]
     room = slots + UNROLL
-    low, high = power(slots + 1), power(received)
-
-    lines = starts.shape[1]
-    for i in range(starts.shape[0]):
+    low = power(slots + 1)
+
+    lines = stride - steps * fields * nblk
+    for i in range(starts.shape[0] // lines):
         code = x_ref[pl.ds(i * stride + stride - lines, lines), :]
         at = (code * steps + i * stride).astype(jnp.int32)
-        starts[i] = jnp.where(code >= 0.0, at, -1)
+        starts[pl.ds(i * lines, lines), :] = jnp.where(code >= 0.0, at, -1)
     copy = pltpu.make_async_copy(starts, base_ref, sem)
     copy.start()
+    acc[...] = jnp.zeros_like(acc) if before is None else before[...]
     copy.wait()
 
     def batch(i, carry):
         for u in range(UNROLL):
             entry = list_ref[group * room + i * UNROLL + u]
             j = entry % low
-            slot = (entry // low) % high
-            base = base_ref[entry // (low * high), slot // capacity, slot % capacity]
+            base = base_ref[entry // (low * width), (entry // low) % width]
             j = jnp.where(base < 0, slots, j)
             base = jnp.maximum(base, 0)
             x = jnp.concatenate(
@@ -240,19 +258,14 @@
 
 def remap_kernel(dims, group, first, list_ref, total_ref, x_ref, split_ref, *refs):
     if first:
-        acc, starts, base_ref, sem = refs
-        acc[...] = jnp.zeros_like(acc)
-    else:
-        before, acc, starts, base_ref, sem = refs
-        acc[...] = before[...]
-    remap_group(dims, group, list_ref, total_ref, x_ref, split_ref, acc, starts, base_ref, sem)
+        refs = (None,) + refs
+    remap_group(dims, group, list_ref, total_ref, x_ref, split_ref, *refs)
 
 
 def last_kernel(dims, group, groups, list_ref, total_ref, x_ref, split_ref, before, state_ref, kind_ref, out_ref, acc, starts, base_ref, sem):
     steps, fields, nblk = dims[:3]
     span = nblk * steps
-    acc[...] = before[...]
-    remap_group(dims, group, list_ref, total_ref, x_ref, split_ref, acc, starts, base_ref, sem)
+    remap_group(dims, group, list_ref, total_ref, x_ref, split_ref, before, acc, starts, base_ref, sem)
     is_air = total_ref[groups] > 0
     for m in range(steps):
         for j in range(nblk // 8):
@@ -271,7 +284,7 @@
     steps, fields, nblk, sources, received, capacity, stride = dims
     width = x.shape[1]
     groups = totals.shape[0] - 1
-    table = (tiles, stride - steps * fields * nblk, width)
+    table = (tiles * (stride - steps * fields * nblk), width)
     sums = (steps * 8 * nblk + 8, width)
     smem = pl.BlockSpec(memory_space=pltpu.SMEM)
     vmem = pl.BlockSpec(memory_space=pltpu.VMEM)
@@ -344,19 +357,20 @@
 
     spare = jnp.zeros(((8 - fields) * span, width), jnp.float32)
     others = [passed(across, within(pairs)) for pairs in passes]
-    near = jnp.concatenate([across] + others + [spare])
     held = 1 + len(passes)
-    sibling = passed(near, siblings)
-
-    dims = (steps, fields, nblk, sources, received, capacity, stride)
-    last = (mine, surface_kind.reshape(nblk, width))
-    sums = remap(dims, 0, lists, totals, near, held, split)
     if relayed:
         by_eight = [o.reshape(-1, 8, width) for o in others]
         relay = passed(
             jnp.where(even[None] > 0, by_eight[1], by_eight[0]).reshape(stride, width),
             within([(p, p ^ 2) if p % 2 == 0 else (p, p ^ 4) for p in range(half)]),
         )
+    near = jnp.concatenate([across] + others + [spare])
+    sibling = passed(near, siblings)
+
+    dims = (steps, fields, nblk, sources, received, capacity, stride)
+    last = (mine, surface_kind.reshape(nblk, width))
+    sums = remap(dims, 0, lists, totals, near, held, split)
+    if relayed:
         sums = remap(dims, 1, lists, totals, sibling, held, split, sums)
         relay, sums = ahead(relay, sums)
         extra = jnp.concatenate([relay, passed(relay, siblings), spare])

time: 34.6 us -> 32 us (0.925)
  local copies, waits for them, and re-layouts: 2.05 us -> 0.02 us
  Pallas kernels: 16.6 us -> 15.7 us
  starting transfers between devices: 9.08 us -> 9.89 us
  waiting for transfers between devices: 6.2 us -> 5.84 us
    unnamed x10 -> x4, local copies, waits for them, and re-layouts: 2.04 us -> 0.01 us
    pallas_call x3, Pallas kernels: 8.97 us -> 7.69 us  [remap(): pl.pallas_call(body, out_shape=out, in_specs=specs, out_specs=vmem, scrat...]
    ppermute x7, starting transfers between devices: 9.08 us -> 9.89 us  [passed(): return lax.ppermute(array, 'comp', pairs)]
    pallas_call x1, Pallas kernels: 6.21 us -> 6.65 us  [prepare(): pl.pallas_call(lambda *refs: prepare_kernel(dims, chunks, *refs), out_sha...]
    ppermute x7, waiting for transfers between devices: 6.2 us -> 5.84 us  [passed(): return lax.ppermute(array, 'comp', pairs)]
  transfers between devices with their start and end apart: 7 -> 7, of which waited for: 4 -> 3; matrix products, arithmetic and copies ran while one was open for 0% -> 0% of each run, Pallas kernels for 42% -> 39%
where the time goes in v4:
time: 32 us; the launch traced here: 31.7 us
  Pallas kernels  15.7 us (49%)
  starting transfers between devices  9.89 us (31%)
  waiting for transfers between devices  5.84 us (18%)
    ppermute x7, starting transfers between devices, passed(): return lax.ppermute(array, 'comp', pairs)  9.89 us
    pallas_call x3, Pallas kernels, remap(): pl.pallas_call(body, out_shape=out, in_specs=specs, out_specs=vmem, scrat...  7.69 us
    pallas_call x1, Pallas kernels, prepare(): pl.pallas_call(lambda *refs: prepare_kernel(dims, chunks, *refs), out_sha...  6.65 us
    ppermute x7, waiting for transfers between devices, passed(): return lax.ppermute(array, 'comp', pairs)  5.84 us
    pallas_call x1, Pallas kernels, encode(): pl.pallas_call(encode_kernel, out_shape=jax.ShapeDtypeStruct((neigh + -ne...  1.4 us
  transfers between devices with their start and end apart: 7, of which 3 were waited for; matrix products, arithmetic and copies ran while one was open for 0% of the time, Pallas kernels for 39%

profile of v4, /device:TPU:0, one launch (start us, length us, event | category | flops | bytes accessed | tf_op | source)
XLA Modules:
  0.0 31.7 jit_solution(18373323800728936792)
XLA Ops:
  0.0 5.0 %collective-permute-start = (f32[400,128]{1,0:T(8,128)}, f32[400,128]{1,0:T(8,128)S(1)}, u32[]{:S(2)}, u32[]{:S(2)}) collective-permute-start(f32[400,128]{1,0:T(8,128)} %bitcast.16), channel_id=1, source_target_pairs={{0,12},{1,13},{2,14},{3,15},{4,8},{5,9},{6,10},{7,11},{8,4},{9,5},... | collective-permute-start | bytes 614408 | tf_op jit(solution)/shard_map/ppermute | solution.py:333
  5.0 1.4 %encode.1 = f32[8,128]{1,0:T(8,128)} custom-call(s32[8,32]{1,0:T(8,128)} %bitcast.20, s32[1,8]{1,0:T(1,128)} %count_ref.1), custom_call_target="tpu_custom_call" | custom-call | flops 4096 | bytes 8192 | tf_op jit(solution)/shard_map/encode/pallas_call | solution.py:67
  6.4 0.0 collective-permute-start.1
  6.5 6.6 %prepare.1 = (bf16[161,128,256]{2,1,0:T(8,128)(2,1)S(1)}, s32[528]{0:T(1024)S(1)}, s32[4]{0:T(128)S(1)}, s32[8,128]{1,0:T(8,128)S(1)}) custom-call(s32[4,40]{1,0:T(4,128)} %bitcast.21, s32[40]{0:T(128)} %refs_1_.1, s32[16,10]{1,0:T(8,128)} %constant.6.clone.refs_2_, f32[160,128,128]{2,1,0:T(8,128)} %bitcast.19), custom_call_target="tpu_custom_call" | custom-call | flops 10485760 | bytes 20971520 | tf_op jit(solution)/shard_map/prepare/pallas_call | solution.py:158
  13.1 0.0 collective-permute-done.1
  13.1 0.0 collective-permute-done
  13.2 1.6 %collective-permute-start.2 = (f32[408,128]{1,0:T(8,128)S(1)}, f32[408,128]{1,0:T(8,128)S(1)}, u32[]{:S(2)}, u32[]{:S(2)}) collective-permute-start(f32[408,128]{1,0:T(8,128)S(1)} %pad_maximum_fusion.2), channel_id=1, source_target_pairs={{0,4},{1,5},{2,6},{3,7},{4,0},{5,1},{6,2},{7,3},{8,12},{9,13},{10,... | collective-permute-start | bytes 626696 | tf_op jit(solution)/shard_map/ppermute | solution.py:333
  14.7 1.5 %collective-permute-start.3 = (f32[408,128]{1,0:T(8,128)S(1)}, f32[408,128]{1,0:T(8,128)S(1)}, u32[]{:S(2)}, u32[]{:S(2)}) collective-permute-start(f32[408,128]{1,0:T(8,128)S(1)} %pad_maximum_fusion.2), channel_id=1, source_target_pairs={{0,2},{1,3},{2,0},{3,1},{4,6},{5,7},{6,4},{7,5},{8,10},{9,11},{10,... | collective-permute-start | bytes 626696 | tf_op jit(solution)/shard_map/ppermute | solution.py:333
  16.2 3.6 %collective-permute-done.2 = f32[408,128]{1,0:T(8,128)S(1)} collective-permute-done((f32[408,128]{1,0:T(8,128)S(1)}, f32[408,128]{1,0:T(8,128)S(1)}, u32[]{:S(2)}, u32[]{:S(2)}) %collective-permute-start.2) | collective-permute-done | bytes 208928 | tf_op jit(solution)/shard_map/ppermute | solution.py:333
  19.8 0.8 %collective-permute-done.3 = f32[408,128]{1,0:T(8,128)S(1)} collective-permute-done((f32[408,128]{1,0:T(8,128)S(1)}, f32[408,128]{1,0:T(8,128)S(1)}, u32[]{:S(2)}, u32[]{:S(2)}) %collective-permute-start.3) | collective-permute-done | bytes 208928 | tf_op jit(solution)/shard_map/ppermute | solution.py:333
  20.7 0.1 pad_maximum_fusion.refs_2_
  20.7 0.1 collective-permute-start.5
  20.8 1.6 %collective-permute-start.4 = (f32[408,128]{1,0:T(8,128)S(1)}, f32[408,128]{1,0:T(8,128)S(1)}, u32[]{:S(2)}, u32[]{:S(2)}) collective-permute-start(f32[408,128]{1,0:T(8,128)S(1)} %bitcast_select_fusion), channel_id=1, source_target_pairs={{0,2},{1,5},{2,0},{3,7},{4,6},{5,1},{6,4},{7,3},{8,10},{9,13},{10,... | collective-permute-start | bytes 626696 | tf_op jit(solution)/shard_map/ppermute | solution.py:333
  22.4 0.0 copy-start
  22.4 0.0 copy-start.1
  22.4 2.2 %remap_0.1.refs_4_ = f32[648,128]{1,0:T(8,128)S(1)} custom-call(s32[528]{0:T(1024)S(1)} %get-tuple-element.14.refs_0_, s32[4]{0:T(128)S(1)} %get-tuple-element.15.refs_1_, f32[1464,128]{1,0:T(8,128)S(1)} %pad_maximum_fusion.refs_2_, bf16[161,128,256]{2,1,0:T(8,128)(2,1)S(1)} %get-tuple-element.18.refs_3_), custom_call_target="tpu_custom_call" | custom-call | flops 83886080 | bytes 5275648 | tf_op jit(solution)/shard_map/remap_0/pallas_call | solution.py:306
  24.6 0.0 collective-permute-done.5.refs_2_
  24.6 2.2 %remap_1.1.refs_4_ = f32[648,128]{1,0:T(8,128)S(1)} custom-call(s32[528]{0:T(1024)S(1)} %get-tuple-element.14.refs_0_, s32[4]{0:T(128)S(1)} %get-tuple-element.15.refs_1_, f32[1464,128]{1,0:T(8,128)S(1)} %collective-permute-done.5.refs_2_, bf16[161,128,256]{2,1,0:T(8,128)(2,1)S(1)} %get-tuple-element.18.refs_3_, f32[648,128]{1,0:T(8,128)S(1)} %remap_0.1.refs_4_), custom_call_target="tpu_custom_call" | custom-call | flops 83886080 | bytes 5275648 | tf_op jit(solution)/shard_map/remap_1/pallas_call | solution.py:306
  26.8 0.0 collective-permute-done.4
  26.9 0.1 collective-permute-start.6
  27.0 1.4 %collective-permute-done.6 = f32[408,128]{1,0:T(8,128)S(1)} collective-permute-done((f32[408,128]{1,0:T(8,128)S(1)}, f32[408,128]{1,0:T(8,128)S(1)}, u32[]{:S(2)}, u32[]{:S(2)}) %collective-permute-start.6) | collective-permute-done | bytes 208928 | tf_op jit(solution)/shard_map/ppermute | solution.py:333
  28.4 0.0 copy-done
  28.4 0.0 copy-done.1
  28.4 3.3 %remap_last.1 = f32[320,128]{1,0:T(8,128)} custom-call(s32[528]{0:T(1024)S(1)} %get-tuple-element.14.refs_0_, s32[4]{0:T(128)S(1)} %get-tuple-element.15.refs_1_, f32[1056,128]{1,0:T(8,128)S(1)} %pad_maximum_fusion.1.refs_2_, bf16[161,128,256]{2,1,0:T(8,128)(2,1)S(1)} %get-tuple-element.18.refs_3_, f32[648,128]{1,0:T(8,128)S(1)} %remap_1.1.refs_4_, ...), custom_call_target="tpu_custom_call" | custom-call | flops 83886080 | bytes 5275648 | tf_op jit(solution)/shard_map/remap_last/pallas_call | solution.py:306
  (5 shorter events, 0.1 us)
Async XLA Ops:
  0.0 13.1 %collective-permute-start = (f32[400,128]{1,0:T(8,128)}, f32[400,128]{1,0:T(8,128)S(1)}, u32[]{:S(2)}, u32[]{:S(2)}) collective-permute-start(f32[400,128]{1,0:T(8,128)} %bitcast.16), channel_id=1, source_target_pairs={{0,12},{1,13},{2,14},{3,15},{4,8},{5,9},{6,10},{7,11},{8,4},{9,5},... | collective-permute-start | bytes 614408 | tf_op jit(solution)/shard_map/ppermute | solution.py:333
  6.4 6.7 %collective-permute-start.1 = (f32[8,128]{1,0:T(8,128)}, f32[8,128]{1,0:T(8,128)S(1)}, u32[]{:S(2)}, u32[]{:S(2)}) collective-permute-start(f32[8,128]{1,0:T(8,128)} %encode.1), channel_id=1, source_target_pairs={{0,12},{1,13},{2,14},{3,15},{4,8},{5,9},{6,10},{7,11},{8,4},{9,5},... | collective-permute-start | bytes 12296 | tf_op jit(solution)/shard_map/ppermute | solution.py:333
  13.2 6.7 %collective-permute-start.2 = (f32[408,128]{1,0:T(8,128)S(1)}, f32[408,128]{1,0:T(8,128)S(1)}, u32[]{:S(2)}, u32[]{:S(2)}) collective-permute-start(f32[408,128]{1,0:T(8,128)S(1)} %pad_maximum_fusion.2), channel_id=1, source_target_pairs={{0,4},{1,5},{2,6},{3,7},{4,0},{5,1},{6,2},{7,3},{8,12},{9,13},{10,... | collective-permute-start | bytes 626696 | tf_op jit(solution)/shard_map/ppermute | solution.py:333
  14.7 5.9 %collective-permute-start.3 = (f32[408,128]{1,0:T(8,128)S(1)}, f32[408,128]{1,0:T(8,128)S(1)}, u32[]{:S(2)}, u32[]{:S(2)}) collective-permute-start(f32[408,128]{1,0:T(8,128)S(1)} %pad_maximum_fusion.2), channel_id=1, source_target_pairs={{0,2},{1,3},{2,0},{3,1},{4,6},{5,7},{6,4},{7,5},{8,10},{9,11},{10,... | collective-permute-start | bytes 626696 | tf_op jit(solution)/shard_map/ppermute | solution.py:333
  20.7 3.9 %collective-permute-start.5 = (f32[1464,128]{1,0:T(8,128)S(1)}, f32[1464,128]{1,0:T(8,128)S(1)}, u32[]{:S(2)}, u32[]{:S(2)}) collective-permute-start(f32[1464,128]{1,0:T(8,128)S(1)} %pad_maximum_fusion.refs_2_), channel_id=1, source_target_pairs={{0,1},{1,0},{2,3},{3,2},{4,5},{5,4},{6,7},{7,6},{8,9},{9,8},{10,11... | collective-permute-start | bytes 2248712 | tf_op jit(solution)/shard_map/ppermute | solution.py:333
  20.8 6.0 %collective-permute-start.4 = (f32[408,128]{1,0:T(8,128)S(1)}, f32[408,128]{1,0:T(8,128)S(1)}, u32[]{:S(2)}, u32[]{:S(2)}) collective-permute-start(f32[408,128]{1,0:T(8,128)S(1)} %bitcast_select_fusion), channel_id=1, source_target_pairs={{0,2},{1,5},{2,0},{3,7},{4,6},{5,1},{6,4},{7,3},{8,10},{9,13},{10,... | collective-permute-start | bytes 626696 | tf_op jit(solution)/shard_map/ppermute | solution.py:333
  22.4 6.0 %copy-start = (f32[2,5,5120]{2,0,1:T(2,128)S(1)}, f32[2,5,5120]{2,0,1:T(2,128)}, u32[]{:S(2)}) copy-start(f32[2,5,5120]{2,0,1:T(2,128)} %param.8) | copy-start | bytes 614404
  22.4 6.0 %copy-start.1 = (s32[5120]{0:T(1024)S(1)}, s32[5120]{0:T(1024)}, u32[]{:S(2)}) copy-start(s32[5120]{0:T(1024)} %param.9) | copy-start | bytes 61444
  26.9 1.5 %collective-permute-start.6 = (f32[408,128]{1,0:T(8,128)S(1)}, f32[408,128]{1,0:T(8,128)S(1)}, u32[]{:S(2)}, u32[]{:S(2)}) collective-permute-start(f32[408,128]{1,0:T(8,128)S(1)} %collective-permute-done.4), channel_id=1, source_target_pairs={{0,1},{1,0},{2,3},{3,2},{4,5},{5,4},{6,7},{7,6},{8,9},{9,8},{10,11... | collective-permute-start | bytes 626696 | tf_op jit(solution)/shard_map/ppermute | solution.py:333

commit v5 on v4

--- a/solution.py
+++ b/solution.py
@@ -22,7 +22,7 @@
         land = 4
         for p, n, s in offsets:
             chip, other = (s ^ p ^ land) // 2, (s ^ p) % 2
-            where[p, n] = 2 * 16 + other if chip == 3 else other * 16 + chip
+            where[p, n] = (2 + other) * 16 if chip == 3 else other * 16 + chip
         return passes, True, land, where
     wanted = set()
     for p, n, s in offsets:
@@ -82,7 +82,7 @@
 
 
 def prepare_kernel(
-    dims, chunks, slot_hbm, count_hbm, facts_hbm, w_hbm, split_ref, list_ref, total_ref, even_ref,
+    dims, chunks, slot_hbm, count_hbm, facts_hbm, w_hbm, split_ref, plan_ref, even_ref,
     buf, slot_ref, count_ref, facts_ref, sems, small_sems,
 ):
     nblk, sources, capacity, groups, received = dims
@@ -107,51 +107,49 @@
     for copy in small:
         copy.wait()
 
-    room = slots + UNROLL
     low = power(slots + 1)
     lines = neigh + -neigh % 8
-    for g in range(groups):
-        total_ref[g] = 0
-
-    def block(b, carry):
+    even_ref[...] = jnp.full(even_ref.shape, facts_ref[tile, neigh])
+    split_ref[slots] = jnp.zeros(split_ref.shape[1:], split_ref.dtype)
+
+    def block(b, numbers):
         count = count_ref[b]
+        numbers = list(numbers)
         for k in range(sources):
+            j = b * sources + k
             slot = slot_ref[k, b]
             place = facts_ref[tile, slot // capacity]
-            g = place // 16
-            n = total_ref[g]
             at = ((place % 16) * lines + slot // capacity) * width + slot % capacity
-            list_ref[g * room + n] = at * low + b * sources + k
-            total_ref[g] = n + (k < count).astype(jnp.int32)
-        return carry
-
-    lax.fori_loop(0, nblk, block, 0)
-    total_ref[groups] = facts_ref[tile, neigh + 1]
-    even_ref[...] = jnp.full(even_ref.shape, facts_ref[tile, neigh])
-    for g in range(groups):
-        n = total_ref[g]
-        for u in range(UNROLL):
-            list_ref[g * room + n + u] = slots
-
-    split_ref[slots] = jnp.zeros(split_ref.shape[1:], split_ref.dtype)
-    for i in range(chunks):
-        copies[i].wait()
-
-        def one(j, carry):
+            group = place // 16
+            n = numbers[0]
+            for g in range(1, groups):
+                n = jnp.where(group == g, numbers[g], n)
+            plan_ref[group, n] = at * low + j
+            for g in range(groups):
+                numbers[g] += ((group == g) & (k < count)).astype(jnp.int32)
             w = buf[j]
             first = w.astype(jnp.bfloat16)
             rest = (w - first.astype(jnp.float32)).astype(jnp.bfloat16)
             split_ref[j, :, :width] = first
             split_ref[j, :, width:] = rest
-            return carry
-
-        lax.fori_loop(i * per, (i + 1) * per, one, 0, unroll=2)
+        return tuple(numbers)
+
+    numbers = (jnp.int32(0),) * groups
+    blocks = nblk // chunks
+    for i in range(chunks):
+        copies[i].wait()
+        numbers = lax.fori_loop(i * blocks, (i + 1) * blocks, block, numbers)
+    for g in range(groups):
+        for u in range(UNROLL):
+            plan_ref[g, numbers[g] + u] = slots
+        plan_ref[groups, g] = numbers[g]
+    plan_ref[groups, groups] = facts_ref[tile, neigh + 1]
 
 
 def prepare(slot, count, facts, weight, dims):
     nblk, sources, capacity, groups, received = dims
     slots, width, _ = weight.shape
-    chunks = 10 if slots % 10 == 0 else 1
+    chunks = 10 if nblk % 10 == 0 else 1
     smem = pl.BlockSpec(memory_space=pltpu.SMEM)
     vmem = pl.BlockSpec(memory_space=pltpu.VMEM)
     args = [pltpu.with_memory_space_constraint(a, pltpu.HBM) for a in (slot, count, facts, weight)]
@@ -159,12 +157,11 @@
         lambda *refs: prepare_kernel(dims, chunks, *refs),
         out_shape=(
             pltpu.VMEM((slots + 1, width, 2 * width), jnp.bfloat16),
-            jax.ShapeDtypeStruct((groups * (slots + UNROLL),), jnp.int32),
-            jax.ShapeDtypeStruct((groups + 1,), jnp.int32),
+            jax.ShapeDtypeStruct((groups + 1, slots + UNROLL + -(slots + UNROLL) % 128), jnp.int32),
             jax.ShapeDtypeStruct((8, width), jnp.int32),
         ),
         in_specs=[pl.BlockSpec(memory_space=pl.ANY)] * 4,
-        out_specs=(vmem, smem, smem, vmem),
+        out_specs=(vmem, smem, vmem),
         scratch_shapes=[
             pltpu.VMEM(weight.shape, jnp.float32),
             pltpu.SMEM(slot.shape, jnp.int32),
@@ -211,31 +208,35 @@
     )
 
 
-def remap_group(dims, group, list_ref, total_ref, x_ref, split_ref, before, acc, starts, base_ref, sem):
+def remap_group(dims, group, plan_any, x_ref, split_ref, before, acc, plan_ref, starts, base_ref, sems):
     steps, fields, nblk, sources, received, capacity, stride = dims
     span = nblk * steps
     rows = 8
     slots, width = nblk * sources, split_ref.shape[1]
-    room = slots + UNROLL
     low = power(slots + 1)
+    groups = plan_ref.shape[0] - 1
+    fetch = pltpu.make_async_copy(plan_any, plan_ref, sems.at[0])
+    fetch.start()
 
     lines = stride - steps * fields * nblk
     for i in range(starts.shape[0] // lines):
         code = x_ref[pl.ds(i * stride + stride - lines, lines), :]
         at = (code * steps + i * stride).astype(jnp.int32)
         starts[pl.ds(i * lines, lines), :] = jnp.where(code >= 0.0, at, -1)
-    copy = pltpu.make_async_copy(starts, base_ref, sem)
+    copy = pltpu.make_async_copy(starts, base_ref, sems.at[1])
     copy.start()
     acc[...] = jnp.zeros_like(acc) if before is None else before[...]
+    fetch.wait()
     copy.wait()
 
     def batch(i, carry):
+        places = []
         for u in range(UNROLL):
-            entry = list_ref[group * room + i * UNROLL + u]
-            j = entry % low
+            entry = plan_ref[group, i * UNROLL + u]
             base = base_ref[entry // (low * width), (entry // low) % width]
-            j = jnp.where(base < 0, slots, j)
-            base = jnp.maximum(base, 0)
+            j = jnp.where(base < 0, slots, entry % low)
+            places.append((j, jnp.maximum(base, 0)))
+        for j, base in places:
             x = jnp.concatenate(
                 [x_ref[pl.ds(base + m, rows, stride=span), :] for m in range(steps)], axis=0
             )
@@ -253,20 +254,26 @@
                 acc[at, :] += both[m * rows:(m + 1) * rows]
         return carry
 
-    lax.fori_loop(0, (total_ref[group] + UNROLL - 1) // UNROLL, batch, 0)
-
-
-def remap_kernel(dims, group, first, list_ref, total_ref, x_ref, split_ref, *refs):
+    lax.fori_loop(0, (plan_ref[groups, group] + UNROLL - 1) // UNROLL, batch, 0)
+
+
+def remap_kernel(dims, group, first, plan_any, x_ref, split_ref, *refs):
     if first:
         refs = (None,) + refs
-    remap_group(dims, group, list_ref, total_ref, x_ref, split_ref, *refs)
-
-
-def last_kernel(dims, group, groups, list_ref, total_ref, x_ref, split_ref, before, state_ref, kind_ref, out_ref, acc, starts, base_ref, sem):
+    remap_group(dims, group, plan_any, x_ref, split_ref, *refs)
+
+
+def last_kernel(
+    dims, group, plan_any, x_ref, split_ref, before, state_ref, kind_ref, out_ref, acc, plan_ref,
+    starts, base_ref, sems,
+):
     steps, fields, nblk = dims[:3]
     span = nblk * steps
-    remap_group(dims, group, list_ref, total_ref, x_ref, split_ref, before, acc, starts, base_ref, sem)
-    is_air = total_ref[groups] > 0
+    remap_group(
+        dims, group, plan_any, x_ref, split_ref, before, acc, plan_ref, starts, base_ref, sems
+    )
+    groups = plan_ref.shape[0] - 1
+    is_air = plan_ref[groups, groups] > 0
     for m in range(steps):
         for j in range(nblk // 8):
             mapped = [acc[pl.ds((m * 8 + f) * nblk + 8 * j, 8), :] for f in range(fields)]
@@ -280,17 +287,20 @@
                 out_ref[pl.ds(m * 4 * nblk + 32 * j + o, 8, stride=4), :] = value
 
 
-def remap(dims, group, lists, totals, x, tiles, split, before=None, last=None):
+def remap(dims, group, plan, x, tiles, split, before=None, last=None):
     steps, fields, nblk, sources, received, capacity, stride = dims
     width = x.shape[1]
-    groups = totals.shape[0] - 1
     table = (tiles * (stride - steps * fields * nblk), width)
     sums = (steps * 8 * nblk + 8, width)
-    smem = pl.BlockSpec(memory_space=pltpu.SMEM)
     vmem = pl.BlockSpec(memory_space=pltpu.VMEM)
-    scratch = [pltpu.VMEM(table, jnp.int32), pltpu.SMEM(table, jnp.int32), pltpu.SemaphoreType.DMA]
-    args = [lists, totals, x, pltpu.with_memory_space_constraint(split, pltpu.VMEM)]
-    specs = [smem, smem, vmem, vmem]
+    scratch = [
+        pltpu.SMEM(plan.shape, jnp.int32),
+        pltpu.VMEM(table, jnp.int32),
+        pltpu.SMEM(table, jnp.int32),
+        pltpu.SemaphoreType.DMA((2,)),
+    ]
+    args = [plan, x, pltpu.with_memory_space_constraint(split, pltpu.VMEM)]
+    specs = [pl.BlockSpec(memory_space=pl.ANY), vmem, vmem]
     if before is not None:
         args.append(before)
         specs.append(vmem)
@@ -302,7 +312,7 @@
         specs += [vmem, vmem]
         out = jax.ShapeDtypeStruct((steps * nblk * 4, width), jnp.float32)
         scratch = [pltpu.VMEM(sums, jnp.float32)] + scratch
-        body = lambda *refs: last_kernel(dims, group, groups, *refs)
+        body = lambda *refs: last_kernel(dims, group, *refs)
     return pl.pallas_call(
         body,
         out_shape=out,
@@ -346,14 +356,14 @@
     over = [(i, (i % half ^ land) + (half if i < half else 0)) for i in range(tiles)]
     across = jnp.concatenate([passed(mine, over), passed(table, over)])
 
-    groups = 3 if relayed else 2
+    groups = 4 if relayed else 2
     received = neigh * capacity
-    split, lists, totals, even = prepare(
+    split, plan, even = prepare(
         src_slot.T, src_count, jnp.asarray(tile_facts(tiles, where)),
         remap_weight.reshape(nblk * sources, width, width),
         (nblk, sources, capacity, groups, received),
     )
-    across, lists = ahead(across, lists)
+    across, plan = ahead(across, plan)
 
     spare = jnp.zeros(((8 - fields) * span, width), jnp.float32)
     others = [passed(across, within(pairs)) for pairs in passes]
@@ -369,14 +379,15 @@
 
     dims = (steps, fields, nblk, sources, received, capacity, stride)
     last = (mine, surface_kind.reshape(nblk, width))
-    sums = remap(dims, 0, lists, totals, near, held, split)
+    sums = remap(dims, 0, plan, near, held, split)
     if relayed:
-        sums = remap(dims, 1, lists, totals, sibling, held, split, sums)
+        sums = remap(dims, 1, plan, sibling, held, split, sums)
         relay, sums = ahead(relay, sums)
-        extra = jnp.concatenate([relay, passed(relay, siblings), spare])
-        out = remap(dims, 2, lists, totals, extra, 2, split, sums, last)
+        met = passed(relay, siblings)
+        sums = remap(dims, 2, plan, jnp.concatenate([relay, spare]), 1, split, sums)
+        out = remap(dims, 3, plan, jnp.concatenate([met, spare]), 1, split, sums, last)
     else:
-        out = remap(dims, 1, lists, totals, sibling, held, split, sums, last)
+        out = remap(dims, 1, plan, sibling, held, split, sums, last)
     out = out.reshape(steps, nblk, 4, width).transpose(0, 2, 1, 3)
     return out.reshape(steps, 4, nblk * width)
 

time: 32 us -> 31.5 us (0.984)
  waiting for transfers between devices: 5.84 us -> 5.07 us
    ppermute x7, waiting for transfers between devices: 5.84 us -> 5.07 us  [passed(): return lax.ppermute(array, 'comp', pairs)]
    pallas_call x3 -> x4, Pallas kernels: 7.69 us -> 7.98 us  [remap(): pl.pallas_call(body, out_shape=out, in_specs=specs, out_specs=vmem, scrat...]
  transfers between devices with their start and end apart: 7 -> 7, of which waited for: 3 -> 3; matrix products, arithmetic and copies ran while one was open for 0% -> 0% of each run, Pallas kernels for 39% -> 42%
where the time goes in v5:
time: 31.5 us
  Pallas kernels  15.9 us (50%)
  starting transfers between devices  9.9 us (31%)
  waiting for transfers between devices  5.07 us (16%)
    ppermute x7, starting transfers between devices, passed(): return lax.ppermute(array, 'comp', pairs)  9.9 us
    pallas_call x4, Pallas kernels, remap(): pl.pallas_call(body, out_shape=out, in_specs=specs, out_specs=vmem, scrat...  7.98 us
    pallas_call x1, Pallas kernels, prepare(): pl.pallas_call(lambda *refs: prepare_kernel(dims, chunks, *refs), out_sha...  6.54 us
    ppermute x7, waiting for transfers between devices, passed(): return lax.ppermute(array, 'comp', pairs)  5.07 us
    pallas_call x1, Pallas kernels, encode(): pl.pallas_call(encode_kernel, out_shape=jax.ShapeDtypeStruct((neigh + -ne...  1.4 us
  transfers between devices with their start and end apart: 7, of which 3 were waited for; matrix products, arithmetic and copies ran while one was open for 0% of the time, Pallas kernels for 42%

profile of v5, /device:TPU:0, one launch (start us, length us, event | category | flops | bytes accessed | tf_op | source)
XLA Modules:
  0.0 31.5 jit_solution(13924328209418898552)
XLA Ops:
  0.0 5.0 %collective-permute-start = (f32[400,128]{1,0:T(8,128)}, f32[400,128]{1,0:T(8,128)S(1)}, u32[]{:S(2)}, u32[]{:S(2)}) collective-permute-start(f32[400,128]{1,0:T(8,128)} %bitcast.16), channel_id=1, source_target_pairs={{0,12},{1,13},{2,14},{3,15},{4,8},{5,9},{6,10},{7,11},{8,4},{9,5},... | collective-permute-start | bytes 614408 | tf_op jit(solution)/shard_map/ppermute | solution.py:343
  5.0 1.4 %encode.1 = f32[8,128]{1,0:T(8,128)} custom-call(s32[8,32]{1,0:T(8,128)} %bitcast.20, s32[1,8]{1,0:T(1,128)} %count_ref.1), custom_call_target="tpu_custom_call" | custom-call | flops 4096 | bytes 8192 | tf_op jit(solution)/shard_map/encode/pallas_call | solution.py:67
  6.4 0.0 collective-permute-start.1
  6.5 6.5 %prepare.1 = (bf16[161,128,256]{2,1,0:T(8,128)(2,1)S(1)}, s32[5,256]{1,0:T(8,128)S(1)}, s32[8,128]{1,0:T(8,128)S(1)}) custom-call(s32[4,40]{1,0:T(4,128)} %bitcast.21, s32[40]{0:T(128)} %refs_1_.1, s32[16,10]{1,0:T(8,128)} %constant.6.clone.refs_2_, f32[160,128,128]{2,1,0:T(8,128)} %bitcast.19), custom_call_target="tpu_custom_call" | custom-call | flops 10485760 | bytes 20971520 | tf_op jit(solution)/shard_map/prepare/pallas_call | solution.py:156
  13.0 0.0 collective-permute-done.1
  13.0 0.0 collective-permute-done
  13.0 1.7 %collective-permute-start.2 = (f32[408,128]{1,0:T(8,128)S(1)}, f32[408,128]{1,0:T(8,128)S(1)}, u32[]{:S(2)}, u32[]{:S(2)}) collective-permute-start(f32[408,128]{1,0:T(8,128)S(1)} %pad_maximum_fusion), channel_id=1, source_target_pairs={{0,4},{1,5},{2,6},{3,7},{4,0},{5,1},{6,2},{7,3},{8,12},{9,13},{10,... | collective-permute-start | bytes 626696 | tf_op jit(solution)/shard_map/ppermute | solution.py:343
  14.7 1.5 %collective-permute-start.3 = (f32[408,128]{1,0:T(8,128)S(1)}, f32[408,128]{1,0:T(8,128)S(1)}, u32[]{:S(2)}, u32[]{:S(2)}) collective-permute-start(f32[408,128]{1,0:T(8,128)S(1)} %pad_maximum_fusion), channel_id=1, source_target_pairs={{0,2},{1,3},{2,0},{3,1},{4,6},{5,7},{6,4},{7,5},{8,10},{9,11},{10,... | collective-permute-start | bytes 626696 | tf_op jit(solution)/shard_map/ppermute | solution.py:343
  16.2 0.1 pad.5.clone
  16.3 3.4 %collective-permute-done.2 = f32[408,128]{1,0:T(8,128)S(1)} collective-permute-done((f32[408,128]{1,0:T(8,128)S(1)}, f32[408,128]{1,0:T(8,128)S(1)}, u32[]{:S(2)}, u32[]{:S(2)}) %collective-permute-start.2) | collective-permute-done | bytes 208928 | tf_op jit(solution)/shard_map/ppermute | solution.py:343
  19.7 0.9 %collective-permute-done.3 = f32[408,128]{1,0:T(8,128)S(1)} collective-permute-done((f32[408,128]{1,0:T(8,128)S(1)}, f32[408,128]{1,0:T(8,128)S(1)}, u32[]{:S(2)}, u32[]{:S(2)}) %collective-permute-start.3) | collective-permute-done | bytes 208928 | tf_op jit(solution)/shard_map/ppermute | solution.py:343
  20.6 0.3 maximum_maximum_fusion.refs_1_
  20.9 0.1 collective-permute-start.5
  21.0 1.6 %collective-permute-start.4 = (f32[408,128]{1,0:T(8,128)S(1)}, f32[408,128]{1,0:T(8,128)S(1)}, u32[]{:S(2)}, u32[]{:S(2)}) collective-permute-start(f32[408,128]{1,0:T(8,128)S(1)} %bitcast_select_fusion), channel_id=1, source_target_pairs={{0,2},{1,5},{2,0},{3,7},{4,6},{5,1},{6,4},{7,3},{8,10},{9,13},{10,... | collective-permute-start | bytes 626696 | tf_op jit(solution)/shard_map/ppermute | solution.py:343
  22.6 1.8 %remap_0.1.refs_3_ = f32[648,128]{1,0:T(8,128)S(1)} custom-call(s32[5,256]{1,0:T(8,128)S(1)} %get-tuple-element.13.refs_0_, f32[1464,128]{1,0:T(8,128)S(1)} %maximum_maximum_fusion.refs_1_, bf16[161,128,256]{2,1,0:T(8,128)(2,1)S(1)} %get-tuple-element.16.refs_2_), custom_call_target="tpu_custom_call" | custom-call | flops 83886080 | bytes 5275648 | tf_op jit(solution)/shard_map/remap_0/pallas_call | solution.py:316
  24.4 0.0 copy-start
  24.4 0.0 copy-start.1
  24.4 0.0 collective-permute-done.5.refs_1_
  24.4 1.8 %remap_1.1.refs_3_ = f32[648,128]{1,0:T(8,128)S(1)} custom-call(s32[5,256]{1,0:T(8,128)S(1)} %get-tuple-element.13.refs_0_, f32[1464,128]{1,0:T(8,128)S(1)} %collective-permute-done.5.refs_1_, bf16[161,128,256]{2,1,0:T(8,128)(2,1)S(1)} %get-tuple-element.16.refs_2_, f32[648,128]{1,0:T(8,128)S(1)} %remap_0.1.refs_3_), custom_call_target="tpu_custom_call" | custom-call | flops 83886080 | bytes 5275648 | tf_op jit(solution)/shard_map/remap_1/pallas_call | solution.py:316
  26.2 0.7 %collective-permute-done.4 = f32[408,128]{1,0:T(8,128)S(1)} collective-permute-done((f32[408,128]{1,0:T(8,128)S(1)}, f32[408,128]{1,0:T(8,128)S(1)}, u32[]{:S(2)}, u32[]{:S(2)}) %collective-permute-start.4) | collective-permute-done | bytes 208928 | tf_op jit(solution)/shard_map/ppermute | solution.py:343
  26.9 0.0 collective-permute-start.6
  26.9 1.6 %remap_2.1.refs_3_ = f32[648,128]{1,0:T(8,128)S(1)} custom-call(s32[5,256]{1,0:T(8,128)S(1)} %get-tuple-element.13.refs_0_, f32[648,128]{1,0:T(8,128)S(1)} %concatenate.15.refs_1_, bf16[161,128,256]{2,1,0:T(8,128)(2,1)S(1)} %get-tuple-element.16.refs_2_, f32[648,128]{1,0:T(8,128)S(1)} %remap_1.1.refs_3_), custom_call_target="tpu_custom_call" | custom-call | flops 83886080 | bytes 5275648 | tf_op jit(solution)/shard_map/remap_2/pallas_call | solution.py:316
  28.6 0.0 collective-permute-done.6
  28.6 0.0 copy-done
  28.6 0.0 copy-done.1
  28.6 2.8 %remap_last.1 = f32[320,128]{1,0:T(8,128)} custom-call(s32[5,256]{1,0:T(8,128)S(1)} %get-tuple-element.13.refs_0_, f32[648,128]{1,0:T(8,128)S(1)} %concatenate.14.refs_1_, bf16[161,128,256]{2,1,0:T(8,128)(2,1)S(1)} %get-tuple-element.16.refs_2_, f32[648,128]{1,0:T(8,128)S(1)} %remap_2.1.refs_3_, f32[400,128]{1,0:T(8,128)S(1)} %bitcast.17, s32[40,128]{1,0:T(8,128)S(1)} %bitcast.18), custom_call_target="tpu_custom_call" | custom-call | flops 83886080 | bytes 5275648 | tf_op jit(solution)/shard_map/remap_last/pallas_call | solution.py:316
  (6 shorter events, 0.1 us)
Async XLA Ops:
  0.0 13.0 %collective-permute-start = (f32[400,128]{1,0:T(8,128)}, f32[400,128]{1,0:T(8,128)S(1)}, u32[]{:S(2)}, u32[]{:S(2)}) collective-permute-start(f32[400,128]{1,0:T(8,128)} %bitcast.16), channel_id=1, source_target_pairs={{0,12},{1,13},{2,14},{3,15},{4,8},{5,9},{6,10},{7,11},{8,4},{9,5},... | collective-permute-start | bytes 614408 | tf_op jit(solution)/shard_map/ppermute | solution.py:343
  6.4 6.5 %collective-permute-start.1 = (f32[8,128]{1,0:T(8,128)}, f32[8,128]{1,0:T(8,128)S(1)}, u32[]{:S(2)}, u32[]{:S(2)}) collective-permute-start(f32[8,128]{1,0:T(8,128)} %encode.1), channel_id=1, source_target_pairs={{0,12},{1,13},{2,14},{3,15},{4,8},{5,9},{6,10},{7,11},{8,4},{9,5},... | collective-permute-start | bytes 12296 | tf_op jit(solution)/shard_map/ppermute | solution.py:343
  13.0 6.7 %collective-permute-start.2 = (f32[408,128]{1,0:T(8,128)S(1)}, f32[408,128]{1,0:T(8,128)S(1)}, u32[]{:S(2)}, u32[]{:S(2)}) collective-permute-start(f32[408,128]{1,0:T(8,128)S(1)} %pad_maximum_fusion), channel_id=1, source_target_pairs={{0,4},{1,5},{2,6},{3,7},{4,0},{5,1},{6,2},{7,3},{8,12},{9,13},{10,... | collective-permute-start | bytes 626696 | tf_op jit(solution)/shard_map/ppermute | solution.py:343
  14.7 5.9 %collective-permute-start.3 = (f32[408,128]{1,0:T(8,128)S(1)}, f32[408,128]{1,0:T(8,128)S(1)}, u32[]{:S(2)}, u32[]{:S(2)}) collective-permute-start(f32[408,128]{1,0:T(8,128)S(1)} %pad_maximum_fusion), channel_id=1, source_target_pairs={{0,2},{1,3},{2,0},{3,1},{4,6},{5,7},{6,4},{7,5},{8,10},{9,11},{10,... | collective-permute-start | bytes 626696 | tf_op jit(solution)/shard_map/ppermute | solution.py:343
  20.9 3.5 %collective-permute-start.5 = (f32[1464,128]{1,0:T(8,128)S(1)}, f32[1464,128]{1,0:T(8,128)S(1)}, u32[]{:S(2)}, u32[]{:S(2)}) collective-permute-start(f32[1464,128]{1,0:T(8,128)S(1)} %maximum_maximum_fusion.refs_1_), channel_id=1, source_target_pairs={{0,1},{1,0},{2,3},{3,2},{4,5},{5,4},{6,7},{7,6},{8,9},{9,8},{10,11... | collective-permute-start | bytes 2248712 | tf_op jit(solution)/shard_map/ppermute | solution.py:343
  21.0 5.9 %collective-permute-start.4 = (f32[408,128]{1,0:T(8,128)S(1)}, f32[408,128]{1,0:T(8,128)S(1)}, u32[]{:S(2)}, u32[]{:S(2)}) collective-permute-start(f32[408,128]{1,0:T(8,128)S(1)} %bitcast_select_fusion), channel_id=1, source_target_pairs={{0,2},{1,5},{2,0},{3,7},{4,6},{5,1},{6,4},{7,3},{8,10},{9,13},{10,... | collective-permute-start | bytes 626696 | tf_op jit(solution)/shard_map/ppermute | solution.py:343
  24.4 4.2 %copy-start = (f32[2,5,5120]{2,0,1:T(2,128)S(1)}, f32[2,5,5120]{2,0,1:T(2,128)}, u32[]{:S(2)}) copy-start(f32[2,5,5120]{2,0,1:T(2,128)} %param.8) | copy-start | bytes 614404
  24.4 4.2 %copy-start.1 = (s32[5120]{0:T(1024)S(1)}, s32[5120]{0:T(1024)}, u32[]{:S(2)}) copy-start(s32[5120]{0:T(1024)} %param.9) | copy-start | bytes 61444
  26.9 1.7 %collective-permute-start.6 = (f32[408,128]{1,0:T(8,128)S(1)}, f32[408,128]{1,0:T(8,128)S(1)}, u32[]{:S(2)}, u32[]{:S(2)}) collective-permute-start(f32[408,128]{1,0:T(8,128)S(1)} %collective-permute-done.4), channel_id=1, source_target_pairs={{0,1},{1,0},{2,3},{3,2},{4,5},{5,4},{6,7},{7,6},{8,9},{9,8},{10,11... | collective-permute-start | bytes 626696 | tf_op jit(solution)/shard_map/ppermute | solution.py:343

commit v6 on v5

--- a/solution.py
+++ b/solution.py
@@ -18,10 +18,15 @@
         if 0 <= p + n - before < half
     ]
     if half == 8:
-        passes = [[(p, p ^ 2) for p in range(half)], [(p, p ^ 4) for p in range(half)]]
+        passes = [
+            [(p, p ^ (4 if p % 2 else 2)) for p in range(half)],
+            [(p, p ^ (2 if p % 2 else 4)) for p in range(half)],
+        ]
         land = 4
         for p, n, s in offsets:
             chip, other = (s ^ p ^ land) // 2, (s ^ p) % 2
+            if s % 2 and chip in (1, 2):
+                chip = 3 - chip
             where[p, n] = (2 + other) * 16 if chip == 3 else other * 16 + chip
         return passes, True, land, where
     wanted = set()
@@ -49,7 +54,7 @@
 def tile_facts(tiles, where):
     half = tiles // 2
     return np.array(
-        [[*where[t % half], t % 2 == 0, t < half] for t in range(tiles)], np.int32
+        [[*where[t % half], t < half] for t in range(tiles)], np.int32
     )
 
 
@@ -78,11 +83,19 @@
     return 1 << (n - 1).bit_length()
 
 
+def over(x, n):
+    return x >> (n.bit_length() - 1) if n == power(n) else lax.div(x, jnp.int32(n))
+
+
+def rest_of(x, n):
+    return x & (n - 1) if n == power(n) else lax.rem(x, jnp.int32(n))
+
+
 UNROLL = 16
 
 
 def prepare_kernel(
-    dims, chunks, slot_hbm, count_hbm, facts_hbm, w_hbm, split_ref, plan_ref, even_ref,
+    dims, chunks, slot_hbm, count_hbm, facts_hbm, w_hbm, split_ref, plan_ref,
     buf, slot_ref, count_ref, facts_ref, sems, small_sems,
 ):
     nblk, sources, capacity, groups, received = dims
@@ -109,24 +122,27 @@
 
     low = power(slots + 1)
     lines = neigh + -neigh % 8
-    even_ref[...] = jnp.full(even_ref.shape, facts_ref[tile, neigh])
     split_ref[slots] = jnp.zeros(split_ref.shape[1:], split_ref.dtype)
 
     def block(b, numbers):
         count = count_ref[b]
         numbers = list(numbers)
+        slot = [slot_ref[k, b] for k in range(sources)]
+        place = [facts_ref[tile, over(s, capacity)] for s in slot]
+        spots = []
         for k in range(sources):
-            j = b * sources + k
-            slot = slot_ref[k, b]
-            place = facts_ref[tile, slot // capacity]
-            at = ((place % 16) * lines + slot // capacity) * width + slot % capacity
-            group = place // 16
+            line = rest_of(place[k], 16) * lines + over(slot[k], capacity)
+            group = over(place[k], 16)
             n = numbers[0]
             for g in range(1, groups):
                 n = jnp.where(group == g, numbers[g], n)
-            plan_ref[group, n] = at * low + j
             for g in range(groups):
                 numbers[g] += ((group == g) & (k < count)).astype(jnp.int32)
+            spots.append((group, n, (line * width + rest_of(slot[k], capacity)) * low + b * sources + k))
+        for group, n, entry in spots:
+            plan_ref[group, n] = entry
+        for k in range(sources):
+            j = b * sources + k
             w = buf[j]
             first = w.astype(jnp.bfloat16)
             rest = (w - first.astype(jnp.float32)).astype(jnp.bfloat16)
@@ -138,12 +154,12 @@
     blocks = nblk // chunks
     for i in range(chunks):
         copies[i].wait()
-        numbers = lax.fori_loop(i * blocks, (i + 1) * blocks, block, numbers)
+        numbers = lax.fori_loop(i * blocks, (i + 1) * blocks, block, numbers, unroll=2)
     for g in range(groups):
         for u in range(UNROLL):
             plan_ref[g, numbers[g] + u] = slots
         plan_ref[groups, g] = numbers[g]
-    plan_ref[groups, groups] = facts_ref[tile, neigh + 1]
+    plan_ref[groups, groups] = facts_ref[tile, neigh]
 
 
 def prepare(slot, count, facts, weight, dims):
@@ -157,11 +173,10 @@
         lambda *refs: prepare_kernel(dims, chunks, *refs),
         out_shape=(
             pltpu.VMEM((slots + 1, width, 2 * width), jnp.bfloat16),
-            jax.ShapeDtypeStruct((groups + 1, slots + UNROLL + -(slots + UNROLL) % 128), jnp.int32),
-            jax.ShapeDtypeStruct((8, width), jnp.int32),
+            pltpu.SMEM((groups + 1, slots + UNROLL + -(slots + UNROLL) % 128), jnp.int32),
         ),
         in_specs=[pl.BlockSpec(memory_space=pl.ANY)] * 4,
-        out_specs=(vmem, smem, vmem),
+        out_specs=(vmem, smem),
         scratch_shapes=[
             pltpu.VMEM(weight.shape, jnp.float32),
             pltpu.SMEM(slot.shape, jnp.int32),
@@ -215,8 +230,7 @@
     slots, width = nblk * sources, split_ref.shape[1]
     low = power(slots + 1)
     groups = plan_ref.shape[0] - 1
-    fetch = pltpu.make_async_copy(plan_any, plan_ref, sems.at[0])
-    fetch.start()
+    plan_ref = plan_any
 
     lines = stride - steps * fields * nblk
     for i in range(starts.shape[0] // lines):
@@ -226,20 +240,22 @@
     copy = pltpu.make_async_copy(starts, base_ref, sems.at[1])
     copy.start()
     acc[...] = jnp.zeros_like(acc) if before is None else before[...]
-    fetch.wait()
     copy.wait()
+
+    spare = jnp.zeros((rows - fields, width), jnp.float32)
 
     def batch(i, carry):
         places = []
         for u in range(UNROLL):
             entry = plan_ref[group, i * UNROLL + u]
-            base = base_ref[entry // (low * width), (entry // low) % width]
-            j = jnp.where(base < 0, slots, entry % low)
+            base = base_ref[over(entry, low * width), rest_of(over(entry, low), width)]
+            j = jnp.where(base < 0, slots, rest_of(entry, low))
             places.append((j, jnp.maximum(base, 0)))
         for j, base in places:
-            x = jnp.concatenate(
-                [x_ref[pl.ds(base + m, rows, stride=span), :] for m in range(steps)], axis=0
-            )
+            x = []
+            for m in range(steps):
+                x += [x_ref[pl.ds(base + m, fields, stride=span), :], spare]
+            x = jnp.concatenate(x, axis=0)
             first = x.astype(jnp.bfloat16)
             rest = (x - first.astype(jnp.float32)).astype(jnp.bfloat16)
             both = jnp.dot(
@@ -250,11 +266,11 @@
             n = rows * steps
             both = both[:n] + both[n:]
             for m in range(steps):
-                at = pl.ds(m * rows * nblk + j // sources, rows, stride=nblk)
+                at = pl.ds(m * rows * nblk + over(j, sources), rows, stride=nblk)
                 acc[at, :] += both[m * rows:(m + 1) * rows]
         return carry
 
-    lax.fori_loop(0, (plan_ref[groups, group] + UNROLL - 1) // UNROLL, batch, 0)
+    lax.fori_loop(0, over(plan_ref[groups, group] + UNROLL - 1, UNROLL), batch, 0)
 
 
 def remap_kernel(dims, group, first, plan_any, x_ref, split_ref, *refs):
@@ -272,6 +288,7 @@
     remap_group(
         dims, group, plan_any, x_ref, split_ref, before, acc, plan_ref, starts, base_ref, sems
     )
+    plan_ref = plan_any
     groups = plan_ref.shape[0] - 1
     is_air = plan_ref[groups, groups] > 0
     for m in range(steps):
@@ -299,8 +316,8 @@
         pltpu.SMEM(table, jnp.int32),
         pltpu.SemaphoreType.DMA((2,)),
     ]
-    args = [plan, x, pltpu.with_memory_space_constraint(split, pltpu.VMEM)]
-    specs = [pl.BlockSpec(memory_space=pl.ANY), vmem, vmem]
+    args = [pltpu.with_memory_space_constraint(plan, pltpu.SMEM), x, pltpu.with_memory_space_constraint(split, pltpu.VMEM)]
+    specs = [pl.BlockSpec(memory_space=pltpu.SMEM), vmem, vmem]
     if before is not None:
         args.append(before)
         specs.append(vmem)
@@ -358,23 +375,18 @@
 
     groups = 4 if relayed else 2
     received = neigh * capacity
-    split, plan, even = prepare(
+    split, plan = prepare(
         src_slot.T, src_count, jnp.asarray(tile_facts(tiles, where)),
         remap_weight.reshape(nblk * sources, width, width),
         (nblk, sources, capacity, groups, received),
     )
     across, plan = ahead(across, plan)
 
-    spare = jnp.zeros(((8 - fields) * span, width), jnp.float32)
     others = [passed(across, within(pairs)) for pairs in passes]
     held = 1 + len(passes)
     if relayed:
-        by_eight = [o.reshape(-1, 8, width) for o in others]
-        relay = passed(
-            jnp.where(even[None] > 0, by_eight[1], by_eight[0]).reshape(stride, width),
-            within([(p, p ^ 2) if p % 2 == 0 else (p, p ^ 4) for p in range(half)]),
-        )
-    near = jnp.concatenate([across] + others + [spare])
+        relay = passed(others[1], within(passes[0]))
+    near = jnp.concatenate([across] + others)
     sibling = passed(near, siblings)
 
     dims = (steps, fields, nblk, sources, received, capacity, stride)
@@ -384,8 +396,8 @@
         sums = remap(dims, 1, plan, sibling, held, split, sums)
         relay, sums = ahead(relay, sums)
         met = passed(relay, siblings)
-        sums = remap(dims, 2, plan, jnp.concatenate([relay, spare]), 1, split, sums)
-        out = remap(dims, 3, plan, jnp.concatenate([met, spare]), 1, split, sums, last)
+        sums = remap(dims, 2, plan, relay, 1, split, sums)
+        out = remap(dims, 3, plan, met, 1, split, sums, last)
     else:
         out = remap(dims, 1, plan, sibling, held, split, sums, last)
     out = out.reshape(steps, nblk, 4, width).transpose(0, 2, 1, 3)

time: 31.5 us -> 29.7 us (0.943)
  Pallas kernels: 15.9 us -> 12 us
  waiting for transfers between devices: 5.07 us -> 6.63 us
  starting transfers between devices: 9.9 us -> 10.8 us
    pallas_call x4, Pallas kernels: 7.98 us -> 5.95 us  [remap(): pl.pallas_call(body, out_shape=out, in_specs=specs, out_specs=vmem, scrat...]
    pallas_call x1, Pallas kernels: 6.54 us -> 4.61 us  [prepare(): pl.pallas_call(lambda *refs: prepare_kernel(dims, chunks, *refs), out_sha...]
    ppermute x7, waiting for transfers between devices: 5.07 us -> 6.63 us  [passed(): return lax.ppermute(array, 'comp', pairs)]
    ppermute x7, starting transfers between devices: 9.9 us -> 10.8 us  [passed(): return lax.ppermute(array, 'comp', pairs)]
  transfers between devices with their start and end apart: 7 -> 7, of which waited for: 3 -> 4; matrix products, arithmetic and copies ran while one was open for 0% -> 0% of each run, Pallas kernels for 42% -> 34%
where the time goes in v6:
time: 29.7 us; the launch traced here: 29.5 us
  Pallas kernels  12 us (40%)
  starting transfers between devices  10.8 us (36%)
  waiting for transfers between devices  6.63 us (22%)
    ppermute x7, starting transfers between devices, passed(): return lax.ppermute(array, 'comp', pairs)  10.8 us
    ppermute x7, waiting for transfers between devices, passed(): return lax.ppermute(array, 'comp', pairs)  6.63 us
    pallas_call x4, Pallas kernels, remap(): pl.pallas_call(body, out_shape=out, in_specs=specs, out_specs=vmem, scrat...  5.95 us
    pallas_call x1, Pallas kernels, prepare(): pl.pallas_call(lambda *refs: prepare_kernel(dims, chunks, *refs), out_sha...  4.61 us
    pallas_call x1, Pallas kernels, encode(): pl.pallas_call(encode_kernel, out_shape=jax.ShapeDtypeStruct((neigh + -ne...  1.4 us
  transfers between devices with their start and end apart: 7, of which 4 were waited for; matrix products, arithmetic and copies ran while one was open for 0% of the time, Pallas kernels for 34%

profile of v6, /device:TPU:0, one launch (start us, length us, event | category | flops | bytes accessed | tf_op | source)
XLA Modules:
  0.0 29.5 jit_solution(12477587242602122357)
XLA Ops:
  0.0 5.0 %collective-permute-start = (f32[400,128]{1,0:T(8,128)}, f32[400,128]{1,0:T(8,128)S(1)}, u32[]{:S(2)}, u32[]{:S(2)}) collective-permute-start(f32[400,128]{1,0:T(8,128)} %bitcast.14), channel_id=1, source_target_pairs={{0,12},{1,13},{2,14},{3,15},{4,8},{5,9},{6,10},{7,11},{8,4},{9,5},... | collective-permute-start | bytes 614408 | tf_op jit(solution)/shard_map/ppermute | solution.py:360
  5.0 1.4 %encode.1 = f32[8,128]{1,0:T(8,128)} custom-call(s32[8,32]{1,0:T(8,128)} %bitcast.18, s32[1,8]{1,0:T(1,128)} %count_ref.1), custom_call_target="tpu_custom_call" | custom-call | flops 4096 | bytes 8192 | tf_op jit(solution)/shard_map/encode/pallas_call | solution.py:72
  6.4 0.0 collective-permute-start.1
  6.5 4.6 %prepare.1 = (bf16[161,128,256]{2,1,0:T(8,128)(2,1)S(1)}, s32[5,256]{1,0:T(8,128)S(4)}) custom-call(s32[4,40]{1,0:T(4,128)} %bitcast.19, s32[40]{0:T(128)} %refs_1_.1, s32[16,9]{1,0:T(8,128)} %constant.2.clone.refs_2_, f32[160,128,128]{2,1,0:T(8,128)} %bitcast.17), custom_call_target="tpu_custom_call" | custom-call | flops 10485760 | bytes 20971520 | tf_op jit(solution)/shard_map/prepare/pallas_call | solution.py:172
  11.1 1.1 %collective-permute-done.1 = f32[8,128]{1,0:T(8,128)S(1)} collective-permute-done((f32[8,128]{1,0:T(8,128)}, f32[8,128]{1,0:T(8,128)S(1)}, u32[]{:S(2)}, u32[]{:S(2)}) %collective-permute-start.1) | collective-permute-done | bytes 4128 | tf_op jit(solution)/shard_map/ppermute | solution.py:360
  12.2 0.0 collective-permute-done
  12.2 1.6 %collective-permute-start.4 = (f32[408,128]{1,0:T(8,128)S(1)}, f32[408,128]{1,0:T(8,128)S(1)}, u32[]{:S(2)}, u32[]{:S(2)}) collective-permute-start(f32[408,128]{1,0:T(8,128)S(1)} %pad_maximum_fusion), channel_id=1, source_target_pairs={{0,2},{1,5},{2,0},{3,7},{4,6},{5,1},{6,4},{7,3},{8,10},{9,13},{10,... | collective-permute-start | bytes 626696 | tf_op jit(solution)/shard_map/ppermute | solution.py:360
  13.8 2.5 %collective-permute-start.2 = (f32[408,128]{1,0:T(8,128)S(1)}, f32[408,128]{1,0:T(8,128)S(1)}, u32[]{:S(2)}, u32[]{:S(2)}) collective-permute-start(f32[408,128]{1,0:T(8,128)S(1)} %pad_maximum_fusion), channel_id=1, source_target_pairs={{0,4},{1,3},{2,6},{3,1},{4,0},{5,7},{6,2},{7,5},{8,12},{9,11},{10,... | collective-permute-start | bytes 626696 | tf_op jit(solution)/shard_map/ppermute | solution.py:360
  16.2 3.8 %collective-permute-done.4 = f32[408,128]{1,0:T(8,128)S(1)} collective-permute-done((f32[408,128]{1,0:T(8,128)S(1)}, f32[408,128]{1,0:T(8,128)S(1)}, u32[]{:S(2)}, u32[]{:S(2)}) %collective-permute-start.4) | collective-permute-done | bytes 208928 | tf_op jit(solution)/shard_map/ppermute | solution.py:360
  20.1 0.0 collective-permute-done.2
  20.1 0.1 collective-permute-start.5
  20.2 1.5 %collective-permute-start.3 = (f32[408,128]{1,0:T(8,128)S(1)}, f32[408,128]{1,0:T(8,128)S(1)}, u32[]{:S(2)}, u32[]{:S(2)}) collective-permute-start(f32[408,128]{1,0:T(8,128)S(1)} %collective-permute-done.2), channel_id=1, source_target_pairs={{0,2},{1,5},{2,0},{3,7},{4,6},{5,1},{6,4},{7,3},{8,10},{9,13},{10,... | collective-permute-start | bytes 626696 | tf_op jit(solution)/shard_map/ppermute | solution.py:360
  21.8 1.4 %remap_0.1.refs_3_ = f32[648,128]{1,0:T(8,128)S(1)} custom-call(s32[5,256]{1,0:T(8,128)S(4)} %get-tuple-element.12.refs_0_, f32[1224,128]{1,0:T(8,128)S(1)} %constant_dynamic-update-slice_fusion.refs_1_, bf16[161,128,256]{2,1,0:T(8,128)(2,1)S(1)} %get-tuple-element.14.refs_2_), custom_call_target="tpu_custom_call" | custom-call | flops 83886080 | bytes 5275648 | tf_op jit(solution)/shard_map/remap_0/pallas_call | solution.py:333
  23.1 0.0 copy-start
  23.1 0.0 copy-start.1
  23.2 0.0 collective-permute-done.5.refs_1_
  23.2 1.4 %remap_1.1.refs_3_ = f32[648,128]{1,0:T(8,128)S(1)} custom-call(s32[5,256]{1,0:T(8,128)S(4)} %get-tuple-element.12.refs_0_, f32[1224,128]{1,0:T(8,128)S(1)} %collective-permute-done.5.refs_1_, bf16[161,128,256]{2,1,0:T(8,128)(2,1)S(1)} %get-tuple-element.14.refs_2_, f32[648,128]{1,0:T(8,128)S(1)} %remap_0.1.refs_3_), custom_call_target="tpu_custom_call" | custom-call | flops 83886080 | bytes 5275648 | tf_op jit(solution)/shard_map/remap_1/pallas_call | solution.py:333
  24.5 1.5 %collective-permute-done.3.refs_1_ = f32[408,128]{1,0:T(8,128)S(1)} collective-permute-done((f32[408,128]{1,0:T(8,128)S(1)}, f32[408,128]{1,0:T(8,128)S(1)}, u32[]{:S(2)}, u32[]{:S(2)}) %collective-permute-start.3) | collective-permute-done | bytes 208928 | tf_op jit(solution)/shard_map/ppermute | solution.py:360
  26.0 0.0 collective-permute-start.6
  26.0 1.2 %remap_2.1.refs_3_ = f32[648,128]{1,0:T(8,128)S(1)} custom-call(s32[5,256]{1,0:T(8,128)S(4)} %get-tuple-element.12.refs_0_, f32[408,128]{1,0:T(8,128)S(1)} %collective-permute-done.3.refs_1_, bf16[161,128,256]{2,1,0:T(8,128)(2,1)S(1)} %get-tuple-element.14.refs_2_, f32[648,128]{1,0:T(8,128)S(1)} %remap_1.1.refs_3_), custom_call_target="tpu_custom_call" | custom-call | flops 83886080 | bytes 5275648 | tf_op jit(solution)/shard_map/remap_2/pallas_call | solution.py:333
  27.3 0.2 collective-permute-done.6.refs_1_
  27.5 0.0 copy-done
  27.5 0.0 copy-done.1
  27.5 2.0 %remap_last.1 = f32[320,128]{1,0:T(8,128)} custom-call(s32[5,256]{1,0:T(8,128)S(4)} %get-tuple-element.12.refs_0_, f32[408,128]{1,0:T(8,128)S(1)} %collective-permute-done.6.refs_1_, bf16[161,128,256]{2,1,0:T(8,128)(2,1)S(1)} %get-tuple-element.14.refs_2_, f32[648,128]{1,0:T(8,128)S(1)} %remap_2.1.refs_3_, f32[400,128]{1,0:T(8,128)S(1)} %bitcast.15, ...), custom_call_target="tpu_custom_call" | custom-call | flops 83886080 | bytes 5275648 | tf_op jit(solution)/shard_map/remap_last/pallas_call | solution.py:333
  (4 shorter events, 0.1 us)
Async XLA Ops:
  0.0 12.2 %collective-permute-start = (f32[400,128]{1,0:T(8,128)}, f32[400,128]{1,0:T(8,128)S(1)}, u32[]{:S(2)}, u32[]{:S(2)}) collective-permute-start(f32[400,128]{1,0:T(8,128)} %bitcast.14), channel_id=1, source_target_pairs={{0,12},{1,13},{2,14},{3,15},{4,8},{5,9},{6,10},{7,11},{8,4},{9,5},... | collective-permute-start | bytes 614408 | tf_op jit(solution)/shard_map/ppermute | solution.py:360
  6.4 5.7 %collective-permute-start.1 = (f32[8,128]{1,0:T(8,128)}, f32[8,128]{1,0:T(8,128)S(1)}, u32[]{:S(2)}, u32[]{:S(2)}) collective-permute-start(f32[8,128]{1,0:T(8,128)} %encode.1), channel_id=1, source_target_pairs={{0,12},{1,13},{2,14},{3,15},{4,8},{5,9},{6,10},{7,11},{8,4},{9,5},... | collective-permute-start | bytes 12296 | tf_op jit(solution)/shard_map/ppermute | solution.py:360
  12.2 7.8 %collective-permute-start.4 = (f32[408,128]{1,0:T(8,128)S(1)}, f32[408,128]{1,0:T(8,128)S(1)}, u32[]{:S(2)}, u32[]{:S(2)}) collective-permute-start(f32[408,128]{1,0:T(8,128)S(1)} %pad_maximum_fusion), channel_id=1, source_target_pairs={{0,2},{1,5},{2,0},{3,7},{4,6},{5,1},{6,4},{7,3},{8,10},{9,13},{10,... | collective-permute-start | bytes 626696 | tf_op jit(solution)/shard_map/ppermute | solution.py:360
  13.8 6.3 %collective-permute-start.2 = (f32[408,128]{1,0:T(8,128)S(1)}, f32[408,128]{1,0:T(8,128)S(1)}, u32[]{:S(2)}, u32[]{:S(2)}) collective-permute-start(f32[408,128]{1,0:T(8,128)S(1)} %pad_maximum_fusion), channel_id=1, source_target_pairs={{0,4},{1,3},{2,6},{3,1},{4,0},{5,7},{6,2},{7,5},{8,12},{9,11},{10,... | collective-permute-start | bytes 626696 | tf_op jit(solution)/shard_map/ppermute | solution.py:360
  20.1 3.1 %collective-permute-start.5 = (f32[1224,128]{1,0:T(8,128)S(1)}, f32[1224,128]{1,0:T(8,128)S(1)}, u32[]{:S(2)}, u32[]{:S(2)}) collective-permute-start(f32[1224,128]{1,0:T(8,128)S(1)} %constant_dynamic-update-slice_fusion.refs_1_), channel_id=1, source_target_pairs={{0,1},{1,0},{2,3},{3,2},{4,5},{5,4},{6,7},{7,6},{8,9},{9,8},{10,11... | collective-permute-start | bytes 1880072 | tf_op jit(solution)/shard_map/ppermute | solution.py:360
  20.2 5.8 %collective-permute-start.3 = (f32[408,128]{1,0:T(8,128)S(1)}, f32[408,128]{1,0:T(8,128)S(1)}, u32[]{:S(2)}, u32[]{:S(2)}) collective-permute-start(f32[408,128]{1,0:T(8,128)S(1)} %collective-permute-done.2), channel_id=1, source_target_pairs={{0,2},{1,5},{2,0},{3,7},{4,6},{5,1},{6,4},{7,3},{8,10},{9,13},{10,... | collective-permute-start | bytes 626696 | tf_op jit(solution)/shard_map/ppermute | solution.py:360
  23.1 4.4 %copy-start = (f32[2,5,5120]{2,0,1:T(2,128)S(1)}, f32[2,5,5120]{2,0,1:T(2,128)}, u32[]{:S(2)}) copy-start(f32[2,5,5120]{2,0,1:T(2,128)} %param.8) | copy-start | bytes 614404
  23.1 4.4 %copy-start.1 = (s32[5120]{0:T(1024)S(1)}, s32[5120]{0:T(1024)}, u32[]{:S(2)}) copy-start(s32[5120]{0:T(1024)} %param.9) | copy-start | bytes 61444
  26.0 1.5 %collective-permute-start.6 = (f32[408,128]{1,0:T(8,128)S(1)}, f32[408,128]{1,0:T(8,128)S(1)}, u32[]{:S(2)}, u32[]{:S(2)}) collective-permute-start(f32[408,128]{1,0:T(8,128)S(1)} %collective-permute-done.3.refs_1_), channel_id=1, source_target_pairs={{0,1},{1,0},{2,3},{3,2},{4,5},{5,4},{6,7},{7,6},{8,9},{9,8},{10,11... | collective-permute-start | bytes 626696 | tf_op jit(solution)/shard_map/ppermute | solution.py:360

commit v7 on v6

--- a/solution.py
+++ b/solution.py
@@ -92,6 +92,7 @@
 
 
 UNROLL = 16
+LATE = 32
 
 
 def prepare_kernel(
@@ -156,7 +157,7 @@
         copies[i].wait()
         numbers = lax.fori_loop(i * blocks, (i + 1) * blocks, block, numbers, unroll=2)
     for g in range(groups):
-        for u in range(UNROLL):
+        for u in range(LATE):
             plan_ref[g, numbers[g] + u] = slots
         plan_ref[groups, g] = numbers[g]
     plan_ref[groups, groups] = facts_ref[tile, neigh]
@@ -173,7 +174,7 @@
         lambda *refs: prepare_kernel(dims, chunks, *refs),
         out_shape=(
             pltpu.VMEM((slots + 1, width, 2 * width), jnp.bfloat16),
-            pltpu.SMEM((groups + 1, slots + UNROLL + -(slots + UNROLL) % 128), jnp.int32),
+            pltpu.SMEM((groups + 1, slots + LATE + -(slots + LATE) % 128), jnp.int32),
         ),
         in_specs=[pl.BlockSpec(memory_space=pl.ANY)] * 4,
         out_specs=(vmem, smem),
@@ -223,35 +224,15 @@
     )
 
 
-def remap_group(dims, group, plan_any, x_ref, split_ref, before, acc, plan_ref, starts, base_ref, sems):
+def add_slots(dims, number, spot, x_ref, split_ref, acc, each=UNROLL):
     steps, fields, nblk, sources, received, capacity, stride = dims
     span = nblk * steps
     rows = 8
-    slots, width = nblk * sources, split_ref.shape[1]
-    low = power(slots + 1)
-    groups = plan_ref.shape[0] - 1
-    plan_ref = plan_any
-
-    lines = stride - steps * fields * nblk
-    for i in range(starts.shape[0] // lines):
-        code = x_ref[pl.ds(i * stride + stride - lines, lines), :]
-        at = (code * steps + i * stride).astype(jnp.int32)
-        starts[pl.ds(i * lines, lines), :] = jnp.where(code >= 0.0, at, -1)
-    copy = pltpu.make_async_copy(starts, base_ref, sems.at[1])
-    copy.start()
-    acc[...] = jnp.zeros_like(acc) if before is None else before[...]
-    copy.wait()
-
+    width = split_ref.shape[1]
     spare = jnp.zeros((rows - fields, width), jnp.float32)
 
     def batch(i, carry):
-        places = []
-        for u in range(UNROLL):
-            entry = plan_ref[group, i * UNROLL + u]
-            base = base_ref[over(entry, low * width), rest_of(over(entry, low), width)]
-            j = jnp.where(base < 0, slots, rest_of(entry, low))
-            places.append((j, jnp.maximum(base, 0)))
-        for j, base in places:
+        for j, base in [spot(i * each + u) for u in range(each)]:
             x = []
             for m in range(steps):
                 x += [x_ref[pl.ds(base + m, fields, stride=span), :], spare]
@@ -270,27 +251,100 @@
                 acc[at, :] += both[m * rows:(m + 1) * rows]
         return carry
 
-    lax.fori_loop(0, over(plan_ref[groups, group] + UNROLL - 1, UNROLL), batch, 0)
-
-
-def remap_kernel(dims, group, first, plan_any, x_ref, split_ref, *refs):
-    if first:
-        refs = (None,) + refs
-    remap_group(dims, group, plan_any, x_ref, split_ref, *refs)
-
-
-def last_kernel(
-    dims, group, plan_any, x_ref, split_ref, before, state_ref, kind_ref, out_ref, acc, plan_ref,
-    starts, base_ref, sems,
+    lax.fori_loop(0, over(number + each - 1, each), batch, 0)
+
+
+def find_starts(dims, x_ref, tiles, at, starts):
+    steps, fields, nblk, sources, received, capacity, stride = dims
+    lines = stride - steps * fields * nblk
+    for i in range(tiles):
+        code = x_ref[pl.ds(i * stride + stride - lines, lines), :]
+        row = (code * steps + i * stride).astype(jnp.int32)
+        starts[pl.ds(at + i * lines, lines), :] = jnp.where(code >= 0.0, row, -1)
+
+
+def found(dims, entry, line, base_ref):
+    steps, fields, nblk, sources, received, capacity, stride = dims
+    low, width = power(nblk * sources + 1), base_ref.shape[1]
+    base = base_ref[line + over(entry, low * width), rest_of(over(entry, low), width)]
+    j = jnp.where(base < 0, nblk * sources, rest_of(entry, low))
+    return j, jnp.maximum(base, 0)
+
+
+def remap_kernel(dims, group, last, plan_ref, x_ref, split_ref, *refs):
+    refs = list(refs)
+    before = refs.pop(0) if group else None
+    state_ref, kind_ref = (refs.pop(0), refs.pop(0)) if last else (None, None)
+    out_ref = refs.pop(0)
+    acc = refs.pop(0) if last else out_ref
+    starts, base_ref, sem = refs
+    groups = plan_ref.shape[0] - 1
+    lines = dims[-1] - dims[0] * dims[1] * dims[2]
+    find_starts(dims, x_ref, starts.shape[0] // lines, 0, starts)
+    copy = pltpu.make_async_copy(starts, base_ref, sem)
+    copy.start()
+    acc[...] = jnp.zeros_like(acc) if before is None else before[...]
+    copy.wait()
+    add_slots(
+        dims, plan_ref[groups, group], lambda i: found(dims, plan_ref[group, i], 0, base_ref),
+        x_ref, split_ref, acc,
+    )
+    if last:
+        write_fluxes(dims, plan_ref[groups, groups] > 0, state_ref, kind_ref, acc, out_ref)
+
+
+def second_kernel(
+    dims, tiles, plan_ref, x_ref, table_ref, split_ref, before, acc, spots_ref, starts, base_ref, sem,
 ):
+    groups = plan_ref.shape[0] - 1
+    steps = dims[0]
+    lines = dims[-1] - dims[0] * dims[1] * dims[2]
+    low = power(dims[2] * dims[3] + 1)
+    find_starts(dims, x_ref, tiles, 0, starts)
+    for g, code in enumerate((table_ref[...], x_ref[pl.ds(tiles * dims[-1], lines), :])):
+        row = jnp.where(code >= 0.0, (code * steps).astype(jnp.int32), -1)
+        starts[pl.ds((tiles + g) * lines, lines), :] = row
+    copy = pltpu.make_async_copy(starts, base_ref, sem)
+    copy.start()
+    acc[...] = before[...]
+    copy.wait()
+    add_slots(
+        dims, plan_ref[groups, 1], lambda i: found(dims, plan_ref[1, i], 0, base_ref),
+        x_ref, split_ref, acc,
+    )
+    for g in range(2):
+
+        def place(i, carry):
+            for u in range(LATE):
+                at = i * LATE + u
+                j, base = found(dims, plan_ref[2 + g, at], (tiles + g) * lines, base_ref)
+                spots_ref[g, at] = base * low + j
+            return carry
+
+        lax.fori_loop(0, over(plan_ref[groups, 2 + g] + LATE - 1, LATE), place, 0)
+
+
+def relayed_kernel(dims, group, last, plan_ref, spots_ref, x_ref, split_ref, before, *refs):
+    if last:
+        state_ref, kind_ref, out_ref, acc = refs
+    else:
+        (acc,) = refs
+    groups = plan_ref.shape[0] - 1
+    low = power(dims[2] * dims[3] + 1)
+
+    def spot(i):
+        entry = spots_ref[group - 2, i]
+        return rest_of(entry, low), over(entry, low)
+
+    acc[...] = before[...]
+    add_slots(dims, plan_ref[groups, group], spot, x_ref, split_ref, acc, LATE)
+    if last:
+        write_fluxes(dims, plan_ref[groups, groups] > 0, state_ref, kind_ref, acc, out_ref)
+
+
+def write_fluxes(dims, is_air, state_ref, kind_ref, acc, out_ref):
     steps, fields, nblk = dims[:3]
     span = nblk * steps
-    remap_group(
-        dims, group, plan_any, x_ref, split_ref, before, acc, plan_ref, starts, base_ref, sems
-    )
-    plan_ref = plan_any
-    groups = plan_ref.shape[0] - 1
-    is_air = plan_ref[groups, groups] > 0
     for m in range(steps):
         for j in range(nblk // 8):
             mapped = [acc[pl.ds((m * 8 + f) * nblk + 8 * j, 8), :] for f in range(fields)]
@@ -304,37 +358,45 @@
                 out_ref[pl.ds(m * 4 * nblk + 32 * j + o, 8, stride=4), :] = value
 
 
-def remap(dims, group, plan, x, tiles, split, before=None, last=None):
+def remap(dims, group, plan, x, tiles, split, before=None, last=None, table=None, spots=None):
     steps, fields, nblk, sources, received, capacity, stride = dims
     width = x.shape[1]
-    table = (tiles * (stride - steps * fields * nblk), width)
-    sums = (steps * 8 * nblk + 8, width)
+    lines = stride - steps * fields * nblk
+    sums = jax.ShapeDtypeStruct((steps * 8 * nblk + 8, width), jnp.float32)
+    smem = pl.BlockSpec(memory_space=pltpu.SMEM)
     vmem = pl.BlockSpec(memory_space=pltpu.VMEM)
-    scratch = [
-        pltpu.SMEM(plan.shape, jnp.int32),
-        pltpu.VMEM(table, jnp.int32),
-        pltpu.SMEM(table, jnp.int32),
-        pltpu.SemaphoreType.DMA((2,)),
-    ]
-    args = [pltpu.with_memory_space_constraint(plan, pltpu.SMEM), x, pltpu.with_memory_space_constraint(split, pltpu.VMEM)]
-    specs = [pl.BlockSpec(memory_space=pltpu.SMEM), vmem, vmem]
-    if before is not None:
-        args.append(before)
-        specs.append(vmem)
-    if last is None:
-        out = jax.ShapeDtypeStruct(sums, jnp.float32)
-        body = lambda *refs: remap_kernel(dims, group, before is None, *refs)
+    fixed = pltpu.with_memory_space_constraint
+    args = [(fixed(plan, pltpu.SMEM), smem)]
+    if spots is not None:
+        args.append((fixed(spots, pltpu.SMEM), smem))
+    args.append((x, vmem))
+    if table is not None:
+        args.append((table, vmem))
+    args.append((fixed(split, pltpu.VMEM), vmem))
+    args += [(a, vmem) for a in (before,) + (last or ()) if a is not None]
+    found_in = ((tiles + 2 * (table is not None)) * lines, width)
+    scratch = []
+    if spots is None:
+        scratch = [
+            pltpu.VMEM(found_in, jnp.int32), pltpu.SMEM(found_in, jnp.int32), pltpu.SemaphoreType.DMA,
+        ]
+    out, out_specs = sums, vmem
+    if last is not None:
+        out = jax.ShapeDtypeStruct((steps * nblk * 4, width), jnp.float32)
+        scratch = [pltpu.VMEM(sums.shape, jnp.float32)] + scratch
+    if table is not None:
+        body = lambda *refs: second_kernel(dims, tiles, *refs)
+        out = (sums, pltpu.SMEM((2, plan.shape[1]), jnp.int32))
+        out_specs = (vmem, smem)
+    elif spots is not None:
+        body = lambda *refs: relayed_kernel(dims, group, last is not None, *refs)
     else:
-        args += list(last)
-        specs += [vmem, vmem]
-        out = jax.ShapeDtypeStruct((steps * nblk * 4, width), jnp.float32)
-        scratch = [pltpu.VMEM(sums, jnp.float32)] + scratch
-        body = lambda *refs: last_kernel(dims, group, *refs)
+        body = lambda *refs: remap_kernel(dims, group, last is not None, *refs)
     return pl.pallas_call(
         body,
         out_shape=out,
-        in_specs=specs,
-        out_specs=vmem,
+        in_specs=[spec for _, spec in args],
+        out_specs=out_specs,
         scratch_shapes=scratch,
         compiler_params=pltpu.CompilerParams(vmem_limit_bytes=16 * 2**20),
         cost_estimate=pl.CostEstimate(
@@ -343,7 +405,7 @@
             transcendentals=0 if last is None else 2 * steps * nblk * width,
         ),
         name="remap_last" if last is not None else "remap_%d" % group,
-    )(*args)
+    )(*[arg for arg, _ in args])
 
 
 def local(state, surface_kind, send_block, send_count, src_slot, src_count, remap_weight):
@@ -370,8 +432,8 @@
     mine = state.reshape(steps, fields, nblk, width).transpose(1, 2, 0, 3).reshape(rows, width)
     table = encode(send_block[0], send_count, width)
     stride = rows + table.shape[0]
-    over = [(i, (i % half ^ land) + (half if i < half else 0)) for i in range(tiles)]
-    across = jnp.concatenate([passed(mine, over), passed(table, over)])
+    crossing = [(i, (i % half ^ land) + (half if i < half else 0)) for i in range(tiles)]
+    landed, table = passed(mine, crossing), passed(table, crossing)
 
     groups = 4 if relayed else 2
     received = neigh * capacity
@@ -380,24 +442,26 @@
         remap_weight.reshape(nblk * sources, width, width),
         (nblk, sources, capacity, groups, received),
     )
-    across, plan = ahead(across, plan)
+    (landed, table), plan = ahead((landed, table), plan)
+    across = jnp.concatenate([landed, table])
 
     others = [passed(across, within(pairs)) for pairs in passes]
     held = 1 + len(passes)
     if relayed:
         relay = passed(others[1], within(passes[0]))
-    near = jnp.concatenate([across] + others)
+        table = passed(table, within([(p, p ^ 6) for p in range(half)]))
+    near = jnp.concatenate([across] + others + [table] * relayed)
     sibling = passed(near, siblings)
 
     dims = (steps, fields, nblk, sources, received, capacity, stride)
     last = (mine, surface_kind.reshape(nblk, width))
     sums = remap(dims, 0, plan, near, held, split)
     if relayed:
-        sums = remap(dims, 1, plan, sibling, held, split, sums)
+        sums, spots = remap(dims, 1, plan, sibling, held, split, sums, table=table)
         relay, sums = ahead(relay, sums)
         met = passed(relay, siblings)
-        sums = remap(dims, 2, plan, relay, 1, split, sums)
-        out = remap(dims, 3, plan, met, 1, split, sums, last)
+        sums = remap(dims, 2, plan, relay, 1, split, sums, spots=spots)
+        out = remap(dims, 3, plan, met, 1, split, sums, last, spots=spots)
     else:
         out = remap(dims, 1, plan, sibling, held, split, sums, last)
     out = out.reshape(steps, nblk, 4, width).transpose(0, 2, 1, 3)

time: 29.7 us -> 29.6 us (level)
  waiting for transfers between devices: 6.63 us -> 7.69 us
  Pallas kernels: 12 us -> 11.2 us
  starting transfers between devices: 10.8 us -> 10.2 us
    ppermute x7 -> x8, waiting for transfers between devices: 6.63 us -> 7.69 us  [passed(): return lax.ppermute(array, 'comp', pairs)]
    pallas_call x4, Pallas kernels: 5.95 us -> 5.07 us  [remap(): pl.pallas_call(body, out_shape=out, in_specs=[spec for _, spec in args],...]
    ppermute x7 -> x8, starting transfers between devices: 10.8 us -> 10.2 us  [passed(): return lax.ppermute(array, 'comp', pairs)]
  transfers between devices with their start and end apart: 7 -> 8, of which waited for: 4 -> 5; matrix products, arithmetic and copies ran while one was open for 0% -> 0% of each run, Pallas kernels for 34% -> 34%
where the time goes in v7:
time: 29.6 us; the launch traced here: 29.3 us
  Pallas kernels  11.2 us (38%)
  starting transfers between devices  10.2 us (34%)
  waiting for transfers between devices  7.69 us (26%)
    ppermute x8, starting transfers between devices, passed(): return lax.ppermute(array, 'comp', pairs)  10.2 us
    ppermute x8, waiting for transfers between devices, passed(): return lax.ppermute(array, 'comp', pairs)  7.69 us
    pallas_call x4, Pallas kernels, remap(): pl.pallas_call(body, out_shape=out, in_specs=[spec for _, spec in args],...  5.07 us
    pallas_call x1, Pallas kernels, prepare(): pl.pallas_call(lambda *refs: prepare_kernel(dims, chunks, *refs), out_sha...  4.74 us
    pallas_call x1, Pallas kernels, encode(): pl.pallas_call(encode_kernel, out_shape=jax.ShapeDtypeStruct((neigh + -ne...  1.4 us
  transfers between devices with their start and end apart: 8, of which 5 were waited for; matrix products, arithmetic and copies ran while one was open for 0% of the time, Pallas kernels for 34%

profile of v7, /device:TPU:0, one launch (start us, length us, event | category | flops | bytes accessed | tf_op | source)
XLA Modules:
  0.0 29.3 jit_solution(12886701426031830872)
XLA Ops:
  0.0 5.0 %collective-permute-start = (f32[400,128]{1,0:T(8,128)}, f32[400,128]{1,0:T(8,128)S(1)}, u32[]{:S(2)}, u32[]{:S(2)}) collective-permute-start(f32[400,128]{1,0:T(8,128)} %bitcast.14), channel_id=1, source_target_pairs={{0,12},{1,13},{2,14},{3,15},{4,8},{5,9},{6,10},{7,11},{8,4},{9,5},... | collective-permute-start | bytes 614408 | tf_op jit(solution)/shard_map/ppermute | solution.py:422
  5.0 1.4 %encode.1 = f32[8,128]{1,0:T(8,128)} custom-call(s32[8,32]{1,0:T(8,128)} %bitcast.18, s32[1,8]{1,0:T(1,128)} %count_ref.1), custom_call_target="tpu_custom_call" | custom-call | flops 4096 | bytes 8192 | tf_op jit(solution)/shard_map/encode/pallas_call | solution.py:72
  6.4 0.0 collective-permute-start.1
  6.5 4.7 %prepare.1 = (bf16[161,128,256]{2,1,0:T(8,128)(2,1)S(1)}, s32[5,256]{1,0:T(8,128)S(4)}) custom-call(s32[4,40]{1,0:T(4,128)} %bitcast.19, s32[40]{0:T(128)} %refs_1_.1, s32[16,9]{1,0:T(8,128)} %constant.2.clone.refs_2_, f32[160,128,128]{2,1,0:T(8,128)} %bitcast.17), custom_call_target="tpu_custom_call" | custom-call | flops 10485760 | bytes 20971520 | tf_op jit(solution)/shard_map/prepare/pallas_call | solution.py:173
  11.2 1.0 %collective-permute-done.1 = f32[8,128]{1,0:T(8,128)S(1)} collective-permute-done((f32[8,128]{1,0:T(8,128)}, f32[8,128]{1,0:T(8,128)S(1)}, u32[]{:S(2)}, u32[]{:S(2)}) %collective-permute-start.1) | collective-permute-done | bytes 4128 | tf_op jit(solution)/shard_map/ppermute | solution.py:422
  12.2 0.0 collective-permute-done
  12.2 1.6 %collective-permute-start.2 = (f32[408,128]{1,0:T(8,128)S(1)}, f32[408,128]{1,0:T(8,128)S(1)}, u32[]{:S(2)}, u32[]{:S(2)}) collective-permute-start(f32[408,128]{1,0:T(8,128)S(1)} %get-tuple-element.25), channel_id=1, source_target_pairs={{0,2},{1,5},{2,0},{3,7},{4,6},{5,1},{6,4},{7,3},{8,10},{9,13},{10,... | collective-permute-start | bytes 626696 | tf_op jit(solution)/shard_map/ppermute | solution.py:422
  13.8 2.5 %collective-permute-start.3 = (f32[408,128]{1,0:T(8,128)S(1)}, f32[408,128]{1,0:T(8,128)S(1)}, u32[]{:S(2)}, u32[]{:S(2)}) collective-permute-start(f32[408,128]{1,0:T(8,128)S(1)} %get-tuple-element.25), channel_id=1, source_target_pairs={{0,4},{1,3},{2,6},{3,1},{4,0},{5,7},{6,2},{7,5},{8,12},{9,11},{10,... | collective-permute-start | bytes 626696 | tf_op jit(solution)/shard_map/ppermute | solution.py:422
  16.2 0.0 collective-permute-start.4
  16.3 3.9 %collective-permute-done.2 = f32[408,128]{1,0:T(8,128)S(1)} collective-permute-done((f32[408,128]{1,0:T(8,128)S(1)}, f32[408,128]{1,0:T(8,128)S(1)}, u32[]{:S(2)}, u32[]{:S(2)}) %collective-permute-start.2) | collective-permute-done | bytes 208928 | tf_op jit(solution)/shard_map/ppermute | solution.py:422
  20.1 0.0 collective-permute-done.3
  20.2 0.6 %collective-permute-done.4.refs_2_ = f32[8,128]{1,0:T(8,128)S(1)} collective-permute-done((f32[8,128]{1,0:T(8,128)S(1)}, f32[8,128]{1,0:T(8,128)S(1)}, u32[]{:S(2)}, u32[]{:S(2)}) %collective-permute-start.4) | collective-permute-done | bytes 4128 | tf_op jit(solution)/shard_map/ppermute | solution.py:422
  20.8 0.0 collective-permute-start.5
  20.8 1.1 %collective-permute-start.6 = (f32[408,128]{1,0:T(8,128)S(1)}, f32[408,128]{1,0:T(8,128)S(1)}, u32[]{:S(2)}, u32[]{:S(2)}) collective-permute-start(f32[408,128]{1,0:T(8,128)S(1)} %collective-permute-done.3), channel_id=1, source_target_pairs={{0,2},{1,5},{2,0},{3,7},{4,6},{5,1},{6,4},{7,3},{8,10},{9,13},{10,... | collective-permute-start | bytes 626696 | tf_op jit(solution)/shard_map/ppermute | solution.py:422
  21.9 1.4 %remap_0.1.refs_4_ = f32[648,128]{1,0:T(8,128)S(1)} custom-call(s32[5,256]{1,0:T(8,128)S(4)} %get-tuple-element.15.refs_0_, f32[1232,128]{1,0:T(8,128)S(1)} %constant_dynamic-update-slice_fusion.2.refs_1_, bf16[161,128,256]{2,1,0:T(8,128)(2,1)S(1)} %get-tuple-element.18.refs_2_.refs_3_), custom_call_target="tpu_custom_call" | custom-call | flops 83886080 | bytes 5275648 | tf_op jit(solution)/shard_map/remap_0/pallas_call | solution.py:395
  23.3 0.0 copy-start
  23.3 0.0 copy-start.1
  23.3 0.0 collective-permute-done.5.refs_1_
  23.3 2.0 %remap_1.1 = (f32[648,128]{1,0:T(8,128)S(1)}, s32[2,256]{1,0:T(2,128)S(4)}) custom-call(s32[5,256]{1,0:T(8,128)S(4)} %get-tuple-element.15.refs_0_, f32[1232,128]{1,0:T(8,128)S(1)} %collective-permute-done.5.refs_1_, f32[8,128]{1,0:T(8,128)S(1)} %collective-permute-done.4.refs_2_, bf16[161,128,256]{2,1,0:T(8,128)(2,1)S(1)} %get-tuple-element.18.refs_2_.refs_3_, ...), custom_call_target="tpu_custom_call" | custom-call | flops 83886080 | bytes 5275648 | tf_op jit(solution)/shard_map/remap_1/pallas_call | solution.py:395
  25.3 1.3 %collective-permute-done.6.refs_2_ = f32[408,128]{1,0:T(8,128)S(1)} collective-permute-done((f32[408,128]{1,0:T(8,128)S(1)}, f32[408,128]{1,0:T(8,128)S(1)}, u32[]{:S(2)}, u32[]{:S(2)}) %collective-permute-start.6) | collective-permute-done | bytes 208928 | tf_op jit(solution)/shard_map/ppermute | solution.py:422
  26.6 0.0 collective-permute-start.7
  26.6 0.5 %remap_2.1.refs_4_ = f32[648,128]{1,0:T(8,128)S(1)} custom-call(s32[5,256]{1,0:T(8,128)S(4)} %get-tuple-element.15.refs_0_, s32[2,256]{1,0:T(2,128)S(4)} %get-tuple-element.19.refs_1_, f32[408,128]{1,0:T(8,128)S(1)} %collective-permute-done.6.refs_2_, bf16[161,128,256]{2,1,0:T(8,128)(2,1)S(1)} %get-tuple-element.18.refs_2_.refs_3_, ...), custom_call_target="tpu_custom_call" | custom-call | flops 83886080 | bytes 5275648 | tf_op jit(solution)/shard_map/remap_2/pallas_call | solution.py:395
  27.0 1.0 %collective-permute-done.7.refs_2_ = f32[408,128]{1,0:T(8,128)S(1)} collective-permute-done((f32[408,128]{1,0:T(8,128)S(1)}, f32[408,128]{1,0:T(8,128)S(1)}, u32[]{:S(2)}, u32[]{:S(2)}) %collective-permute-start.7) | collective-permute-done | bytes 208928 | tf_op jit(solution)/shard_map/ppermute | solution.py:422
  28.0 0.0 copy-done
  28.0 0.0 copy-done.1
  28.0 1.3 %remap_last.1 = f32[320,128]{1,0:T(8,128)} custom-call(s32[5,256]{1,0:T(8,128)S(4)} %get-tuple-element.15.refs_0_, s32[2,256]{1,0:T(2,128)S(4)} %get-tuple-element.19.refs_1_, f32[408,128]{1,0:T(8,128)S(1)} %collective-permute-done.7.refs_2_, bf16[161,128,256]{2,1,0:T(8,128)(2,1)S(1)} %get-tuple-element.18.refs_2_.refs_3_, f32[648,128]{1,0:T(8,128)S(1)} %remap_2.1.refs_4_, ...), custom_call_target="tpu_custom_call" | custom-call | flops 83886080 | bytes 5275648 | tf_op jit(solution)/shard_map/remap_last/pallas_call | solution.py:395
  (5 shorter events, 0.1 us)
Async XLA Ops:
  0.0 12.2 %collective-permute-start = (f32[400,128]{1,0:T(8,128)}, f32[400,128]{1,0:T(8,128)S(1)}, u32[]{:S(2)}, u32[]{:S(2)}) collective-permute-start(f32[400,128]{1,0:T(8,128)} %bitcast.14), channel_id=1, source_target_pairs={{0,12},{1,13},{2,14},{3,15},{4,8},{5,9},{6,10},{7,11},{8,4},{9,5},... | collective-permute-start | bytes 614408 | tf_op jit(solution)/shard_map/ppermute | solution.py:422
  6.4 5.7 %collective-permute-start.1 = (f32[8,128]{1,0:T(8,128)}, f32[8,128]{1,0:T(8,128)S(1)}, u32[]{:S(2)}, u32[]{:S(2)}) collective-permute-start(f32[8,128]{1,0:T(8,128)} %encode.1), channel_id=1, source_target_pairs={{0,12},{1,13},{2,14},{3,15},{4,8},{5,9},{6,10},{7,11},{8,4},{9,5},... | collective-permute-start | bytes 12296 | tf_op jit(solution)/shard_map/ppermute | solution.py:422
  12.2 7.9 %collective-permute-start.2 = (f32[408,128]{1,0:T(8,128)S(1)}, f32[408,128]{1,0:T(8,128)S(1)}, u32[]{:S(2)}, u32[]{:S(2)}) collective-permute-start(f32[408,128]{1,0:T(8,128)S(1)} %get-tuple-element.25), channel_id=1, source_target_pairs={{0,2},{1,5},{2,0},{3,7},{4,6},{5,1},{6,4},{7,3},{8,10},{9,13},{10,... | collective-permute-start | bytes 626696 | tf_op jit(solution)/shard_map/ppermute | solution.py:422
  13.8 6.3 %collective-permute-start.3 = (f32[408,128]{1,0:T(8,128)S(1)}, f32[408,128]{1,0:T(8,128)S(1)}, u32[]{:S(2)}, u32[]{:S(2)}) collective-permute-start(f32[408,128]{1,0:T(8,128)S(1)} %get-tuple-element.25), channel_id=1, source_target_pairs={{0,4},{1,3},{2,6},{3,1},{4,0},{5,7},{6,2},{7,5},{8,12},{9,11},{10,... | collective-permute-start | bytes 626696 | tf_op jit(solution)/shard_map/ppermute | solution.py:422
  16.2 4.5 %collective-permute-start.4 = (f32[8,128]{1,0:T(8,128)S(1)}, f32[8,128]{1,0:T(8,128)S(1)}, u32[]{:S(2)}, u32[]{:S(2)}) collective-permute-start(f32[8,128]{1,0:T(8,128)S(1)} %collective-permute-done.1), channel_id=1, source_target_pairs={{0,6},{1,7},{2,4},{3,5},{4,2},{5,3},{6,0},{7,1},{8,14},{9,15},{10,... | collective-permute-start | bytes 12296 | tf_op jit(solution)/shard_map/ppermute | solution.py:422
  20.8 2.5 %collective-permute-start.5 = (f32[1232,128]{1,0:T(8,128)S(1)}, f32[1232,128]{1,0:T(8,128)S(1)}, u32[]{:S(2)}, u32[]{:S(2)}) collective-permute-start(f32[1232,128]{1,0:T(8,128)S(1)} %constant_dynamic-update-slice_fusion.2.refs_1_), channel_id=1, source_target_pairs={{0,1},{1,0},{2,3},{3,2},{4,5},{5,4},{6,7},{7,6},{8,9},{9,8},{10,11... | collective-permute-start | bytes 1892360 | tf_op jit(solution)/shard_map/ppermute | solution.py:422
  20.8 5.8 %collective-permute-start.6 = (f32[408,128]{1,0:T(8,128)S(1)}, f32[408,128]{1,0:T(8,128)S(1)}, u32[]{:S(2)}, u32[]{:S(2)}) collective-permute-start(f32[408,128]{1,0:T(8,128)S(1)} %collective-permute-done.3), channel_id=1, source_target_pairs={{0,2},{1,5},{2,0},{3,7},{4,6},{5,1},{6,4},{7,3},{8,10},{9,13},{10,... | collective-permute-start | bytes 626696 | tf_op jit(solution)/shard_map/ppermute | solution.py:422
  23.3 4.8 %copy-start = (f32[2,5,5120]{2,0,1:T(2,128)S(1)}, f32[2,5,5120]{2,0,1:T(2,128)}, u32[]{:S(2)}) copy-start(f32[2,5,5120]{2,0,1:T(2,128)} %param.8) | copy-start | bytes 614404
  23.3 4.7 %copy-start.1 = (s32[5120]{0:T(1024)S(1)}, s32[5120]{0:T(1024)}, u32[]{:S(2)}) copy-start(s32[5120]{0:T(1024)} %param.9) | copy-start | bytes 61444
  26.6 1.5 %collective-permute-start.7 = (f32[408,128]{1,0:T(8,128)S(1)}, f32[408,128]{1,0:T(8,128)S(1)}, u32[]{:S(2)}, u32[]{:S(2)}) collective-permute-start(f32[408,128]{1,0:T(8,128)S(1)} %collective-permute-done.6.refs_2_), channel_id=1, source_target_pairs={{0,1},{1,0},{2,3},{3,2},{4,5},{5,4},{6,7},{7,6},{8,9},{9,8},{10,11... | collective-permute-start | bytes 626696 | tf_op jit(solution)/shard_map/ppermute | solution.py:422

commit v8 on v7

--- a/solution.py
+++ b/solution.py
@@ -301,7 +301,7 @@
     lines = dims[-1] - dims[0] * dims[1] * dims[2]
     low = power(dims[2] * dims[3] + 1)
     find_starts(dims, x_ref, tiles, 0, starts)
-    for g, code in enumerate((table_ref[...], x_ref[pl.ds(tiles * dims[-1], lines), :])):
+    for g, code in enumerate((x_ref[pl.ds(tiles * dims[-1], lines), :], table_ref[...])):
         row = jnp.where(code >= 0.0, (code * steps).astype(jnp.int32), -1)
         starts[pl.ds((tiles + g) * lines, lines), :] = row
     copy = pltpu.make_async_copy(starts, base_ref, sem)
@@ -449,7 +449,7 @@
     held = 1 + len(passes)
     if relayed:
         relay = passed(others[1], within(passes[0]))
-        table = passed(table, within([(p, p ^ 6) for p in range(half)]))
+        table = passed(table, within([(p, p ^ 7) for p in range(half)]))
     near = jnp.concatenate([across] + others + [table] * relayed)
     sibling = passed(near, siblings)
 

time: 29.6 us -> 29.2 us (0.986)
  waiting for transfers between devices: 7.69 us -> 7.04 us
  starting transfers between devices: 10.2 us -> 10.6 us
    ppermute x8, waiting for transfers between devices: 7.69 us -> 7.04 us  [passed(): return lax.ppermute(array, 'comp', pairs)]
    ppermute x8, starting transfers between devices: 10.2 us -> 10.6 us  [passed(): return lax.ppermute(array, 'comp', pairs)]
where the time goes in v8:
time: 29.2 us; the launch traced here: 29 us
  Pallas kernels  11.2 us (38%)
  starting transfers between devices  10.6 us (36%)
  waiting for transfers between devices  7.04 us (24%)
    ppermute x8, starting transfers between devices, passed(): return lax.ppermute(array, 'comp', pairs)  10.6 us
    ppermute x8, waiting for transfers between devices, passed(): return lax.ppermute(array, 'comp', pairs)  7.04 us
    pallas_call x4, Pallas kernels, remap(): pl.pallas_call(body, out_shape=out, in_specs=[spec for _, spec in args],...  5.04 us
    pallas_call x1, Pallas kernels, prepare(): pl.pallas_call(lambda *refs: prepare_kernel(dims, chunks, *refs), out_sha...  4.74 us
    pallas_call x1, Pallas kernels, encode(): pl.pallas_call(encode_kernel, out_shape=jax.ShapeDtypeStruct((neigh + -ne...  1.4 us
  transfers between devices with their start and end apart: 8, of which 5 were waited for; matrix products, arithmetic and copies ran while one was open for 0% of the time, Pallas kernels for 34%

profile of v8, /device:TPU:0, one launch (start us, length us, event | category | flops | bytes accessed | tf_op | source)
XLA Modules:
  0.0 29.0 jit_solution(7933760214167830074)
XLA Ops:
  0.0 5.0 %collective-permute-start = (f32[400,128]{1,0:T(8,128)}, f32[400,128]{1,0:T(8,128)S(1)}, u32[]{:S(2)}, u32[]{:S(2)}) collective-permute-start(f32[400,128]{1,0:T(8,128)} %bitcast.14), channel_id=1, source_target_pairs={{0,12},{1,13},{2,14},{3,15},{4,8},{5,9},{6,10},{7,11},{8,4},{9,5},... | collective-permute-start | bytes 614408 | tf_op jit(solution)/shard_map/ppermute | solution.py:422
  5.0 1.4 %encode.1 = f32[8,128]{1,0:T(8,128)} custom-call(s32[8,32]{1,0:T(8,128)} %bitcast.18, s32[1,8]{1,0:T(1,128)} %count_ref.1), custom_call_target="tpu_custom_call" | custom-call | flops 4096 | bytes 8192 | tf_op jit(solution)/shard_map/encode/pallas_call | solution.py:72
  6.4 0.0 collective-permute-start.1
  6.5 4.7 %prepare.1 = (bf16[161,128,256]{2,1,0:T(8,128)(2,1)S(1)}, s32[5,256]{1,0:T(8,128)S(4)}) custom-call(s32[4,40]{1,0:T(4,128)} %bitcast.19, s32[40]{0:T(128)} %refs_1_.1, s32[16,9]{1,0:T(8,128)} %constant.2.clone.refs_2_, f32[160,128,128]{2,1,0:T(8,128)} %bitcast.17), custom_call_target="tpu_custom_call" | custom-call | flops 10485760 | bytes 20971520 | tf_op jit(solution)/shard_map/prepare/pallas_call | solution.py:173
  11.2 1.0 %collective-permute-done.1 = f32[8,128]{1,0:T(8,128)S(1)} collective-permute-done((f32[8,128]{1,0:T(8,128)}, f32[8,128]{1,0:T(8,128)S(1)}, u32[]{:S(2)}, u32[]{:S(2)}) %collective-permute-start.1) | collective-permute-done | bytes 4128 | tf_op jit(solution)/shard_map/ppermute | solution.py:422
  12.2 0.0 collective-permute-done
  12.2 1.6 %collective-permute-start.2 = (f32[408,128]{1,0:T(8,128)S(1)}, f32[408,128]{1,0:T(8,128)S(1)}, u32[]{:S(2)}, u32[]{:S(2)}) collective-permute-start(f32[408,128]{1,0:T(8,128)S(1)} %get-tuple-element.25), channel_id=1, source_target_pairs={{0,2},{1,5},{2,0},{3,7},{4,6},{5,1},{6,4},{7,3},{8,10},{9,13},{10,... | collective-permute-start | bytes 626696 | tf_op jit(solution)/shard_map/ppermute | solution.py:422
  13.8 2.5 %collective-permute-start.3 = (f32[408,128]{1,0:T(8,128)S(1)}, f32[408,128]{1,0:T(8,128)S(1)}, u32[]{:S(2)}, u32[]{:S(2)}) collective-permute-start(f32[408,128]{1,0:T(8,128)S(1)} %get-tuple-element.25), channel_id=1, source_target_pairs={{0,4},{1,3},{2,6},{3,1},{4,0},{5,7},{6,2},{7,5},{8,12},{9,11},{10,... | collective-permute-start | bytes 626696 | tf_op jit(solution)/shard_map/ppermute | solution.py:422
  16.2 0.0 collective-permute-start.4
  16.3 3.8 %collective-permute-done.2 = f32[408,128]{1,0:T(8,128)S(1)} collective-permute-done((f32[408,128]{1,0:T(8,128)S(1)}, f32[408,128]{1,0:T(8,128)S(1)}, u32[]{:S(2)}, u32[]{:S(2)}) %collective-permute-start.2) | collective-permute-done | bytes 208928 | tf_op jit(solution)/shard_map/ppermute | solution.py:422
  20.1 0.0 collective-permute-done.3
  20.1 0.2 collective-permute-done.4.refs_2_
  20.4 0.1 collective-permute-start.5
  20.5 1.4 %collective-permute-start.6 = (f32[408,128]{1,0:T(8,128)S(1)}, f32[408,128]{1,0:T(8,128)S(1)}, u32[]{:S(2)}, u32[]{:S(2)}) collective-permute-start(f32[408,128]{1,0:T(8,128)S(1)} %collective-permute-done.3), channel_id=1, source_target_pairs={{0,2},{1,5},{2,0},{3,7},{4,6},{5,1},{6,4},{7,3},{8,10},{9,13},{10,... | collective-permute-start | bytes 626696 | tf_op jit(solution)/shard_map/ppermute | solution.py:422
  21.9 1.4 %remap_0.1.refs_4_ = f32[648,128]{1,0:T(8,128)S(1)} custom-call(s32[5,256]{1,0:T(8,128)S(4)} %get-tuple-element.15.refs_0_, f32[1232,128]{1,0:T(8,128)S(1)} %constant_dynamic-update-slice_fusion.2.refs_1_, bf16[161,128,256]{2,1,0:T(8,128)(2,1)S(1)} %get-tuple-element.18.refs_2_.refs_3_), custom_call_target="tpu_custom_call" | custom-call | flops 83886080 | bytes 5275648 | tf_op jit(solution)/shard_map/remap_0/pallas_call | solution.py:395
  23.2 0.0 copy-start
  23.2 0.0 copy-start.1
  23.3 0.0 collective-permute-done.5.refs_1_
  23.3 2.0 %remap_1.1 = (f32[648,128]{1,0:T(8,128)S(1)}, s32[2,256]{1,0:T(2,128)S(4)}) custom-call(s32[5,256]{1,0:T(8,128)S(4)} %get-tuple-element.15.refs_0_, f32[1232,128]{1,0:T(8,128)S(1)} %collective-permute-done.5.refs_1_, f32[8,128]{1,0:T(8,128)S(1)} %collective-permute-done.4.refs_2_, bf16[161,128,256]{2,1,0:T(8,128)(2,1)S(1)} %get-tuple-element.18.refs_2_.refs_3_, ...), custom_call_target="tpu_custom_call" | custom-call | flops 83886080 | bytes 5275648 | tf_op jit(solution)/shard_map/remap_1/pallas_call | solution.py:395
  25.2 1.0 %collective-permute-done.6.refs_2_ = f32[408,128]{1,0:T(8,128)S(1)} collective-permute-done((f32[408,128]{1,0:T(8,128)S(1)}, f32[408,128]{1,0:T(8,128)S(1)}, u32[]{:S(2)}, u32[]{:S(2)}) %collective-permute-start.6) | collective-permute-done | bytes 208928 | tf_op jit(solution)/shard_map/ppermute | solution.py:422
  26.3 0.0 collective-permute-start.7
  26.3 0.5 %remap_2.1.refs_4_ = f32[648,128]{1,0:T(8,128)S(1)} custom-call(s32[5,256]{1,0:T(8,128)S(4)} %get-tuple-element.15.refs_0_, s32[2,256]{1,0:T(2,128)S(4)} %get-tuple-element.19.refs_1_, f32[408,128]{1,0:T(8,128)S(1)} %collective-permute-done.6.refs_2_, bf16[161,128,256]{2,1,0:T(8,128)(2,1)S(1)} %get-tuple-element.18.refs_2_.refs_3_, ...), custom_call_target="tpu_custom_call" | custom-call | flops 83886080 | bytes 5275648 | tf_op jit(solution)/shard_map/remap_2/pallas_call | solution.py:395
  26.8 1.0 %collective-permute-done.7.refs_2_ = f32[408,128]{1,0:T(8,128)S(1)} collective-permute-done((f32[408,128]{1,0:T(8,128)S(1)}, f32[408,128]{1,0:T(8,128)S(1)}, u32[]{:S(2)}, u32[]{:S(2)}) %collective-permute-start.7) | collective-permute-done | bytes 208928 | tf_op jit(solution)/shard_map/ppermute | solution.py:422
  27.7 0.0 copy-done
  27.7 0.0 copy-done.1
  27.7 1.2 %remap_last.1 = f32[320,128]{1,0:T(8,128)} custom-call(s32[5,256]{1,0:T(8,128)S(4)} %get-tuple-element.15.refs_0_, s32[2,256]{1,0:T(2,128)S(4)} %get-tuple-element.19.refs_1_, f32[408,128]{1,0:T(8,128)S(1)} %collective-permute-done.7.refs_2_, bf16[161,128,256]{2,1,0:T(8,128)(2,1)S(1)} %get-tuple-element.18.refs_2_.refs_3_, f32[648,128]{1,0:T(8,128)S(1)} %remap_2.1.refs_4_, ...), custom_call_target="tpu_custom_call" | custom-call | flops 83886080 | bytes 5275648 | tf_op jit(solution)/shard_map/remap_last/pallas_call | solution.py:395
  (5 shorter events, 0.1 us)
Async XLA Ops:
  0.0 12.2 %collective-permute-start = (f32[400,128]{1,0:T(8,128)}, f32[400,128]{1,0:T(8,128)S(1)}, u32[]{:S(2)}, u32[]{:S(2)}) collective-permute-start(f32[400,128]{1,0:T(8,128)} %bitcast.14), channel_id=1, source_target_pairs={{0,12},{1,13},{2,14},{3,15},{4,8},{5,9},{6,10},{7,11},{8,4},{9,5},... | collective-permute-start | bytes 614408 | tf_op jit(solution)/shard_map/ppermute | solution.py:422
  6.4 5.7 %collective-permute-start.1 = (f32[8,128]{1,0:T(8,128)}, f32[8,128]{1,0:T(8,128)S(1)}, u32[]{:S(2)}, u32[]{:S(2)}) collective-permute-start(f32[8,128]{1,0:T(8,128)} %encode.1), channel_id=1, source_target_pairs={{0,12},{1,13},{2,14},{3,15},{4,8},{5,9},{6,10},{7,11},{8,4},{9,5},... | collective-permute-start | bytes 12296 | tf_op jit(solution)/shard_map/ppermute | solution.py:422
  12.2 7.8 %collective-permute-start.2 = (f32[408,128]{1,0:T(8,128)S(1)}, f32[408,128]{1,0:T(8,128)S(1)}, u32[]{:S(2)}, u32[]{:S(2)}) collective-permute-start(f32[408,128]{1,0:T(8,128)S(1)} %get-tuple-element.25), channel_id=1, source_target_pairs={{0,2},{1,5},{2,0},{3,7},{4,6},{5,1},{6,4},{7,3},{8,10},{9,13},{10,... | collective-permute-start | bytes 626696 | tf_op jit(solution)/shard_map/ppermute | solution.py:422
  13.8 6.3 %collective-permute-start.3 = (f32[408,128]{1,0:T(8,128)S(1)}, f32[408,128]{1,0:T(8,128)S(1)}, u32[]{:S(2)}, u32[]{:S(2)}) collective-permute-start(f32[408,128]{1,0:T(8,128)S(1)} %get-tuple-element.25), channel_id=1, source_target_pairs={{0,4},{1,3},{2,6},{3,1},{4,0},{5,7},{6,2},{7,5},{8,12},{9,11},{10,... | collective-permute-start | bytes 626696 | tf_op jit(solution)/shard_map/ppermute | solution.py:422
  16.2 4.1 %collective-permute-start.4 = (f32[8,128]{1,0:T(8,128)S(1)}, f32[8,128]{1,0:T(8,128)S(1)}, u32[]{:S(2)}, u32[]{:S(2)}) collective-permute-start(f32[8,128]{1,0:T(8,128)S(1)} %collective-permute-done.1), channel_id=1, source_target_pairs={{0,7},{1,6},{2,5},{3,4},{4,3},{5,2},{6,1},{7,0},{8,15},{9,14},{10,... | collective-permute-start | bytes 12296 | tf_op jit(solution)/shard_map/ppermute | solution.py:422
  20.4 2.9 %collective-permute-start.5 = (f32[1232,128]{1,0:T(8,128)S(1)}, f32[1232,128]{1,0:T(8,128)S(1)}, u32[]{:S(2)}, u32[]{:S(2)}) collective-permute-start(f32[1232,128]{1,0:T(8,128)S(1)} %constant_dynamic-update-slice_fusion.2.refs_1_), channel_id=1, source_target_pairs={{0,1},{1,0},{2,3},{3,2},{4,5},{5,4},{6,7},{7,6},{8,9},{9,8},{10,11... | collective-permute-start | bytes 1892360 | tf_op jit(solution)/shard_map/ppermute | solution.py:422
  20.5 5.8 %collective-permute-start.6 = (f32[408,128]{1,0:T(8,128)S(1)}, f32[408,128]{1,0:T(8,128)S(1)}, u32[]{:S(2)}, u32[]{:S(2)}) collective-permute-start(f32[408,128]{1,0:T(8,128)S(1)} %collective-permute-done.3), channel_id=1, source_target_pairs={{0,2},{1,5},{2,0},{3,7},{4,6},{5,1},{6,4},{7,3},{8,10},{9,13},{10,... | collective-permute-start | bytes 626696 | tf_op jit(solution)/shard_map/ppermute | solution.py:422
  23.2 4.5 %copy-start = (f32[2,5,5120]{2,0,1:T(2,128)S(1)}, f32[2,5,5120]{2,0,1:T(2,128)}, u32[]{:S(2)}) copy-start(f32[2,5,5120]{2,0,1:T(2,128)} %param.8) | copy-start | bytes 614404
  23.2 4.5 %copy-start.1 = (s32[5120]{0:T(1024)S(1)}, s32[5120]{0:T(1024)}, u32[]{:S(2)}) copy-start(s32[5120]{0:T(1024)} %param.9) | copy-start | bytes 61444
  26.3 1.5 %collective-permute-start.7 = (f32[408,128]{1,0:T(8,128)S(1)}, f32[408,128]{1,0:T(8,128)S(1)}, u32[]{:S(2)}, u32[]{:S(2)}) collective-permute-start(f32[408,128]{1,0:T(8,128)S(1)} %collective-permute-done.6.refs_2_), channel_id=1, source_target_pairs={{0,1},{1,0},{2,3},{3,2},{4,5},{5,4},{6,7},{7,6},{8,9},{9,8},{10,11... | collective-permute-start | bytes 626696 | tf_op jit(solution)/shard_map/ppermute | solution.py:422

commit v9 on v8

--- a/solution.py
+++ b/solution.py
@@ -27,7 +27,7 @@
             chip, other = (s ^ p ^ land) // 2, (s ^ p) % 2
             if s % 2 and chip in (1, 2):
                 chip = 3 - chip
-            where[p, n] = (2 + other) * 16 if chip == 3 else other * 16 + chip
+            where[p, n] = (3 - other) * 16 if chip == 3 else other * 16 + chip
         return passes, True, land, where
     wanted = set()
     for p, n, s in offsets:
@@ -301,7 +301,7 @@
     lines = dims[-1] - dims[0] * dims[1] * dims[2]
     low = power(dims[2] * dims[3] + 1)
     find_starts(dims, x_ref, tiles, 0, starts)
-    for g, code in enumerate((x_ref[pl.ds(tiles * dims[-1], lines), :], table_ref[...])):
+    for g, code in enumerate((table_ref[...], x_ref[pl.ds(tiles * dims[-1], lines), :])):
         row = jnp.where(code >= 0.0, (code * steps).astype(jnp.int32), -1)
         starts[pl.ds((tiles + g) * lines, lines), :] = row
     copy = pltpu.make_async_copy(starts, base_ref, sem)
@@ -448,7 +448,7 @@
     others = [passed(across, within(pairs)) for pairs in passes]
     held = 1 + len(passes)
     if relayed:
-        relay = passed(others[1], within(passes[0]))
+        relay = passed(others[1], within([(s, t ^ 1) for s, t in passes[0]]))
         table = passed(table, within([(p, p ^ 7) for p in range(half)]))
     near = jnp.concatenate([across] + others + [table] * relayed)
     sibling = passed(near, siblings)

time: 29.2 us -> 28.7 us (0.983)
  waiting for transfers between devices: 7.04 us -> 6.15 us
  starting transfers between devices: 10.6 us -> 11 us
    ppermute x8, waiting for transfers between devices: 7.04 us -> 6.15 us  [passed(): return lax.ppermute(array, 'comp', pairs)]
    ppermute x8, starting transfers between devices: 10.6 us -> 11 us  [passed(): return lax.ppermute(array, 'comp', pairs)]
  transfers between devices with their start and end apart: 8 -> 8, of which waited for: 5 -> 5; matrix products, arithmetic and copies ran while one was open for 0% -> 0% of each run, Pallas kernels for 34% -> 35%
where the time goes in v9:
time: 28.7 us; the launch traced here: 28.5 us
  Pallas kernels  11.2 us (39%)
  starting transfers between devices  11 us (38%)
  waiting for transfers between devices  6.15 us (21%)
    ppermute x8, starting transfers between devices, passed(): return lax.ppermute(array, 'comp', pairs)  11 us
    ppermute x8, waiting for transfers between devices, passed(): return lax.ppermute(array, 'comp', pairs)  6.15 us
    pallas_call x4, Pallas kernels, remap(): pl.pallas_call(body, out_shape=out, in_specs=[spec for _, spec in args],...  5.06 us
    pallas_call x1, Pallas kernels, prepare(): pl.pallas_call(lambda *refs: prepare_kernel(dims, chunks, *refs), out_sha...  4.74 us
    pallas_call x1, Pallas kernels, encode(): pl.pallas_call(encode_kernel, out_shape=jax.ShapeDtypeStruct((neigh + -ne...  1.4 us
  transfers between devices with their start and end apart: 8, of which 5 were waited for; matrix products, arithmetic and copies ran while one was open for 0% of the time, Pallas kernels for 35%

profile of v9, /device:TPU:0, one launch (start us, length us, event | category | flops | bytes accessed | tf_op | source)
XLA Modules:
  0.0 28.5 jit_solution(1118487778874039127)
XLA Ops:
  0.0 5.0 %collective-permute-start = (f32[400,128]{1,0:T(8,128)}, f32[400,128]{1,0:T(8,128)S(1)}, u32[]{:S(2)}, u32[]{:S(2)}) collective-permute-start(f32[400,128]{1,0:T(8,128)} %bitcast.14), channel_id=1, source_target_pairs={{0,12},{1,13},{2,14},{3,15},{4,8},{5,9},{6,10},{7,11},{8,4},{9,5},... | collective-permute-start | bytes 614408 | tf_op jit(solution)/shard_map/ppermute | solution.py:422
  5.0 1.4 %encode.1 = f32[8,128]{1,0:T(8,128)} custom-call(s32[8,32]{1,0:T(8,128)} %bitcast.18, s32[1,8]{1,0:T(1,128)} %count_ref.1), custom_call_target="tpu_custom_call" | custom-call | flops 4096 | bytes 8192 | tf_op jit(solution)/shard_map/encode/pallas_call | solution.py:72
  6.4 0.0 collective-permute-start.1
  6.5 4.7 %prepare.1 = (bf16[161,128,256]{2,1,0:T(8,128)(2,1)S(1)}, s32[5,256]{1,0:T(8,128)S(4)}) custom-call(s32[4,40]{1,0:T(4,128)} %bitcast.19, s32[40]{0:T(128)} %refs_1_.1, s32[16,9]{1,0:T(8,128)} %constant.2.clone.refs_2_, f32[160,128,128]{2,1,0:T(8,128)} %bitcast.17), custom_call_target="tpu_custom_call" | custom-call | flops 10485760 | bytes 20971520 | tf_op jit(solution)/shard_map/prepare/pallas_call | solution.py:173
  11.2 1.0 %collective-permute-done.1 = f32[8,128]{1,0:T(8,128)S(1)} collective-permute-done((f32[8,128]{1,0:T(8,128)}, f32[8,128]{1,0:T(8,128)S(1)}, u32[]{:S(2)}, u32[]{:S(2)}) %collective-permute-start.1) | collective-permute-done | bytes 4128 | tf_op jit(solution)/shard_map/ppermute | solution.py:422
  12.2 0.0 collective-permute-done
  12.2 1.6 %collective-permute-start.2 = (f32[408,128]{1,0:T(8,128)S(1)}, f32[408,128]{1,0:T(8,128)S(1)}, u32[]{:S(2)}, u32[]{:S(2)}) collective-permute-start(f32[408,128]{1,0:T(8,128)S(1)} %get-tuple-element.25), channel_id=1, source_target_pairs={{0,2},{1,5},{2,0},{3,7},{4,6},{5,1},{6,4},{7,3},{8,10},{9,13},{10,... | collective-permute-start | bytes 626696 | tf_op jit(solution)/shard_map/ppermute | solution.py:422
  13.8 2.5 %collective-permute-start.3 = (f32[408,128]{1,0:T(8,128)S(1)}, f32[408,128]{1,0:T(8,128)S(1)}, u32[]{:S(2)}, u32[]{:S(2)}) collective-permute-start(f32[408,128]{1,0:T(8,128)S(1)} %get-tuple-element.25), channel_id=1, source_target_pairs={{0,4},{1,3},{2,6},{3,1},{4,0},{5,7},{6,2},{7,5},{8,12},{9,11},{10,... | collective-permute-start | bytes 626696 | tf_op jit(solution)/shard_map/ppermute | solution.py:422
  16.2 0.0 collective-permute-start.4
  16.3 3.8 %collective-permute-done.2 = f32[408,128]{1,0:T(8,128)S(1)} collective-permute-done((f32[408,128]{1,0:T(8,128)S(1)}, f32[408,128]{1,0:T(8,128)S(1)}, u32[]{:S(2)}, u32[]{:S(2)}) %collective-permute-start.2) | collective-permute-done | bytes 208928 | tf_op jit(solution)/shard_map/ppermute | solution.py:422
  20.1 0.0 collective-permute-done.3
  20.1 0.2 collective-permute-done.4.refs_2_
  20.4 0.1 collective-permute-start.5
  20.5 1.4 %collective-permute-start.6 = (f32[408,128]{1,0:T(8,128)S(1)}, f32[408,128]{1,0:T(8,128)S(1)}, u32[]{:S(2)}, u32[]{:S(2)}) collective-permute-start(f32[408,128]{1,0:T(8,128)S(1)} %collective-permute-done.3), channel_id=1, source_target_pairs={{0,3},{1,4},{2,1},{3,6},{4,7},{5,0},{6,5},{7,2},{8,11},{9,12},{10,... | collective-permute-start | bytes 626696 | tf_op jit(solution)/shard_map/ppermute | solution.py:422
  21.9 1.4 %remap_0.1.refs_4_ = f32[648,128]{1,0:T(8,128)S(1)} custom-call(s32[5,256]{1,0:T(8,128)S(4)} %get-tuple-element.15.refs_0_, f32[1232,128]{1,0:T(8,128)S(1)} %constant_dynamic-update-slice_fusion.2.refs_1_, bf16[161,128,256]{2,1,0:T(8,128)(2,1)S(1)} %get-tuple-element.18.refs_2_.refs_3_), custom_call_target="tpu_custom_call" | custom-call | flops 83886080 | bytes 5275648 | tf_op jit(solution)/shard_map/remap_0/pallas_call | solution.py:395
  23.3 0.0 copy-start
  23.3 0.0 copy-start.1
  23.3 0.0 collective-permute-done.5.refs_1_
  23.3 2.0 %remap_1.1 = (f32[648,128]{1,0:T(8,128)S(1)}, s32[2,256]{1,0:T(2,128)S(4)}) custom-call(s32[5,256]{1,0:T(8,128)S(4)} %get-tuple-element.15.refs_0_, f32[1232,128]{1,0:T(8,128)S(1)} %collective-permute-done.5.refs_1_, f32[8,128]{1,0:T(8,128)S(1)} %collective-permute-done.4.refs_2_, bf16[161,128,256]{2,1,0:T(8,128)(2,1)S(1)} %get-tuple-element.18.refs_2_.refs_3_, ...), custom_call_target="tpu_custom_call" | custom-call | flops 83886080 | bytes 5275648 | tf_op jit(solution)/shard_map/remap_1/pallas_call | solution.py:395
  25.3 0.5 %collective-permute-done.6.refs_2_ = f32[408,128]{1,0:T(8,128)S(1)} collective-permute-done((f32[408,128]{1,0:T(8,128)S(1)}, f32[408,128]{1,0:T(8,128)S(1)}, u32[]{:S(2)}, u32[]{:S(2)}) %collective-permute-start.6) | collective-permute-done | bytes 208928 | tf_op jit(solution)/shard_map/ppermute | solution.py:422
  25.8 0.3 %collective-permute-start.7 = (f32[408,128]{1,0:T(8,128)S(1)}, f32[408,128]{1,0:T(8,128)S(1)}, u32[]{:S(2)}, u32[]{:S(2)}) collective-permute-start(f32[408,128]{1,0:T(8,128)S(1)} %collective-permute-done.6.refs_2_), channel_id=1, source_target_pairs={{0,1},{1,0},{2,3},{3,2},{4,5},{5,4},{6,7},{7,6},{8,9},{9,8},{10,11... | collective-permute-start | bytes 626696 | tf_op jit(solution)/shard_map/ppermute | solution.py:422
  26.1 0.5 %remap_2.1.refs_4_ = f32[648,128]{1,0:T(8,128)S(1)} custom-call(s32[5,256]{1,0:T(8,128)S(4)} %get-tuple-element.15.refs_0_, s32[2,256]{1,0:T(2,128)S(4)} %get-tuple-element.19.refs_1_, f32[408,128]{1,0:T(8,128)S(1)} %collective-permute-done.6.refs_2_, bf16[161,128,256]{2,1,0:T(8,128)(2,1)S(1)} %get-tuple-element.18.refs_2_.refs_3_, ...), custom_call_target="tpu_custom_call" | custom-call | flops 83886080 | bytes 5275648 | tf_op jit(solution)/shard_map/remap_2/pallas_call | solution.py:395
  26.6 0.6 %collective-permute-done.7.refs_2_ = f32[408,128]{1,0:T(8,128)S(1)} collective-permute-done((f32[408,128]{1,0:T(8,128)S(1)}, f32[408,128]{1,0:T(8,128)S(1)}, u32[]{:S(2)}, u32[]{:S(2)}) %collective-permute-start.7) | collective-permute-done | bytes 208928 | tf_op jit(solution)/shard_map/ppermute | solution.py:422
  27.2 0.0 copy-done
  27.2 0.0 copy-done.1
  27.2 1.3 %remap_last.1 = f32[320,128]{1,0:T(8,128)} custom-call(s32[5,256]{1,0:T(8,128)S(4)} %get-tuple-element.15.refs_0_, s32[2,256]{1,0:T(2,128)S(4)} %get-tuple-element.19.refs_1_, f32[408,128]{1,0:T(8,128)S(1)} %collective-permute-done.7.refs_2_, bf16[161,128,256]{2,1,0:T(8,128)(2,1)S(1)} %get-tuple-element.18.refs_2_.refs_3_, f32[648,128]{1,0:T(8,128)S(1)} %remap_2.1.refs_4_, ...), custom_call_target="tpu_custom_call" | custom-call | flops 83886080 | bytes 5275648 | tf_op jit(solution)/shard_map/remap_last/pallas_call | solution.py:395
  (5 shorter events, 0.1 us)
Async XLA Ops:
  0.0 12.2 %collective-permute-start = (f32[400,128]{1,0:T(8,128)}, f32[400,128]{1,0:T(8,128)S(1)}, u32[]{:S(2)}, u32[]{:S(2)}) collective-permute-start(f32[400,128]{1,0:T(8,128)} %bitcast.14), channel_id=1, source_target_pairs={{0,12},{1,13},{2,14},{3,15},{4,8},{5,9},{6,10},{7,11},{8,4},{9,5},... | collective-permute-start | bytes 614408 | tf_op jit(solution)/shard_map/ppermute | solution.py:422
  6.4 5.7 %collective-permute-start.1 = (f32[8,128]{1,0:T(8,128)}, f32[8,128]{1,0:T(8,128)S(1)}, u32[]{:S(2)}, u32[]{:S(2)}) collective-permute-start(f32[8,128]{1,0:T(8,128)} %encode.1), channel_id=1, source_target_pairs={{0,12},{1,13},{2,14},{3,15},{4,8},{5,9},{6,10},{7,11},{8,4},{9,5},... | collective-permute-start | bytes 12296 | tf_op jit(solution)/shard_map/ppermute | solution.py:422
  12.2 7.8 %collective-permute-start.2 = (f32[408,128]{1,0:T(8,128)S(1)}, f32[408,128]{1,0:T(8,128)S(1)}, u32[]{:S(2)}, u32[]{:S(2)}) collective-permute-start(f32[408,128]{1,0:T(8,128)S(1)} %get-tuple-element.25), channel_id=1, source_target_pairs={{0,2},{1,5},{2,0},{3,7},{4,6},{5,1},{6,4},{7,3},{8,10},{9,13},{10,... | collective-permute-start | bytes 626696 | tf_op jit(solution)/shard_map/ppermute | solution.py:422
  13.8 6.3 %collective-permute-start.3 = (f32[408,128]{1,0:T(8,128)S(1)}, f32[408,128]{1,0:T(8,128)S(1)}, u32[]{:S(2)}, u32[]{:S(2)}) collective-permute-start(f32[408,128]{1,0:T(8,128)S(1)} %get-tuple-element.25), channel_id=1, source_target_pairs={{0,4},{1,3},{2,6},{3,1},{4,0},{5,7},{6,2},{7,5},{8,12},{9,11},{10,... | collective-permute-start | bytes 626696 | tf_op jit(solution)/shard_map/ppermute | solution.py:422
  16.2 4.1 %collective-permute-start.4 = (f32[8,128]{1,0:T(8,128)S(1)}, f32[8,128]{1,0:T(8,128)S(1)}, u32[]{:S(2)}, u32[]{:S(2)}) collective-permute-start(f32[8,128]{1,0:T(8,128)S(1)} %collective-permute-done.1), channel_id=1, source_target_pairs={{0,7},{1,6},{2,5},{3,4},{4,3},{5,2},{6,1},{7,0},{8,15},{9,14},{10,... | collective-permute-start | bytes 12296 | tf_op jit(solution)/shard_map/ppermute | solution.py:422
  20.4 2.9 %collective-permute-start.5 = (f32[1232,128]{1,0:T(8,128)S(1)}, f32[1232,128]{1,0:T(8,128)S(1)}, u32[]{:S(2)}, u32[]{:S(2)}) collective-permute-start(f32[1232,128]{1,0:T(8,128)S(1)} %constant_dynamic-update-slice_fusion.2.refs_1_), channel_id=1, source_target_pairs={{0,1},{1,0},{2,3},{3,2},{4,5},{5,4},{6,7},{7,6},{8,9},{9,8},{10,11... | collective-permute-start | bytes 1892360 | tf_op jit(solution)/shard_map/ppermute | solution.py:422
  20.5 5.3 %collective-permute-start.6 = (f32[408,128]{1,0:T(8,128)S(1)}, f32[408,128]{1,0:T(8,128)S(1)}, u32[]{:S(2)}, u32[]{:S(2)}) collective-permute-start(f32[408,128]{1,0:T(8,128)S(1)} %collective-permute-done.3), channel_id=1, source_target_pairs={{0,3},{1,4},{2,1},{3,6},{4,7},{5,0},{6,5},{7,2},{8,11},{9,12},{10,... | collective-permute-start | bytes 626696 | tf_op jit(solution)/shard_map/ppermute | solution.py:422
  23.3 3.9 %copy-start = (f32[2,5,5120]{2,0,1:T(2,128)S(1)}, f32[2,5,5120]{2,0,1:T(2,128)}, u32[]{:S(2)}) copy-start(f32[2,5,5120]{2,0,1:T(2,128)} %param.8) | copy-start | bytes 614404
  23.3 3.9 %copy-start.1 = (s32[5120]{0:T(1024)S(1)}, s32[5120]{0:T(1024)}, u32[]{:S(2)}) copy-start(s32[5120]{0:T(1024)} %param.9) | copy-start | bytes 61444
  25.8 1.5 %collective-permute-start.7 = (f32[408,128]{1,0:T(8,128)S(1)}, f32[408,128]{1,0:T(8,128)S(1)}, u32[]{:S(2)}, u32[]{:S(2)}) collective-permute-start(f32[408,128]{1,0:T(8,128)S(1)} %collective-permute-done.6.refs_2_), channel_id=1, source_target_pairs={{0,1},{1,0},{2,3},{3,2},{4,5},{5,4},{6,7},{7,6},{8,9},{9,8},{10,11... | collective-permute-start | bytes 626696 | tf_op jit(solution)/shard_map/ppermute | solution.py:422

commit v10 on v9

--- a/solution.py
+++ b/solution.py
@@ -91,7 +91,7 @@
     return x & (n - 1) if n == power(n) else lax.rem(x, jnp.int32(n))
 
 
-UNROLL = 16
+UNROLL = 32
 LATE = 32
 
 

time: 28.7 us -> 28.7 us (level)
  waiting for transfers between devices: 6.15 us -> 5.7 us
  Pallas kernels: 11.2 us -> 11.6 us
    ppermute x8, waiting for transfers between devices: 6.15 us -> 5.7 us  [passed(): return lax.ppermute(array, 'comp', pairs)]
    pallas_call x4, Pallas kernels: 5.06 us -> 5.5 us  [remap(): pl.pallas_call(body, out_shape=out, in_specs=[spec for _, spec in args],...]
  transfers between devices with their start and end apart: 8 -> 8, of which waited for: 5 -> 5; matrix products, arithmetic and copies ran while one was open for 0% -> 0% of each run, Pallas kernels for 35% -> 36%
where the time goes in v10:
time: 28.7 us; the launch traced here: 28.5 us
  Pallas kernels  11.6 us (40%)
  starting transfers between devices  11 us (38%)
  waiting for transfers between devices  5.7 us (20%)
    ppermute x8, starting transfers between devices, passed(): return lax.ppermute(array, 'comp', pairs)  11 us
    ppermute x8, waiting for transfers between devices, passed(): return lax.ppermute(array, 'comp', pairs)  5.7 us
    pallas_call x4, Pallas kernels, remap(): pl.pallas_call(body, out_shape=out, in_specs=[spec for _, spec in args],...  5.5 us
    pallas_call x1, Pallas kernels, prepare(): pl.pallas_call(lambda *refs: prepare_kernel(dims, chunks, *refs), out_sha...  4.74 us
    pallas_call x1, Pallas kernels, encode(): pl.pallas_call(encode_kernel, out_shape=jax.ShapeDtypeStruct((neigh + -ne...  1.4 us
  transfers between devices with their start and end apart: 8, of which 5 were waited for; matrix products, arithmetic and copies ran while one was open for 0% of the time, Pallas kernels for 36%

profile of v10, /device:TPU:0, one launch (start us, length us, event | category | flops | bytes accessed | tf_op | source)
XLA Modules:
  0.0 28.5 jit_solution(17764134632891290773)
XLA Ops:
  0.0 5.0 %collective-permute-start = (f32[400,128]{1,0:T(8,128)}, f32[400,128]{1,0:T(8,128)S(1)}, u32[]{:S(2)}, u32[]{:S(2)}) collective-permute-start(f32[400,128]{1,0:T(8,128)} %bitcast.14), channel_id=1, source_target_pairs={{0,12},{1,13},{2,14},{3,15},{4,8},{5,9},{6,10},{7,11},{8,4},{9,5},... | collective-permute-start | bytes 614408 | tf_op jit(solution)/shard_map/ppermute | solution.py:422
  5.0 1.4 %encode.1 = f32[8,128]{1,0:T(8,128)} custom-call(s32[8,32]{1,0:T(8,128)} %bitcast.18, s32[1,8]{1,0:T(1,128)} %count_ref.1), custom_call_target="tpu_custom_call" | custom-call | flops 4096 | bytes 8192 | tf_op jit(solution)/shard_map/encode/pallas_call | solution.py:72
  6.4 0.0 collective-permute-start.1
  6.5 4.7 %prepare.1 = (bf16[161,128,256]{2,1,0:T(8,128)(2,1)S(1)}, s32[5,256]{1,0:T(8,128)S(4)}) custom-call(s32[4,40]{1,0:T(4,128)} %bitcast.19, s32[40]{0:T(128)} %refs_1_.1, s32[16,9]{1,0:T(8,128)} %constant.2.clone.refs_2_, f32[160,128,128]{2,1,0:T(8,128)} %bitcast.17), custom_call_target="tpu_custom_call" | custom-call | flops 10485760 | bytes 20971520 | tf_op jit(solution)/shard_map/prepare/pallas_call | solution.py:173
  11.2 1.0 %collective-permute-done.1 = f32[8,128]{1,0:T(8,128)S(1)} collective-permute-done((f32[8,128]{1,0:T(8,128)}, f32[8,128]{1,0:T(8,128)S(1)}, u32[]{:S(2)}, u32[]{:S(2)}) %collective-permute-start.1) | collective-permute-done | bytes 4128 | tf_op jit(solution)/shard_map/ppermute | solution.py:422
  12.2 0.0 collective-permute-done
  12.2 1.6 %collective-permute-start.2 = (f32[408,128]{1,0:T(8,128)S(1)}, f32[408,128]{1,0:T(8,128)S(1)}, u32[]{:S(2)}, u32[]{:S(2)}) collective-permute-start(f32[408,128]{1,0:T(8,128)S(1)} %get-tuple-element.25), channel_id=1, source_target_pairs={{0,2},{1,5},{2,0},{3,7},{4,6},{5,1},{6,4},{7,3},{8,10},{9,13},{10,... | collective-permute-start | bytes 626696 | tf_op jit(solution)/shard_map/ppermute | solution.py:422
  13.8 2.5 %collective-permute-start.3 = (f32[408,128]{1,0:T(8,128)S(1)}, f32[408,128]{1,0:T(8,128)S(1)}, u32[]{:S(2)}, u32[]{:S(2)}) collective-permute-start(f32[408,128]{1,0:T(8,128)S(1)} %get-tuple-element.25), channel_id=1, source_target_pairs={{0,4},{1,3},{2,6},{3,1},{4,0},{5,7},{6,2},{7,5},{8,12},{9,11},{10,... | collective-permute-start | bytes 626696 | tf_op jit(solution)/shard_map/ppermute | solution.py:422
  16.2 0.0 collective-permute-start.4
  16.3 3.8 %collective-permute-done.2 = f32[408,128]{1,0:T(8,128)S(1)} collective-permute-done((f32[408,128]{1,0:T(8,128)S(1)}, f32[408,128]{1,0:T(8,128)S(1)}, u32[]{:S(2)}, u32[]{:S(2)}) %collective-permute-start.2) | collective-permute-done | bytes 208928 | tf_op jit(solution)/shard_map/ppermute | solution.py:422
  20.1 0.0 collective-permute-done.3
  20.1 0.2 collective-permute-done.4.refs_2_
  20.4 0.1 collective-permute-start.5
  20.5 1.4 %collective-permute-start.6 = (f32[408,128]{1,0:T(8,128)S(1)}, f32[408,128]{1,0:T(8,128)S(1)}, u32[]{:S(2)}, u32[]{:S(2)}) collective-permute-start(f32[408,128]{1,0:T(8,128)S(1)} %collective-permute-done.3), channel_id=1, source_target_pairs={{0,3},{1,4},{2,1},{3,6},{4,7},{5,0},{6,5},{7,2},{8,11},{9,12},{10,... | collective-permute-start | bytes 626696 | tf_op jit(solution)/shard_map/ppermute | solution.py:422
  21.9 1.2 %remap_0.1.refs_4_ = f32[648,128]{1,0:T(8,128)S(1)} custom-call(s32[5,256]{1,0:T(8,128)S(4)} %get-tuple-element.15.refs_0_, f32[1232,128]{1,0:T(8,128)S(1)} %constant_dynamic-update-slice_fusion.2.refs_1_, bf16[161,128,256]{2,1,0:T(8,128)(2,1)S(1)} %get-tuple-element.18.refs_2_.refs_3_), custom_call_target="tpu_custom_call" | custom-call | flops 83886080 | bytes 5275648 | tf_op jit(solution)/shard_map/remap_0/pallas_call | solution.py:395
  23.1 0.0 copy-start
  23.1 0.0 copy-start.1
  23.2 0.0 collective-permute-done.5.refs_1_
  23.2 2.1 %remap_1.1 = (f32[648,128]{1,0:T(8,128)S(1)}, s32[2,256]{1,0:T(2,128)S(4)}) custom-call(s32[5,256]{1,0:T(8,128)S(4)} %get-tuple-element.15.refs_0_, f32[1232,128]{1,0:T(8,128)S(1)} %collective-permute-done.5.refs_1_, f32[8,128]{1,0:T(8,128)S(1)} %collective-permute-done.4.refs_2_, bf16[161,128,256]{2,1,0:T(8,128)(2,1)S(1)} %get-tuple-element.18.refs_2_.refs_3_, ...), custom_call_target="tpu_custom_call" | custom-call | flops 83886080 | bytes 5275648 | tf_op jit(solution)/shard_map/remap_1/pallas_call | solution.py:395
  25.3 0.5 %collective-permute-done.6.refs_2_ = f32[408,128]{1,0:T(8,128)S(1)} collective-permute-done((f32[408,128]{1,0:T(8,128)S(1)}, f32[408,128]{1,0:T(8,128)S(1)}, u32[]{:S(2)}, u32[]{:S(2)}) %collective-permute-start.6) | collective-permute-done | bytes 208928 | tf_op jit(solution)/shard_map/ppermute | solution.py:422
  25.8 0.3 %collective-permute-start.7 = (f32[408,128]{1,0:T(8,128)S(1)}, f32[408,128]{1,0:T(8,128)S(1)}, u32[]{:S(2)}, u32[]{:S(2)}) collective-permute-start(f32[408,128]{1,0:T(8,128)S(1)} %collective-permute-done.6.refs_2_), channel_id=1, source_target_pairs={{0,1},{1,0},{2,3},{3,2},{4,5},{5,4},{6,7},{7,6},{8,9},{9,8},{10,11... | collective-permute-start | bytes 626696 | tf_op jit(solution)/shard_map/ppermute | solution.py:422
  26.1 0.9 %remap_2.1.refs_4_ = f32[648,128]{1,0:T(8,128)S(1)} custom-call(s32[5,256]{1,0:T(8,128)S(4)} %get-tuple-element.15.refs_0_, s32[2,256]{1,0:T(2,128)S(4)} %get-tuple-element.19.refs_1_, f32[408,128]{1,0:T(8,128)S(1)} %collective-permute-done.6.refs_2_, bf16[161,128,256]{2,1,0:T(8,128)(2,1)S(1)} %get-tuple-element.18.refs_2_.refs_3_, ...), custom_call_target="tpu_custom_call" | custom-call | flops 83886080 | bytes 5275648 | tf_op jit(solution)/shard_map/remap_2/pallas_call | solution.py:395
  27.0 0.2 collective-permute-done.7.refs_2_
  27.2 0.0 copy-done
  27.2 0.0 copy-done.1
  27.2 1.2 %remap_last.1 = f32[320,128]{1,0:T(8,128)} custom-call(s32[5,256]{1,0:T(8,128)S(4)} %get-tuple-element.15.refs_0_, s32[2,256]{1,0:T(2,128)S(4)} %get-tuple-element.19.refs_1_, f32[408,128]{1,0:T(8,128)S(1)} %collective-permute-done.7.refs_2_, bf16[161,128,256]{2,1,0:T(8,128)(2,1)S(1)} %get-tuple-element.18.refs_2_.refs_3_, f32[648,128]{1,0:T(8,128)S(1)} %remap_2.1.refs_4_, ...), custom_call_target="tpu_custom_call" | custom-call | flops 83886080 | bytes 5275648 | tf_op jit(solution)/shard_map/remap_last/pallas_call | solution.py:395
  (5 shorter events, 0.1 us)
Async XLA Ops:
  0.0 12.2 %collective-permute-start = (f32[400,128]{1,0:T(8,128)}, f32[400,128]{1,0:T(8,128)S(1)}, u32[]{:S(2)}, u32[]{:S(2)}) collective-permute-start(f32[400,128]{1,0:T(8,128)} %bitcast.14), channel_id=1, source_target_pairs={{0,12},{1,13},{2,14},{3,15},{4,8},{5,9},{6,10},{7,11},{8,4},{9,5},... | collective-permute-start | bytes 614408 | tf_op jit(solution)/shard_map/ppermute | solution.py:422
  6.4 5.7 %collective-permute-start.1 = (f32[8,128]{1,0:T(8,128)}, f32[8,128]{1,0:T(8,128)S(1)}, u32[]{:S(2)}, u32[]{:S(2)}) collective-permute-start(f32[8,128]{1,0:T(8,128)} %encode.1), channel_id=1, source_target_pairs={{0,12},{1,13},{2,14},{3,15},{4,8},{5,9},{6,10},{7,11},{8,4},{9,5},... | collective-permute-start | bytes 12296 | tf_op jit(solution)/shard_map/ppermute | solution.py:422
  12.2 7.8 %collective-permute-start.2 = (f32[408,128]{1,0:T(8,128)S(1)}, f32[408,128]{1,0:T(8,128)S(1)}, u32[]{:S(2)}, u32[]{:S(2)}) collective-permute-start(f32[408,128]{1,0:T(8,128)S(1)} %get-tuple-element.25), channel_id=1, source_target_pairs={{0,2},{1,5},{2,0},{3,7},{4,6},{5,1},{6,4},{7,3},{8,10},{9,13},{10,... | collective-permute-start | bytes 626696 | tf_op jit(solution)/shard_map/ppermute | solution.py:422
  13.8 6.3 %collective-permute-start.3 = (f32[408,128]{1,0:T(8,128)S(1)}, f32[408,128]{1,0:T(8,128)S(1)}, u32[]{:S(2)}, u32[]{:S(2)}) collective-permute-start(f32[408,128]{1,0:T(8,128)S(1)} %get-tuple-element.25), channel_id=1, source_target_pairs={{0,4},{1,3},{2,6},{3,1},{4,0},{5,7},{6,2},{7,5},{8,12},{9,11},{10,... | collective-permute-start | bytes 626696 | tf_op jit(solution)/shard_map/ppermute | solution.py:422
  16.2 4.1 %collective-permute-start.4 = (f32[8,128]{1,0:T(8,128)S(1)}, f32[8,128]{1,0:T(8,128)S(1)}, u32[]{:S(2)}, u32[]{:S(2)}) collective-permute-start(f32[8,128]{1,0:T(8,128)S(1)} %collective-permute-done.1), channel_id=1, source_target_pairs={{0,7},{1,6},{2,5},{3,4},{4,3},{5,2},{6,1},{7,0},{8,15},{9,14},{10,... | collective-permute-start | bytes 12296 | tf_op jit(solution)/shard_map/ppermute | solution.py:422
  20.4 2.8 %collective-permute-start.5 = (f32[1232,128]{1,0:T(8,128)S(1)}, f32[1232,128]{1,0:T(8,128)S(1)}, u32[]{:S(2)}, u32[]{:S(2)}) collective-permute-start(f32[1232,128]{1,0:T(8,128)S(1)} %constant_dynamic-update-slice_fusion.2.refs_1_), channel_id=1, source_target_pairs={{0,1},{1,0},{2,3},{3,2},{4,5},{5,4},{6,7},{7,6},{8,9},{9,8},{10,11... | collective-permute-start | bytes 1892360 | tf_op jit(solution)/shard_map/ppermute | solution.py:422
  20.5 5.3 %collective-permute-start.6 = (f32[408,128]{1,0:T(8,128)S(1)}, f32[408,128]{1,0:T(8,128)S(1)}, u32[]{:S(2)}, u32[]{:S(2)}) collective-permute-start(f32[408,128]{1,0:T(8,128)S(1)} %collective-permute-done.3), channel_id=1, source_target_pairs={{0,3},{1,4},{2,1},{3,6},{4,7},{5,0},{6,5},{7,2},{8,11},{9,12},{10,... | collective-permute-start | bytes 626696 | tf_op jit(solution)/shard_map/ppermute | solution.py:422
  23.1 4.1 %copy-start = (f32[2,5,5120]{2,0,1:T(2,128)S(1)}, f32[2,5,5120]{2,0,1:T(2,128)}, u32[]{:S(2)}) copy-start(f32[2,5,5120]{2,0,1:T(2,128)} %param.8) | copy-start | bytes 614404
  23.1 4.1 %copy-start.1 = (s32[5120]{0:T(1024)S(1)}, s32[5120]{0:T(1024)}, u32[]{:S(2)}) copy-start(s32[5120]{0:T(1024)} %param.9) | copy-start | bytes 61444
  25.8 1.5 %collective-permute-start.7 = (f32[408,128]{1,0:T(8,128)S(1)}, f32[408,128]{1,0:T(8,128)S(1)}, u32[]{:S(2)}, u32[]{:S(2)}) collective-permute-start(f32[408,128]{1,0:T(8,128)S(1)} %collective-permute-done.6.refs_2_), channel_id=1, source_target_pairs={{0,1},{1,0},{2,3},{3,2},{4,5},{5,4},{6,7},{7,6},{8,9},{9,8},{10,11... | collective-permute-start | bytes 626696 | tf_op jit(solution)/shard_map/ppermute | solution.py:422

commit v11 on v10

--- a/solution.py
+++ b/solution.py
@@ -448,7 +448,7 @@
     others = [passed(across, within(pairs)) for pairs in passes]
     held = 1 + len(passes)
     if relayed:
-        relay = passed(others[1], within([(s, t ^ 1) for s, t in passes[0]]))
+        relay = passed(others[0], within([(s, t ^ 1) for s, t in passes[1]]))
         table = passed(table, within([(p, p ^ 7) for p in range(half)]))
     near = jnp.concatenate([across] + others + [table] * relayed)
     sibling = passed(near, siblings)

time: 28.7 us -> 28.8 us (level)
  Pallas kernels: 11.6 us -> 10.9 us
  starting transfers between devices: 11 us -> 11.4 us
    pallas_call x4, Pallas kernels: 5.5 us -> 4.79 us  [remap(): pl.pallas_call(body, out_shape=out, in_specs=[spec for _, spec in args],...]
    ppermute x8, starting transfers between devices: 11 us -> 11.4 us  [passed(): return lax.ppermute(array, 'comp', pairs)]
  transfers between devices with their start and end apart: 8 -> 8, of which waited for: 5 -> 5; matrix products, arithmetic and copies ran while one was open for 0% -> 0% of each run, Pallas kernels for 36% -> 34%
where the time goes in v11:
time: 28.8 us; the launch traced here: 28.4 us
  starting transfers between devices  11.4 us (40%)
  Pallas kernels  10.9 us (38%)
  waiting for transfers between devices  5.94 us (21%)
    ppermute x8, starting transfers between devices, passed(): return lax.ppermute(array, 'comp', pairs)  11.4 us
    ppermute x8, waiting for transfers between devices, passed(): return lax.ppermute(array, 'comp', pairs)  5.94 us
    pallas_call x4, Pallas kernels, remap(): pl.pallas_call(body, out_shape=out, in_specs=[spec for _, spec in args],...  4.79 us
    pallas_call x1, Pallas kernels, prepare(): pl.pallas_call(lambda *refs: prepare_kernel(dims, chunks, *refs), out_sha...  4.74 us
    pallas_call x1, Pallas kernels, encode(): pl.pallas_call(encode_kernel, out_shape=jax.ShapeDtypeStruct((neigh + -ne...  1.4 us
  transfers between devices with their start and end apart: 8, of which 5 were waited for; matrix products, arithmetic and copies ran while one was open for 0% of the time, Pallas kernels for 34%

profile of v11, /device:TPU:0, one launch (start us, length us, event | category | flops | bytes accessed | tf_op | source)
XLA Modules:
  0.0 28.4 jit_solution(8374533654362552012)
XLA Ops:
  0.0 5.0 %collective-permute-start = (f32[400,128]{1,0:T(8,128)}, f32[400,128]{1,0:T(8,128)S(1)}, u32[]{:S(2)}, u32[]{:S(2)}) collective-permute-start(f32[400,128]{1,0:T(8,128)} %bitcast.14), channel_id=1, source_target_pairs={{0,12},{1,13},{2,14},{3,15},{4,8},{5,9},{6,10},{7,11},{8,4},{9,5},... | collective-permute-start | bytes 614408 | tf_op jit(solution)/shard_map/ppermute | solution.py:422
  5.0 1.4 %encode.1 = f32[8,128]{1,0:T(8,128)} custom-call(s32[8,32]{1,0:T(8,128)} %bitcast.18, s32[1,8]{1,0:T(1,128)} %count_ref.1), custom_call_target="tpu_custom_call" | custom-call | flops 4096 | bytes 8192 | tf_op jit(solution)/shard_map/encode/pallas_call | solution.py:72
  6.4 0.0 collective-permute-start.1
  6.5 4.7 %prepare.1 = (bf16[161,128,256]{2,1,0:T(8,128)(2,1)S(1)}, s32[5,256]{1,0:T(8,128)S(4)}) custom-call(s32[4,40]{1,0:T(4,128)} %bitcast.19, s32[40]{0:T(128)} %refs_1_.1, s32[16,9]{1,0:T(8,128)} %constant.2.clone.refs_2_, f32[160,128,128]{2,1,0:T(8,128)} %bitcast.17), custom_call_target="tpu_custom_call" | custom-call | flops 10485760 | bytes 20971520 | tf_op jit(solution)/shard_map/prepare/pallas_call | solution.py:173
  11.2 1.0 %collective-permute-done.1 = f32[8,128]{1,0:T(8,128)S(1)} collective-permute-done((f32[8,128]{1,0:T(8,128)}, f32[8,128]{1,0:T(8,128)S(1)}, u32[]{:S(2)}, u32[]{:S(2)}) %collective-permute-start.1) | collective-permute-done | bytes 4128 | tf_op jit(solution)/shard_map/ppermute | solution.py:422
  12.2 0.0 collective-permute-done
  12.2 1.6 %collective-permute-start.2 = (f32[408,128]{1,0:T(8,128)S(1)}, f32[408,128]{1,0:T(8,128)S(1)}, u32[]{:S(2)}, u32[]{:S(2)}) collective-permute-start(f32[408,128]{1,0:T(8,128)S(1)} %get-tuple-element.25), channel_id=1, source_target_pairs={{0,2},{1,5},{2,0},{3,7},{4,6},{5,1},{6,4},{7,3},{8,10},{9,13},{10,... | collective-permute-start | bytes 626696 | tf_op jit(solution)/shard_map/ppermute | solution.py:422
  13.8 2.5 %collective-permute-start.3 = (f32[408,128]{1,0:T(8,128)S(1)}, f32[408,128]{1,0:T(8,128)S(1)}, u32[]{:S(2)}, u32[]{:S(2)}) collective-permute-start(f32[408,128]{1,0:T(8,128)S(1)} %get-tuple-element.25), channel_id=1, source_target_pairs={{0,4},{1,3},{2,6},{3,1},{4,0},{5,7},{6,2},{7,5},{8,12},{9,11},{10,... | collective-permute-start | bytes 626696 | tf_op jit(solution)/shard_map/ppermute | solution.py:422
  16.2 0.0 collective-permute-start.4
  16.3 3.8 %collective-permute-done.2 = f32[408,128]{1,0:T(8,128)S(1)} collective-permute-done((f32[408,128]{1,0:T(8,128)S(1)}, f32[408,128]{1,0:T(8,128)S(1)}, u32[]{:S(2)}, u32[]{:S(2)}) %collective-permute-start.2) | collective-permute-done | bytes 208928 | tf_op jit(solution)/shard_map/ppermute | solution.py:422
  20.1 0.0 collective-permute-done.3
  20.1 0.2 collective-permute-done.4.refs_2_
  20.4 0.1 collective-permute-start.5
  20.5 1.8 %collective-permute-start.6 = (f32[408,128]{1,0:T(8,128)S(1)}, f32[408,128]{1,0:T(8,128)S(1)}, u32[]{:S(2)}, u32[]{:S(2)}) collective-permute-start(f32[408,128]{1,0:T(8,128)S(1)} %collective-permute-done.2), channel_id=1, source_target_pairs={{0,5},{1,2},{2,7},{3,0},{4,1},{5,6},{6,3},{7,4},{8,13},{9,10},{10,... | collective-permute-start | bytes 626696 | tf_op jit(solution)/shard_map/ppermute | solution.py:422
  22.3 1.2 %remap_0.1.refs_4_ = f32[648,128]{1,0:T(8,128)S(1)} custom-call(s32[5,256]{1,0:T(8,128)S(4)} %get-tuple-element.15.refs_0_, f32[1232,128]{1,0:T(8,128)S(1)} %constant_dynamic-update-slice_fusion.2.refs_1_, bf16[161,128,256]{2,1,0:T(8,128)(2,1)S(1)} %get-tuple-element.18.refs_2_.refs_3_), custom_call_target="tpu_custom_call" | custom-call | flops 83886080 | bytes 5275648 | tf_op jit(solution)/shard_map/remap_0/pallas_call | solution.py:395
  23.5 0.0 copy-start
  23.5 0.0 copy-start.1
  23.5 0.0 collective-permute-done.5.refs_1_
  23.5 1.8 %remap_1.1 = (f32[648,128]{1,0:T(8,128)S(1)}, s32[2,256]{1,0:T(2,128)S(4)}) custom-call(s32[5,256]{1,0:T(8,128)S(4)} %get-tuple-element.15.refs_0_, f32[1232,128]{1,0:T(8,128)S(1)} %collective-permute-done.5.refs_1_, f32[8,128]{1,0:T(8,128)S(1)} %collective-permute-done.4.refs_2_, bf16[161,128,256]{2,1,0:T(8,128)(2,1)S(1)} %get-tuple-element.18.refs_2_.refs_3_, ...), custom_call_target="tpu_custom_call" | custom-call | flops 83886080 | bytes 5275648 | tf_op jit(solution)/shard_map/remap_1/pallas_call | solution.py:395
  25.4 0.3 %collective-permute-done.6.refs_2_ = f32[408,128]{1,0:T(8,128)S(1)} collective-permute-done((f32[408,128]{1,0:T(8,128)S(1)}, f32[408,128]{1,0:T(8,128)S(1)}, u32[]{:S(2)}, u32[]{:S(2)}) %collective-permute-start.6) | collective-permute-done | bytes 208928 | tf_op jit(solution)/shard_map/ppermute | solution.py:422
  25.7 0.4 %collective-permute-start.7 = (f32[408,128]{1,0:T(8,128)S(1)}, f32[408,128]{1,0:T(8,128)S(1)}, u32[]{:S(2)}, u32[]{:S(2)}) collective-permute-start(f32[408,128]{1,0:T(8,128)S(1)} %collective-permute-done.6.refs_2_), channel_id=1, source_target_pairs={{0,1},{1,0},{2,3},{3,2},{4,5},{5,4},{6,7},{7,6},{8,9},{9,8},{10,11... | collective-permute-start | bytes 626696 | tf_op jit(solution)/shard_map/ppermute | solution.py:422
  26.1 0.5 %remap_2.1.refs_4_ = f32[648,128]{1,0:T(8,128)S(1)} custom-call(s32[5,256]{1,0:T(8,128)S(4)} %get-tuple-element.15.refs_0_, s32[2,256]{1,0:T(2,128)S(4)} %get-tuple-element.19.refs_1_, f32[408,128]{1,0:T(8,128)S(1)} %collective-permute-done.6.refs_2_, bf16[161,128,256]{2,1,0:T(8,128)(2,1)S(1)} %get-tuple-element.18.refs_2_.refs_3_, ...), custom_call_target="tpu_custom_call" | custom-call | flops 83886080 | bytes 5275648 | tf_op jit(solution)/shard_map/remap_2/pallas_call | solution.py:395
  26.6 0.6 %collective-permute-done.7.refs_2_ = f32[408,128]{1,0:T(8,128)S(1)} collective-permute-done((f32[408,128]{1,0:T(8,128)S(1)}, f32[408,128]{1,0:T(8,128)S(1)}, u32[]{:S(2)}, u32[]{:S(2)}) %collective-permute-start.7) | collective-permute-done | bytes 208928 | tf_op jit(solution)/shard_map/ppermute | solution.py:422
  27.2 0.0 copy-done
  27.2 0.0 copy-done.1
  27.2 1.2 %remap_last.1 = f32[320,128]{1,0:T(8,128)} custom-call(s32[5,256]{1,0:T(8,128)S(4)} %get-tuple-element.15.refs_0_, s32[2,256]{1,0:T(2,128)S(4)} %get-tuple-element.19.refs_1_, f32[408,128]{1,0:T(8,128)S(1)} %collective-permute-done.7.refs_2_, bf16[161,128,256]{2,1,0:T(8,128)(2,1)S(1)} %get-tuple-element.18.refs_2_.refs_3_, f32[648,128]{1,0:T(8,128)S(1)} %remap_2.1.refs_4_, ...), custom_call_target="tpu_custom_call" | custom-call | flops 83886080 | bytes 5275648 | tf_op jit(solution)/shard_map/remap_last/pallas_call | solution.py:395
  (5 shorter events, 0.1 us)
Async XLA Ops:
  0.0 12.2 %collective-permute-start = (f32[400,128]{1,0:T(8,128)}, f32[400,128]{1,0:T(8,128)S(1)}, u32[]{:S(2)}, u32[]{:S(2)}) collective-permute-start(f32[400,128]{1,0:T(8,128)} %bitcast.14), channel_id=1, source_target_pairs={{0,12},{1,13},{2,14},{3,15},{4,8},{5,9},{6,10},{7,11},{8,4},{9,5},... | collective-permute-start | bytes 614408 | tf_op jit(solution)/shard_map/ppermute | solution.py:422
  6.4 5.7 %collective-permute-start.1 = (f32[8,128]{1,0:T(8,128)}, f32[8,128]{1,0:T(8,128)S(1)}, u32[]{:S(2)}, u32[]{:S(2)}) collective-permute-start(f32[8,128]{1,0:T(8,128)} %encode.1), channel_id=1, source_target_pairs={{0,12},{1,13},{2,14},{3,15},{4,8},{5,9},{6,10},{7,11},{8,4},{9,5},... | collective-permute-start | bytes 12296 | tf_op jit(solution)/shard_map/ppermute | solution.py:422
  12.2 7.8 %collective-permute-start.2 = (f32[408,128]{1,0:T(8,128)S(1)}, f32[408,128]{1,0:T(8,128)S(1)}, u32[]{:S(2)}, u32[]{:S(2)}) collective-permute-start(f32[408,128]{1,0:T(8,128)S(1)} %get-tuple-element.25), channel_id=1, source_target_pairs={{0,2},{1,5},{2,0},{3,7},{4,6},{5,1},{6,4},{7,3},{8,10},{9,13},{10,... | collective-permute-start | bytes 626696 | tf_op jit(solution)/shard_map/ppermute | solution.py:422
  13.8 6.3 %collective-permute-start.3 = (f32[408,128]{1,0:T(8,128)S(1)}, f32[408,128]{1,0:T(8,128)S(1)}, u32[]{:S(2)}, u32[]{:S(2)}) collective-permute-start(f32[408,128]{1,0:T(8,128)S(1)} %get-tuple-element.25), channel_id=1, source_target_pairs={{0,4},{1,3},{2,6},{3,1},{4,0},{5,7},{6,2},{7,5},{8,12},{9,11},{10,... | collective-permute-start | bytes 626696 | tf_op jit(solution)/shard_map/ppermute | solution.py:422
  16.2 4.1 %collective-permute-start.4 = (f32[8,128]{1,0:T(8,128)S(1)}, f32[8,128]{1,0:T(8,128)S(1)}, u32[]{:S(2)}, u32[]{:S(2)}) collective-permute-start(f32[8,128]{1,0:T(8,128)S(1)} %collective-permute-done.1), channel_id=1, source_target_pairs={{0,7},{1,6},{2,5},{3,4},{4,3},{5,2},{6,1},{7,0},{8,15},{9,14},{10,... | collective-permute-start | bytes 12296 | tf_op jit(solution)/shard_map/ppermute | solution.py:422
  20.4 3.2 %collective-permute-start.5 = (f32[1232,128]{1,0:T(8,128)S(1)}, f32[1232,128]{1,0:T(8,128)S(1)}, u32[]{:S(2)}, u32[]{:S(2)}) collective-permute-start(f32[1232,128]{1,0:T(8,128)S(1)} %constant_dynamic-update-slice_fusion.2.refs_1_), channel_id=1, source_target_pairs={{0,1},{1,0},{2,3},{3,2},{4,5},{5,4},{6,7},{7,6},{8,9},{9,8},{10,11... | collective-permute-start | bytes 1892360 | tf_op jit(solution)/shard_map/ppermute | solution.py:422
  20.5 5.2 %collective-permute-start.6 = (f32[408,128]{1,0:T(8,128)S(1)}, f32[408,128]{1,0:T(8,128)S(1)}, u32[]{:S(2)}, u32[]{:S(2)}) collective-permute-start(f32[408,128]{1,0:T(8,128)S(1)} %collective-permute-done.2), channel_id=1, source_target_pairs={{0,5},{1,2},{2,7},{3,0},{4,1},{5,6},{6,3},{7,4},{8,13},{9,10},{10,... | collective-permute-start | bytes 626696 | tf_op jit(solution)/shard_map/ppermute | solution.py:422
  23.5 3.7 %copy-start = (f32[2,5,5120]{2,0,1:T(2,128)S(1)}, f32[2,5,5120]{2,0,1:T(2,128)}, u32[]{:S(2)}) copy-start(f32[2,5,5120]{2,0,1:T(2,128)} %param.8) | copy-start | bytes 614404
  23.5 3.7 %copy-start.1 = (s32[5120]{0:T(1024)S(1)}, s32[5120]{0:T(1024)}, u32[]{:S(2)}) copy-start(s32[5120]{0:T(1024)} %param.9) | copy-start | bytes 61444
  25.7 1.5 %collective-permute-start.7 = (f32[408,128]{1,0:T(8,128)S(1)}, f32[408,128]{1,0:T(8,128)S(1)}, u32[]{:S(2)}, u32[]{:S(2)}) collective-permute-start(f32[408,128]{1,0:T(8,128)S(1)} %collective-permute-done.6.refs_2_), channel_id=1, source_target_pairs={{0,1},{1,0},{2,3},{3,2},{4,5},{5,4},{6,7},{7,6},{8,9},{9,8},{10,11... | collective-permute-start | bytes 626696 | tf_op jit(solution)/shard_map/ppermute | solution.py:422

commit v12 on v9

--- a/solution.py
+++ b/solution.py
@@ -458,7 +458,6 @@
     sums = remap(dims, 0, plan, near, held, split)
     if relayed:
         sums, spots = remap(dims, 1, plan, sibling, held, split, sums, table=table)
-        relay, sums = ahead(relay, sums)
         met = passed(relay, siblings)
         sums = remap(dims, 2, plan, relay, 1, split, sums, spots=spots)
         out = remap(dims, 3, plan, met, 1, split, sums, last, spots=spots)

time: 28.7 us -> 31.6 us (1.10)
  waiting for transfers between devices: 6.15 us -> 8.89 us
    ppermute x8, waiting for transfers between devices: 6.15 us -> 8.89 us  [passed(): return lax.ppermute(array, 'comp', pairs)]
  transfers between devices with their start and end apart: 8 -> 8, of which waited for: 5 -> 4; matrix products, arithmetic and copies ran while one was open for 0% -> 0% of each run, Pallas kernels for 35% -> 32%
where the time goes in v12:
time: 31.6 us; the launch traced here: 31.2 us
  Pallas kernels  11.2 us (35%)
  starting transfers between devices  11 us (35%)
  waiting for transfers between devices  8.89 us (28%)
    ppermute x8, starting transfers between devices, passed(): return lax.ppermute(array, 'comp', pairs)  11 us
    ppermute x8, waiting for transfers between devices, passed(): return lax.ppermute(array, 'comp', pairs)  8.89 us
    pallas_call x4, Pallas kernels, remap(): pl.pallas_call(body, out_shape=out, in_specs=[spec for _, spec in args],...  5.06 us
    pallas_call x1, Pallas kernels, prepare(): pl.pallas_call(lambda *refs: prepare_kernel(dims, chunks, *refs), out_sha...  4.74 us
    pallas_call x1, Pallas kernels, encode(): pl.pallas_call(encode_kernel, out_shape=jax.ShapeDtypeStruct((neigh + -ne...  1.4 us
  transfers between devices with their start and end apart: 8, of which 4 were waited for; matrix products, arithmetic and copies ran while one was open for 0% of the time, Pallas kernels for 32%

profile of v12, /device:TPU:0, one launch (start us, length us, event | category | flops | bytes accessed | tf_op | source)
XLA Modules:
  0.0 31.2 jit_solution(3566010767248407082)
XLA Ops:
  0.0 5.0 %collective-permute-start = (f32[400,128]{1,0:T(8,128)}, f32[400,128]{1,0:T(8,128)S(1)}, u32[]{:S(2)}, u32[]{:S(2)}) collective-permute-start(f32[400,128]{1,0:T(8,128)} %bitcast.14), channel_id=1, source_target_pairs={{0,12},{1,13},{2,14},{3,15},{4,8},{5,9},{6,10},{7,11},{8,4},{9,5},... | collective-permute-start | bytes 614408 | tf_op jit(solution)/shard_map/ppermute | solution.py:422
  5.0 1.4 %encode.1 = f32[8,128]{1,0:T(8,128)} custom-call(s32[8,32]{1,0:T(8,128)} %bitcast.18, s32[1,8]{1,0:T(1,128)} %count_ref.1), custom_call_target="tpu_custom_call" | custom-call | flops 4096 | bytes 8192 | tf_op jit(solution)/shard_map/encode/pallas_call | solution.py:72
  6.4 0.0 collective-permute-start.1
  6.5 4.7 %prepare.1 = (bf16[161,128,256]{2,1,0:T(8,128)(2,1)S(1)}, s32[5,256]{1,0:T(8,128)S(4)}) custom-call(s32[4,40]{1,0:T(4,128)} %bitcast.19, s32[40]{0:T(128)} %refs_1_.1, s32[16,9]{1,0:T(8,128)} %constant.2.clone.refs_2_, f32[160,128,128]{2,1,0:T(8,128)} %bitcast.17), custom_call_target="tpu_custom_call" | custom-call | flops 10485760 | bytes 20971520 | tf_op jit(solution)/shard_map/prepare/pallas_call | solution.py:173
  11.2 1.0 %collective-permute-done.1 = f32[8,128]{1,0:T(8,128)S(1)} collective-permute-done((f32[8,128]{1,0:T(8,128)}, f32[8,128]{1,0:T(8,128)S(1)}, u32[]{:S(2)}, u32[]{:S(2)}) %collective-permute-start.1) | collective-permute-done | bytes 4128 | tf_op jit(solution)/shard_map/ppermute | solution.py:422
  12.2 0.0 collective-permute-done
  12.2 1.6 %collective-permute-start.2 = (f32[408,128]{1,0:T(8,128)S(1)}, f32[408,128]{1,0:T(8,128)S(1)}, u32[]{:S(2)}, u32[]{:S(2)}) collective-permute-start(f32[408,128]{1,0:T(8,128)S(1)} %get-tuple-element.21), channel_id=1, source_target_pairs={{0,2},{1,5},{2,0},{3,7},{4,6},{5,1},{6,4},{7,3},{8,10},{9,13},{10,... | collective-permute-start | bytes 626696 | tf_op jit(solution)/shard_map/ppermute | solution.py:422
  13.8 2.5 %collective-permute-start.3 = (f32[408,128]{1,0:T(8,128)S(1)}, f32[408,128]{1,0:T(8,128)S(1)}, u32[]{:S(2)}, u32[]{:S(2)}) collective-permute-start(f32[408,128]{1,0:T(8,128)S(1)} %get-tuple-element.21), channel_id=1, source_target_pairs={{0,4},{1,3},{2,6},{3,1},{4,0},{5,7},{6,2},{7,5},{8,12},{9,11},{10,... | collective-permute-start | bytes 626696 | tf_op jit(solution)/shard_map/ppermute | solution.py:422
  16.2 0.0 collective-permute-start.4
  16.3 3.8 %collective-permute-done.2 = f32[408,128]{1,0:T(8,128)S(1)} collective-permute-done((f32[408,128]{1,0:T(8,128)S(1)}, f32[408,128]{1,0:T(8,128)S(1)}, u32[]{:S(2)}, u32[]{:S(2)}) %collective-permute-start.2) | collective-permute-done | bytes 208928 | tf_op jit(solution)/shard_map/ppermute | solution.py:422
  20.1 0.0 collective-permute-done.3
  20.1 0.2 collective-permute-done.4.refs_2_
  20.4 0.1 collective-permute-start.5
  20.5 1.4 %collective-permute-start.6 = (f32[408,128]{1,0:T(8,128)S(1)}, f32[408,128]{1,0:T(8,128)S(1)}, u32[]{:S(2)}, u32[]{:S(2)}) collective-permute-start(f32[408,128]{1,0:T(8,128)S(1)} %collective-permute-done.3), channel_id=1, source_target_pairs={{0,3},{1,4},{2,1},{3,6},{4,7},{5,0},{6,5},{7,2},{8,11},{9,12},{10,... | collective-permute-start | bytes 626696 | tf_op jit(solution)/shard_map/ppermute | solution.py:422
  21.9 3.9 %collective-permute-done.6.refs_2_ = f32[408,128]{1,0:T(8,128)S(1)} collective-permute-done((f32[408,128]{1,0:T(8,128)S(1)}, f32[408,128]{1,0:T(8,128)S(1)}, u32[]{:S(2)}, u32[]{:S(2)}) %collective-permute-start.6) | collective-permute-done | bytes 208928 | tf_op jit(solution)/shard_map/ppermute | solution.py:422
  25.8 0.3 %collective-permute-start.7 = (f32[408,128]{1,0:T(8,128)S(1)}, f32[408,128]{1,0:T(8,128)S(1)}, u32[]{:S(2)}, u32[]{:S(2)}) collective-permute-start(f32[408,128]{1,0:T(8,128)S(1)} %collective-permute-done.6.refs_2_), channel_id=1, source_target_pairs={{0,1},{1,0},{2,3},{3,2},{4,5},{5,4},{6,7},{7,6},{8,9},{9,8},{10,11... | collective-permute-start | bytes 626696 | tf_op jit(solution)/shard_map/ppermute | solution.py:422
  26.1 1.4 %remap_0.1.refs_4_ = f32[648,128]{1,0:T(8,128)S(1)} custom-call(s32[5,256]{1,0:T(8,128)S(4)} %get-tuple-element.13.refs_0_, f32[1232,128]{1,0:T(8,128)S(1)} %constant_dynamic-update-slice_fusion.2.refs_1_, bf16[161,128,256]{2,1,0:T(8,128)(2,1)S(1)} %get-tuple-element.16.refs_2_.refs_3_), custom_call_target="tpu_custom_call" | custom-call | flops 83886080 | bytes 5275648 | tf_op jit(solution)/shard_map/remap_0/pallas_call | solution.py:395
  27.5 0.0 copy-start
  27.5 0.0 copy-start.1
  27.5 0.0 collective-permute-done.5.refs_1_
  27.5 2.0 %remap_1.1 = (f32[648,128]{1,0:T(8,128)S(1)}, s32[2,256]{1,0:T(2,128)S(4)}) custom-call(s32[5,256]{1,0:T(8,128)S(4)} %get-tuple-element.13.refs_0_, f32[1232,128]{1,0:T(8,128)S(1)} %collective-permute-done.5.refs_1_, f32[8,128]{1,0:T(8,128)S(1)} %collective-permute-done.4.refs_2_, bf16[161,128,256]{2,1,0:T(8,128)(2,1)S(1)} %get-tuple-element.16.refs_2_.refs_3_, ...), custom_call_target="tpu_custom_call" | custom-call | flops 83886080 | bytes 5275648 | tf_op jit(solution)/shard_map/remap_1/pallas_call | solution.py:395
  29.5 0.5 %remap_2.1.refs_4_ = f32[648,128]{1,0:T(8,128)S(1)} custom-call(s32[5,256]{1,0:T(8,128)S(4)} %get-tuple-element.13.refs_0_, s32[2,256]{1,0:T(2,128)S(4)} %get-tuple-element.17.refs_1_, f32[408,128]{1,0:T(8,128)S(1)} %collective-permute-done.6.refs_2_, bf16[161,128,256]{2,1,0:T(8,128)(2,1)S(1)} %get-tuple-element.16.refs_2_.refs_3_, ...), custom_call_target="tpu_custom_call" | custom-call | flops 83886080 | bytes 5275648 | tf_op jit(solution)/shard_map/remap_2/pallas_call | solution.py:395
  30.0 0.0 collective-permute-done.7.refs_2_
  30.0 0.0 copy-done
  30.0 0.0 copy-done.1
  30.0 1.3 %remap_last.1 = f32[320,128]{1,0:T(8,128)} custom-call(s32[5,256]{1,0:T(8,128)S(4)} %get-tuple-element.13.refs_0_, s32[2,256]{1,0:T(2,128)S(4)} %get-tuple-element.17.refs_1_, f32[408,128]{1,0:T(8,128)S(1)} %collective-permute-done.7.refs_2_, bf16[161,128,256]{2,1,0:T(8,128)(2,1)S(1)} %get-tuple-element.16.refs_2_.refs_3_, f32[648,128]{1,0:T(8,128)S(1)} %remap_2.1.refs_4_, ...), custom_call_target="tpu_custom_call" | custom-call | flops 83886080 | bytes 5275648 | tf_op jit(solution)/shard_map/remap_last/pallas_call | solution.py:395
  (5 shorter events, 0.1 us)
Async XLA Ops:
  0.0 12.2 %collective-permute-start = (f32[400,128]{1,0:T(8,128)}, f32[400,128]{1,0:T(8,128)S(1)}, u32[]{:S(2)}, u32[]{:S(2)}) collective-permute-start(f32[400,128]{1,0:T(8,128)} %bitcast.14), channel_id=1, source_target_pairs={{0,12},{1,13},{2,14},{3,15},{4,8},{5,9},{6,10},{7,11},{8,4},{9,5},... | collective-permute-start | bytes 614408 | tf_op jit(solution)/shard_map/ppermute | solution.py:422
  6.4 5.7 %collective-permute-start.1 = (f32[8,128]{1,0:T(8,128)}, f32[8,128]{1,0:T(8,128)S(1)}, u32[]{:S(2)}, u32[]{:S(2)}) collective-permute-start(f32[8,128]{1,0:T(8,128)} %encode.1), channel_id=1, source_target_pairs={{0,12},{1,13},{2,14},{3,15},{4,8},{5,9},{6,10},{7,11},{8,4},{9,5},... | collective-permute-start | bytes 12296 | tf_op jit(solution)/shard_map/ppermute | solution.py:422
  12.2 7.8 %collective-permute-start.2 = (f32[408,128]{1,0:T(8,128)S(1)}, f32[408,128]{1,0:T(8,128)S(1)}, u32[]{:S(2)}, u32[]{:S(2)}) collective-permute-start(f32[408,128]{1,0:T(8,128)S(1)} %get-tuple-element.21), channel_id=1, source_target_pairs={{0,2},{1,5},{2,0},{3,7},{4,6},{5,1},{6,4},{7,3},{8,10},{9,13},{10,... | collective-permute-start | bytes 626696 | tf_op jit(solution)/shard_map/ppermute | solution.py:422
  13.8 6.3 %collective-permute-start.3 = (f32[408,128]{1,0:T(8,128)S(1)}, f32[408,128]{1,0:T(8,128)S(1)}, u32[]{:S(2)}, u32[]{:S(2)}) collective-permute-start(f32[408,128]{1,0:T(8,128)S(1)} %get-tuple-element.21), channel_id=1, source_target_pairs={{0,4},{1,3},{2,6},{3,1},{4,0},{5,7},{6,2},{7,5},{8,12},{9,11},{10,... | collective-permute-start | bytes 626696 | tf_op jit(solution)/shard_map/ppermute | solution.py:422
  16.2 4.1 %collective-permute-start.4 = (f32[8,128]{1,0:T(8,128)S(1)}, f32[8,128]{1,0:T(8,128)S(1)}, u32[]{:S(2)}, u32[]{:S(2)}) collective-permute-start(f32[8,128]{1,0:T(8,128)S(1)} %collective-permute-done.1), channel_id=1, source_target_pairs={{0,7},{1,6},{2,5},{3,4},{4,3},{5,2},{6,1},{7,0},{8,15},{9,14},{10,... | collective-permute-start | bytes 12296 | tf_op jit(solution)/shard_map/ppermute | solution.py:422
  20.4 7.1 %collective-permute-start.5 = (f32[1232,128]{1,0:T(8,128)S(1)}, f32[1232,128]{1,0:T(8,128)S(1)}, u32[]{:S(2)}, u32[]{:S(2)}) collective-permute-start(f32[1232,128]{1,0:T(8,128)S(1)} %constant_dynamic-update-slice_fusion.2.refs_1_), channel_id=1, source_target_pairs={{0,1},{1,0},{2,3},{3,2},{4,5},{5,4},{6,7},{7,6},{8,9},{9,8},{10,11... | collective-permute-start | bytes 1892360 | tf_op jit(solution)/shard_map/ppermute | solution.py:422
  20.5 5.3 %collective-permute-start.6 = (f32[408,128]{1,0:T(8,128)S(1)}, f32[408,128]{1,0:T(8,128)S(1)}, u32[]{:S(2)}, u32[]{:S(2)}) collective-permute-start(f32[408,128]{1,0:T(8,128)S(1)} %collective-permute-done.3), channel_id=1, source_target_pairs={{0,3},{1,4},{2,1},{3,6},{4,7},{5,0},{6,5},{7,2},{8,11},{9,12},{10,... | collective-permute-start | bytes 626696 | tf_op jit(solution)/shard_map/ppermute | solution.py:422
  25.8 4.2 %collective-permute-start.7 = (f32[408,128]{1,0:T(8,128)S(1)}, f32[408,128]{1,0:T(8,128)S(1)}, u32[]{:S(2)}, u32[]{:S(2)}) collective-permute-start(f32[408,128]{1,0:T(8,128)S(1)} %collective-permute-done.6.refs_2_), channel_id=1, source_target_pairs={{0,1},{1,0},{2,3},{3,2},{4,5},{5,4},{6,7},{7,6},{8,9},{9,8},{10,11... | collective-permute-start | bytes 626696 | tf_op jit(solution)/shard_map/ppermute | solution.py:422
  27.5 2.5 %copy-start = (f32[2,5,5120]{2,0,1:T(2,128)S(1)}, f32[2,5,5120]{2,0,1:T(2,128)}, u32[]{:S(2)}) copy-start(f32[2,5,5120]{2,0,1:T(2,128)} %param.8) | copy-start | bytes 614404
  27.5 2.5 %copy-start.1 = (s32[5120]{0:T(1024)S(1)}, s32[5120]{0:T(1024)}, u32[]{:S(2)}) copy-start(s32[5120]{0:T(1024)} %param.9) | copy-start | bytes 61444
